TPU v7x, 32 devices: a whole 2x2x4 slice. The times are simulated.
32 devices in a mesh: tensor: 2 (over x), dp: 4 (over z), context: 4 (over y, core).
Axes of the slice: x: 2, y: 2, z: 4, core: 2. Of those that a mesh axis runs over, the one named last changes fastest.
Arguments:
- layer_input: bfloat16 [1024, 4, 2048], P('context', 'dp'), may hold values from -6 to 6
- cotangent: bfloat16 [1024, 4, 2048], P('context', 'dp'), may hold values from -6 to 6
- attn_gain: float32 [2048], replicated, may hold values from 0.1 to 1.9
- query_weight: bfloat16 [2048, 2048], P(None, 'tensor'), may hold values from -0.125 to 0.125
- key_matrix: bfloat16 [2048, 256], P(None, 'tensor'), may hold values from -0.125 to 0.125
- value_matrix: bfloat16 [2048, 256], P(None, 'tensor'), may hold values from -0.125 to 0.125
- output_matrix: bfloat16 [2048, 2048], P('tensor'), may hold values from -3 to 3
- feed_gain: float32 [2048], replicated, may hold values from 0.1 to 1.9
- gate_weight: bfloat16 [2048, 5632], P(None, 'tensor'), may hold values from -0.125 to 0.125
- up_weight: bfloat16 [2048, 5632], P(None, 'tensor'), may hold values from -0.125 to 0.125
- down_weight: bfloat16 [5632, 2048], P('tensor'), may hold values from -0.078125 to 0.078125
Outputs:
- layer_output: bfloat16 [1024, 4, 2048], P('context', 'dp')
- input_grad: bfloat16 [1024, 4, 2048], P('context', 'dp')
- attn_gain_grad: float32 [2048], P(('dp', 'context'))
- query_grad: float32 [2048, 2048], P(('dp', 'context'), 'tensor')
- key_grad: float32 [2048, 256], P(('dp', 'context'), 'tensor')
- value_grad: float32 [2048, 256], P(('dp', 'context'), 'tensor')
- out_grad: float32 [2048, 2048], P('tensor', ('dp', 'context'))
- feed_gain_grad: float32 [2048], P(('dp', 'context'))
- gate_grad: float32 [2048, 5632], P(('dp', 'context'), 'tensor')
- up_grad: float32 [2048, 5632], P(('dp', 'context'), 'tensor')
- down_grad: float32 [5632, 2048], P('tensor', ('dp', 'context'))
All inputs are finite; a program needn't handle non-finite values.
Results may differ from a plain program's by a relative error of at most 0.019.
Values may be sent and summed in bfloat16 or wider, within the bound.
No kernel may reach another device: no remote copies, remote signals or barrier semaphores. Data moves between devices by JAX's collectives and lax.ppermute only.
A program may use at most 320 MiB of HBM per device.

v0:
```python
import math

import jax
import jax.numpy as jnp
from jax import lax
from jax.sharding import PartitionSpec as P

HEAD_WIDTH = 64


EPS = 1e-05
ROPE_BASE = 10000.0
NEG_FILL = -1e30


def rope_angles(positions, head_size):
    half_size = head_size // 2
    frequencies = jnp.exp(
        jnp.arange(half_size, dtype=jnp.float32) * (-2.0 * math.log(ROPE_BASE) / head_size)
    )
    return positions.astype(jnp.float32)[:, None] * frequencies[None, :]


def apply_rotary(heads_in, cosine_rows, sine_rows):
    half_size = heads_in.shape[-1] // 2
    first_half = heads_in[..., :half_size]
    second_half = heads_in[..., half_size:]
    return jnp.concatenate(
        [
            first_half * cosine_rows - second_half * sine_rows,
            second_half * cosine_rows + first_half * sine_rows,
        ],
        axis=-1,
    )


def inverse_rotary(heads_in, cosine_rows, sine_rows):
    half_size = heads_in.shape[-1] // 2
    first_half = heads_in[..., :half_size]
    second_half = heads_in[..., half_size:]
    return jnp.concatenate(
        [
            first_half * cosine_rows + second_half * sine_rows,
            second_half * cosine_rows - first_half * sine_rows,
        ],
        axis=-1,
    )


def rms_scale(values_in):
    return lax.rsqrt(jnp.mean(values_in * values_in, axis=-1, keepdims=True) + EPS)


def norm_backward(d_normed, inputs_f, inv_rms, gain_in):
    scaled = d_normed * gain_in
    return inv_rms * scaled - inputs_f * (inv_rms * inv_rms * inv_rms) * jnp.mean(
        scaled * inputs_f, axis=-1, keepdims=True
    )


def attend_piece(query_rows, query_pos, score_scale, state_in, kv_piece, offset):
    run_max, run_sum, accum = state_in
    key_piece, value_piece = kv_piece
    key_count = key_piece.shape[0]
    head_size = query_rows.shape[-1]
    key_heads = key_piece.reshape(key_count, key_piece.shape[1], -1, head_size)
    value_heads = value_piece.reshape(key_count, value_piece.shape[1], -1, head_size)
    scores = (
        jnp.einsum("qsngd,ksnd->qsngk", query_rows, key_heads, preferred_element_type=jnp.float32)
        * score_scale
    )
    key_pos = offset + jnp.arange(key_count, dtype=jnp.int32)
    allowed = (query_pos[:, None] >= key_pos[None, :])[:, None, None, None, :]
    new_max = jnp.maximum(run_max, jnp.max(jnp.where(allowed, scores, NEG_FILL), axis=-1))
    factor = jnp.exp(run_max - new_max)
    weights = jnp.where(allowed, jnp.exp(scores - new_max[..., None]), 0.0)
    new_sum = run_sum * factor + jnp.sum(weights, axis=-1)
    new_accum = accum * factor[..., None] + jnp.einsum(
        "qsngk,ksnd->qsngd",
        weights.astype(jnp.bfloat16),
        value_heads,
        preferred_element_type=jnp.float32,
    )
    return (new_max, new_sum, new_accum)


def on_device(
    layer_input,
    cotangent,
    attn_gain,
    query_weight,
    key_matrix,
    value_matrix,
    output_matrix,
    feed_gain,
    gate_weight,
    up_weight,
    down_weight,
):
    single_float = jnp.float32
    brain_float = jnp.bfloat16
    tok_here, seq_here, width = layer_input.shape
    head_size = HEAD_WIDTH
    q_local = query_weight.shape[1] // head_size
    kv_local = key_matrix.shape[1] // head_size
    group_size = q_local // kv_local
    score_scale = 1.0 / math.sqrt(head_size)
    ctx_count = lax.axis_size("context")
    first_pos = lax.axis_index("context") * tok_here
    query_pos = first_pos + jnp.arange(tok_here, dtype=jnp.int32)
    last_pos = first_pos + tok_here - 1
    angles = rope_angles(query_pos, head_size)
    cosine_rows = jnp.cos(angles)[:, None, None, :]
    sine_rows = jnp.sin(angles)[:, None, None, :]
    inputs_f = layer_input.astype(single_float)
    attn_rms = rms_scale(inputs_f)
    first_normed = (inputs_f * attn_rms * attn_gain).astype(brain_float)
    query_rows = apply_rotary(
        jnp.dot(first_normed, query_weight, preferred_element_type=single_float).reshape(
            tok_here, seq_here, q_local, head_size
        ),
        cosine_rows,
        sine_rows,
    ).astype(brain_float)
    query_rows = query_rows.reshape(tok_here, seq_here, kv_local, group_size, head_size)
    rotated_keys = apply_rotary(
        jnp.dot(first_normed, key_matrix, preferred_element_type=single_float).reshape(
            tok_here, seq_here, kv_local, head_size
        ),
        cosine_rows,
        sine_rows,
    ).astype(brain_float)
    rotated_keys = rotated_keys.reshape(tok_here, seq_here, kv_local * head_size)
    value_rows = jnp.dot(first_normed, value_matrix, preferred_element_type=single_float).astype(
        brain_float
    )

    def fold_piece(state_in, kv_piece, offset):
        return lax.cond(
            offset <= last_pos,
            lambda state_arg: attend_piece(
                query_rows, query_pos, score_scale, state_arg, kv_piece, offset
            ),
            lambda state_arg: state_arg,
            state_in,
        )

    stat_shape = (tok_here, seq_here, kv_local, group_size)
    initial_state = (
        jnp.full(stat_shape, NEG_FILL, single_float),
        jnp.zeros(stat_shape, single_float),
        jnp.zeros(stat_shape + (head_size,), single_float),
    )
    block_ids = jnp.arange(ctx_count, dtype=jnp.int32)
    kv_whole = (
        lax.all_gather(rotated_keys, "context", axis=0, tiled=True),
        lax.all_gather(value_rows, "context", axis=0, tiled=True),
    )
    key_stack = kv_whole[0].reshape(ctx_count, tok_here, seq_here, kv_local * head_size)
    value_stack = kv_whole[1].reshape(ctx_count, tok_here, seq_here, kv_local * head_size)

    def scan_piece(state_in, inputs):
        key_block, value_block, block_index = inputs
        return (fold_piece(state_in, (key_block, value_block), block_index * tok_here), None)

    state, unused = lax.scan(scan_piece, initial_state, (key_stack, value_stack, block_ids))
    run_max, run_sum, accum = state
    logsum_total = run_max + jnp.log(run_sum)
    attention_float = accum / run_sum[..., None]
    attn_b = attention_float.reshape(tok_here, seq_here, q_local * head_size).astype(brain_float)
    attn_proj = lax.psum(
        jnp.dot(attn_b, output_matrix, preferred_element_type=single_float).astype(jnp.bfloat16),
        "tensor",
    ).astype(jnp.float32)
    resid = inputs_f + attn_proj
    feed_rms = rms_scale(resid)
    normed_two = (resid * feed_rms * feed_gain).astype(brain_float)
    gate_values = jnp.dot(normed_two, gate_weight, preferred_element_type=single_float)
    up_values = jnp.dot(normed_two, up_weight, preferred_element_type=single_float)
    sigmoid_gate = jax.nn.sigmoid(gate_values)
    activated = gate_values * sigmoid_gate
    hidden = (activated * up_values).astype(brain_float)
    mixed = lax.psum(
        jnp.dot(hidden, down_weight, preferred_element_type=single_float).astype(jnp.bfloat16),
        "tensor",
    ).astype(jnp.float32)
    layer_output = (resid + mixed).astype(brain_float)
    d_hidden = jnp.dot(cotangent, down_weight.T, preferred_element_type=single_float)
    down_sum = jnp.einsum("tsf,tsd->fd", hidden, cotangent, preferred_element_type=single_float)
    d_gate = (
        d_hidden * up_values * (sigmoid_gate * (1.0 + gate_values * (1.0 - sigmoid_gate)))
    ).astype(brain_float)
    d_up = (d_hidden * activated).astype(brain_float)
    gate_sum = jnp.einsum("tsd,tsf->df", normed_two, d_gate, preferred_element_type=single_float)
    up_sum = jnp.einsum("tsd,tsf->df", normed_two, d_up, preferred_element_type=single_float)
    d_normed_two = lax.psum(
        (
            jnp.dot(d_gate, gate_weight.T, preferred_element_type=single_float)
            + jnp.dot(d_up, up_weight.T, preferred_element_type=single_float)
        ).astype(jnp.bfloat16),
        "tensor",
    ).astype(jnp.float32)
    feed_gain_sum = jnp.sum(d_normed_two * resid * feed_rms, axis=(0, 1))
    d_resid = cotangent.astype(single_float) + norm_backward(
        d_normed_two, resid, feed_rms, feed_gain
    )
    residual_grad_brain = d_resid.astype(brain_float)
    out_sum = jnp.einsum(
        "tsh,tsd->hd", attn_b, residual_grad_brain, preferred_element_type=single_float
    )
    attention_grad = jnp.dot(
        residual_grad_brain, output_matrix.T, preferred_element_type=single_float
    ).reshape(tok_here, seq_here, kv_local, group_size, head_size)
    d_attn_b = attention_grad.astype(brain_float)
    row_delta = jnp.sum(attention_grad * attention_float, axis=-1)
    all_keys, all_values = kv_whole
    key_blocks = all_keys.reshape(ctx_count, tok_here, seq_here, kv_local, head_size)
    value_blocks = all_values.reshape(ctx_count, tok_here, seq_here, kv_local, head_size)

    def back_piece(query_delta, inputs):
        key_block, value_block, block_index = inputs
        offset = block_index * tok_here

        def compute(delta_in):
            scores = (
                jnp.einsum(
                    "qsngd,ksnd->qsngk", query_rows, key_block, preferred_element_type=single_float
                )
                * score_scale
            )
            key_pos = offset + jnp.arange(tok_here, dtype=jnp.int32)
            allowed = (query_pos[:, None] >= key_pos[None, :])[:, None, None, None, :]
            probs = jnp.where(allowed, jnp.exp(scores - logsum_total[..., None]), 0.0)
            d_probs = jnp.einsum(
                "qsngd,ksnd->qsngk", d_attn_b, value_block, preferred_element_type=single_float
            )
            d_scores_b = (probs * (d_probs - row_delta[..., None]) * score_scale).astype(
                brain_float
            )
            delta_out = delta_in + jnp.einsum(
                "qsngk,ksnd->qsngd", d_scores_b, key_block, preferred_element_type=single_float
            )
            d_key = jnp.einsum(
                "qsngk,qsngd->ksnd", d_scores_b, query_rows, preferred_element_type=single_float
            )
            d_value = jnp.einsum(
                "qsngk,qsngd->ksnd",
                probs.astype(brain_float),
                d_attn_b,
                preferred_element_type=single_float,
            )
            return (delta_out, d_key, d_value)

        def skip_piece(delta_in):
            zero_block = jnp.zeros(key_block.shape, single_float)
            return (delta_in, zero_block, zero_block)

        delta_next, d_key, d_value = lax.cond(offset <= last_pos, compute, skip_piece, query_delta)
        return (delta_next, (d_key, d_value))

    zero_query = jnp.zeros((tok_here, seq_here, kv_local, group_size, head_size), single_float)
    query_delta, (key_parts, value_parts) = lax.scan(
        back_piece, zero_query, (key_blocks, value_blocks, block_ids)
    )
    kv_terms = jnp.concatenate(
        [
            key_parts.reshape(ctx_count * tok_here, seq_here, kv_local * head_size),
            value_parts.reshape(ctx_count * tok_here, seq_here, kv_local * head_size),
        ],
        axis=-1,
    )
    kv_back = lax.psum_scatter(
        kv_terms.astype(jnp.bfloat16), "context", scatter_dimension=0, tiled=True
    ).astype(jnp.float32)
    key_local = kv_back[..., : kv_local * head_size].reshape(
        tok_here, seq_here, kv_local, head_size
    )
    value_local = kv_back[..., kv_local * head_size :]
    d_query_b = (
        inverse_rotary(
            query_delta.reshape(tok_here, seq_here, q_local, head_size), cosine_rows, sine_rows
        )
        .reshape(tok_here, seq_here, q_local * head_size)
        .astype(brain_float)
    )
    key_grad_brain = (
        inverse_rotary(key_local, cosine_rows, sine_rows)
        .reshape(tok_here, seq_here, kv_local * head_size)
        .astype(brain_float)
    )
    value_grad_brain = value_local.astype(brain_float)
    query_sum = jnp.einsum(
        "tsd,tsh->dh", first_normed, d_query_b, preferred_element_type=single_float
    )
    key_sum = jnp.einsum(
        "tsd,tsh->dh", first_normed, key_grad_brain, preferred_element_type=single_float
    )
    value_sum = jnp.einsum(
        "tsd,tsh->dh", first_normed, value_grad_brain, preferred_element_type=single_float
    )
    d_normed_one = lax.psum(
        (
            jnp.dot(d_query_b, query_weight.T, preferred_element_type=single_float)
            + jnp.dot(key_grad_brain, key_matrix.T, preferred_element_type=single_float)
            + jnp.dot(value_grad_brain, value_matrix.T, preferred_element_type=single_float)
        ).astype(jnp.bfloat16),
        "tensor",
    ).astype(jnp.float32)
    attn_gain_sum = jnp.sum(d_normed_one * inputs_f * attn_rms, axis=(0, 1))
    input_grad = (d_resid + norm_backward(d_normed_one, inputs_f, attn_rms, attn_gain)).astype(
        brain_float
    )
    shares = (
        lax.psum_scatter(attn_gain_sum, ("dp", "context"), scatter_dimension=0, tiled=True),
        lax.psum_scatter(query_sum, ("dp", "context"), scatter_dimension=0, tiled=True),
        lax.psum_scatter(key_sum, ("dp", "context"), scatter_dimension=0, tiled=True),
        lax.psum_scatter(value_sum, ("dp", "context"), scatter_dimension=0, tiled=True),
        lax.psum_scatter(out_sum, ("dp", "context"), scatter_dimension=1, tiled=True),
        lax.psum_scatter(feed_gain_sum, ("dp", "context"), scatter_dimension=0, tiled=True),
        lax.psum_scatter(gate_sum, ("dp", "context"), scatter_dimension=0, tiled=True),
        lax.psum_scatter(up_sum, ("dp", "context"), scatter_dimension=0, tiled=True),
        lax.psum_scatter(down_sum, ("dp", "context"), scatter_dimension=1, tiled=True),
    )
    return (
        layer_output,
        input_grad,
        shares[0],
        shares[1],
        shares[2],
        shares[3],
        shares[4],
        shares[5],
        shares[6],
        shares[7],
        shares[8],
    )


def solution(mesh):
    in_specs = (
        P("context", "dp", None),
        P("context", "dp", None),
        P(),
        P(None, "tensor"),
        P(None, "tensor"),
        P(None, "tensor"),
        P("tensor", None),
        P(),
        P(None, "tensor"),
        P(None, "tensor"),
        P("tensor", None),
    )
    out_specs = (
        P("context", "dp", None),
        P("context", "dp", None),
        P(("dp", "context")),
        P(("dp", "context"), "tensor"),
        P(("dp", "context"), "tensor"),
        P(("dp", "context"), "tensor"),
        P("tensor", ("dp", "context")),
        P(("dp", "context")),
        P(("dp", "context"), "tensor"),
        P(("dp", "context"), "tensor"),
        P("tensor", ("dp", "context")),
    )
    return jax.shard_map(
        on_device, mesh=mesh, in_specs=in_specs, out_specs=out_specs, check_vma=False
    )
```

profile of v0, /device:TPU:0, one launch (start us, length us, event | category | flops | bytes accessed | tf_op | source)
XLA Modules:
  0.0 1366.3 jit_solution(16466389284174769565)
XLA Ops:
  7.3 1.6 fusion.84
  9.5 1.8 convolution_convert_fusion.2
  11.3 7.2 all-gather
  18.5 0.8 copy.56
  20.6 5.9 all_gather.6
  26.4 0.8 copy.55
  27.3 6.5 copy.54
  33.8 3.5 convolution_bitcast_fusion
  37.7 9.0 while.33
  39.0 3.8 conditional.6
  39.1 0.9 constant_dynamic-slice_fusion
  40.8 0.9 fusion.8
  41.7 1.1 fusion.16
  47.6 4.4 fusion.72
  52.4 52.6 %all-reduce.8.cloned.1.call-done = bf16[256,1,2048]{2,0,1:T(8,128)(2,1)} async-done(((bf16[256,1,2048]{2,0,1:T(8,128)(2,1)}), bf16[256,1,2048]{2,0,1:T(8,128)(2,1)}) %all-reduce.8.cloned.1.call-update) | async-done | bytes 1048592 | tf_op jit(solution)/shard_map/psum | solution.py:171
  105.0 1.7 multiply_reduce_fusion
  107.9 9.6 fusion.121
  117.6 4.7 fusion.120
  122.3 14.5 %multiply_convert_fusion = (bf16[256,2816]{1,0:T(8,128)(2,1)S(1)}, bf16[256,2816]{1,0:T(8,128)(2,1)S(1)}, bf16[256,2816]{1,0:T(8,128)(2,1)}) fusion(f32[256,2816]{1,0:T(8,128)} %fusion.120, f32[256,2816]{1,0:T(8,128)} %fusion.121, bf16[2816,2048]{1,0:T(8,128)(2,1)} %param.29, bf16[256,1,2048]{2,0,1:T(8,128)(2,1)S(1)} %copy-done.6), kind=kOutput, calls=%fused_computation.73 | convolution fusion | flops 2963603456 | bytes 22675456 | tf_op jit(solution)/shard_map/dot_general | solution.py:188
  136.8 7.1 fusion.122
  143.9 8.4 fusion.75
  152.4 1.1 reshape.683
  153.5 2.0 reshape.682
  155.5 2.3 copy.61
  157.8 1.2 copy.60
  159.0 1.3 log_add_fusion
  160.4 32.2 %all-reduce.10.cloned.1.call-done = bf16[256,1,2048]{2,0,1:T(8,128)(2,1)} async-done(((bf16[256,1,2048]{2,0,1:T(8,128)(2,1)}), bf16[256,1,2048]{2,0,1:T(8,128)(2,1)}) %all-reduce.10.cloned.1.call-update) | async-done | bytes 1048592 | tf_op jit(solution)/shard_map/psum | solution.py:196
  192.6 2.4 fusion.83
  195.1 4.7 bitcast_convert_fusion
  201.2 16.2 %while.34 = (s32[]{:T(128)}, f32[256,1,2,8,64]{0,4,3,2,1:T(8,128)S(1)}, bf16[4,256,1,2,64]{1,4,3,2,0:T(8,128)(2,1)}, bf16[4,256,1,2,64]{1,4,3,2,0:T(8,128)(2,1)}...) while((s32[]{:T(128)}, ...), condition=%wide.region_16.17_spmd.clone, body=%wide.region_13.16_spmd.clone.sunk | while | flops 682951168 | bytes 26140048 | solution.py:262
  201.2 1.3 dynamic_slice.60
  203.1 5.7 conditional.7
  204.3 0.9 fusion.44
  205.2 2.3 fusion.26
  209.5 1.3 dynamic_slice.60
  212.1 1.3 dynamic_slice.60
  214.8 1.3 dynamic_slice.60
  217.4 1.2 copy.63
  218.7 1.2 copy.62
  220.1 0.8 pad_maximum_fusion.1
  221.2 9.0 fusion.74
  231.2 2.7 fusion.123
  233.9 25.4 %reduce-scatter.9.cloned.1.call-done = bf16[256,1,256]{0,2,1:T(8,128)(2,1)} async-done(((bf16[1024,1,256]{0,2,1:T(8,128)(2,1)}), bf16[256,1,256]{0,2,1:T(8,128)(2,1)}) %reduce-scatter.9.cloned.1.call-update) | async-done | bytes 131088 | tf_op jit(solution)/shard_map/reduce_scatter | solution.py:272
  259.2 0.8 slice.48
  260.1 2.1 convolution_add_fusion.1
  262.3 1.4 fusion.73
  263.8 1.6 fusion.107
  265.5 1.6 fusion.105
  267.2 6.5 fusion.92
  273.8 1.0 copy-done.16
  274.7 4.7 fusion.102
  279.7 12.6 fusion.125
  292.4 13.6 fusion.124
  306.1 12.5 fusion.96
  320.5 6.5 all-reduce.12.cloned.1.call-done
  327.0 1.9 fusion.90
  328.8 61.3 %all-reduce.2 = (f32[2048]{0:T(1024)S(1)}, f32[2048]{0:T(1024)S(1)}) all-reduce(f32[2048]{0:T(1024)S(1)} %get-tuple-element.445, f32[2048]{0:T(1024)S(1)} %get-tuple-element.443), channel_id=4, replica_groups=mesh['tensor'=2,'dp'=4,'context'=4] {'dp','context'}, use_global_device_ids=true, to_apply=%region_21.22.clone | all-reduce | flops 4096 | bytes 32768
  391.3 4.6 fusion.78
  395.9 53.5 %reduce-scatter.15.cloned.1.call-done = f32[128,128]{1,0:T(8,128)} async-done(((f32[2048,128]{1,0:T(8,128)}), f32[128,128]{1,0:T(8,128)}) %reduce-scatter.15.cloned.1.call-update) | async-done | bytes 65552 | tf_op jit(solution)/shard_map/reduce_scatter | solution.py:317
  449.4 108.6 %reduce-scatter.17.cloned.1.call-done = f32[1024,128]{1,0:T(8,128)} async-done(((f32[1024,2048]{1,0:T(8,128)}), f32[1024,128]{1,0:T(8,128)}) %reduce-scatter.17.cloned.1.call-update) | async-done | bytes 524304 | tf_op jit(solution)/shard_map/reduce_scatter | solution.py:318
  557.9 109.0 %reduce-scatter.11.cloned.1.call-done = f32[128,1024]{1,0:T(8,128)} async-done(((f32[2048,1024]{1,0:T(8,128)}), f32[128,1024]{1,0:T(8,128)}) %reduce-scatter.11.cloned.1.call-update) | async-done | bytes 524304 | tf_op jit(solution)/shard_map/reduce_scatter | solution.py:315
  667.0 231.3 %reduce-scatter.21.cloned.1.call-done = f32[128,2816]{1,0:T(8,128)} async-done(((f32[2048,2816]{1,0:T(8,128)}), f32[128,2816]{1,0:T(8,128)}) %reduce-scatter.21.cloned.1.call-update) | async-done | bytes 1441808 | tf_op jit(solution)/shard_map/reduce_scatter | solution.py:321
  898.3 230.5 %reduce-scatter.19.cloned.1.call-done = f32[128,2816]{1,0:T(8,128)} async-done(((f32[2048,2816]{1,0:T(8,128)}), f32[128,2816]{1,0:T(8,128)}) %reduce-scatter.19.cloned.1.call-update) | async-done | bytes 1441808 | tf_op jit(solution)/shard_map/reduce_scatter | solution.py:320
  1128.8 230.7 %reduce-scatter.23.cloned.1.call-done = f32[2816,128]{1,0:T(8,128)} async-done(((f32[2816,2048]{1,0:T(8,128)}), f32[2816,128]{1,0:T(8,128)}) %reduce-scatter.23.cloned.1.call-update) | async-done | bytes 1441808 | tf_op jit(solution)/shard_map/reduce_scatter | solution.py:322
  (189 shorter events, 19.2 us)
Async XLA Ops:
  7.2 2.3 copy-start
  7.2 97.8 %all-reduce.8.cloned.1.call-start = ((), (), s32[]{:S(2)}) async-start(), calls=%async_computation.8 | async-start | bytes 2097152 | tf_op jit(solution)/shard_map/psum | solution.py:171
  7.3 12.1 copy-start.13
  9.5 24.3 %copy-start.31 = (f32[256]{0:T(256)}, f32[256]{0:T(256)S(1)}, u32[]{:S(2)}) copy-start(f32[256]{0:T(256)S(1)} %get-tuple-element.525) | copy-start | bytes 3076
  9.5 10.1 copy-start.1
  9.5 10.1 copy-start.25
  20.4 17.0 %copy-start.21 = (f32[256,32]{0,1:T(8,128)}, f32[256,32]{0,1:T(8,128)S(1)}, u32[]{:S(2)}) copy-start(f32[256,32]{0,1:T(8,128)S(1)} %get-tuple-element.522) | copy-start | bytes 98308
  20.4 17.0 %copy-start.23 = (f32[256,32]{0,1:T(8,128)}, f32[256,32]{0,1:T(8,128)S(1)}, u32[]{:S(2)}) copy-start(f32[256,32]{0,1:T(8,128)S(1)} %get-tuple-element.523) | copy-start | bytes 98308
  26.4 7.3 copy-start.10
  46.7 5.4 copy-start.19
  46.8 0.8 copy-start.11
  52.1 55.3 %copy-start.28 = (f32[2048]{0:T(1024)S(1)}, f32[2048]{0:T(1024)}, u32[]{:S(2)}) copy-start(f32[2048]{0:T(1024)} %param.26) | copy-start | bytes 24580
  52.1 140.4 %all-reduce.10.cloned.1.call-start = ((), (), s32[]{:S(2)}) async-start(), calls=%async_computation.9 | async-start | bytes 2097152 | tf_op jit(solution)/shard_map/psum | solution.py:196
  105.0 2.4 copy-start.2
  107.3 10.2 copy-start.33
  107.3 10.2 slice-start
  107.8 9.7 copy-start.5
  107.9 9.7 slice-start.1
  107.9 9.7 slice-start.2
  117.5 4.7 copy-start.6
  136.8 7.1 copy-start.17
  136.8 7.1 copy-start.18
  152.3 106.9 %reduce-scatter.9.cloned.1.call-start = ((), (), s32[]{:S(2)}) async-start(), calls=%async_computation.10 | async-start | bytes 655360 | tf_op jit(solution)/shard_map/reduce_scatter | solution.py:272
  157.8 37.2 %copy-start.29 = (f32[2048]{0:T(1024)S(1)}, f32[2048]{0:T(1024)}, u32[]{:S(2)}) copy-start(f32[2048]{0:T(1024)} %param.26) | copy-start | bytes 24580
  157.8 37.2 %copy-start.34 = (f32[256]{0:T(256)S(1)}, f32[256]{0:T(256)}, u32[]{:S(2)}) copy-start(f32[256]{0:T(256)} %copy-done.33) | copy-start | bytes 3076
  157.8 37.2 %copy-start.38 = (f32[256]{0:T(256)S(1)}, f32[256]{0:T(256)}, u32[]{:S(2)}) copy-start(f32[256]{0:T(256)} %get-tuple-element.526) | copy-start | bytes 3076
  192.6 2.5 copy-start.3
  192.6 2.5 copy-start.7
  192.6 2.5 copy-start.8
  195.1 4.7 copy-start.20
  203.2 0.8 copy-start.37
  203.2 1.0 copy-start.41
  204.3 0.9 copy-start.36
  220.9 106.0 %all-reduce.12.cloned.1.call-start = ((), (), s32[]{:S(2)}) async-start(), calls=%async_computation.18 | async-start | bytes 4194304 | tf_op jit(solution)/shard_map/psum | solution.py:183
  221.1 9.0 copy-start.22
  221.2 9.0 copy-start.24
  221.2 10.0 copy-start.9
  230.4 0.8 copy-start.15
  231.2 29.0 %copy-start.14 = (bf16[2048,128]{1,0:T(8,128)(2,1)S(1)}, bf16[2048,128]{1,0:T(8,128)(2,1)}, u32[]{:S(2)}) copy-start(bf16[2048,128]{1,0:T(8,128)(2,1)} %param.23) | copy-start | bytes 1572868
  260.1 2.1 copy-start.27
  262.2 1.5 copy-start.26
  262.2 1.5 copy-start.32
  263.7 132.2 %reduce-scatter.13.cloned.1.call-start = ((), (), s32[]{:S(2)}) async-start(), calls=%async_computation.12 | async-start | bytes 1114112 | tf_op jit(solution)/shard_map/reduce_scatter | solution.py:316
  265.4 1.7 copy-start.4
  265.4 1.7 copy-start.12
  265.4 1.8 copy-start.30
  265.4 1.8 copy-start.35
  265.4 1.8 copy-start.39
  265.4 184.0 %reduce-scatter.15.cloned.1.call-start = ((), (), s32[]{:S(2)}) async-start(), calls=%async_computation.13 | async-start | bytes 1114112 | tf_op jit(solution)/shard_map/reduce_scatter | solution.py:317
  267.1 290.9 %reduce-scatter.17.cloned.1.call-start = ((), (), s32[]{:S(2)}) async-start(), calls=%async_computation.14 | async-start | bytes 8912896 | tf_op jit(solution)/shard_map/reduce_scatter | solution.py:318
  273.7 1.0 copy-start.16
  273.7 393.3 %reduce-scatter.11.cloned.1.call-start = ((), (), s32[]{:S(2)}) async-start(), calls=%async_computation.11 | async-start | bytes 8912896 | tf_op jit(solution)/shard_map/reduce_scatter | solution.py:315
  279.5 618.8 %reduce-scatter.21.cloned.1.call-start = ((), (), s32[]{:S(2)}) async-start(), calls=%async_computation.16 | async-start | bytes 24510464 | tf_op jit(solution)/shard_map/reduce_scatter | solution.py:321
  292.4 836.5 %reduce-scatter.19.cloned.1.call-start = ((), (), s32[]{:S(2)}) async-start(), calls=%async_computation.15 | async-start | bytes 24510464 | tf_op jit(solution)/shard_map/reduce_scatter | solution.py:320
  306.1 1053.5 %reduce-scatter.23.cloned.1.call-start = ((), (), s32[]{:S(2)}) async-start(), calls=%async_computation.17 | async-start | bytes 24510464 | tf_op jit(solution)/shard_map/reduce_scatter | solution.py:322
  318.6 0.7 copy-start.42
  318.6 72.7 %copy-start.40 = (f32[256]{0:T(256)S(1)}, f32[256]{0:T(256)}, u32[]{:S(2)}) copy-start(f32[256]{0:T(256)} %get-tuple-element.524) | copy-start | bytes 3076
Sparse Core Ops, SparseCore 0:
  52.2 52.7 all-reduce.7
  152.5 40.0 all-reduce.9
  221.0 38.1 reduce-scatter.8
  263.9 63.0 all-reduce.11
  331.0 57.3 reduce-scatter.12
  392.9 56.4 reduce-scatter.14
  454.0 103.8 reduce-scatter.16
  562.6 104.3 reduce-scatter.10
  671.7 226.5 reduce-scatter.20
  902.8 225.9 reduce-scatter.18
  1133.5 225.9 reduce-scatter.22
where the time goes:
time: 1370 us
  waiting for transfers between devices  1080 us (79%)
  matrix products  135 us (10%)
  blocking collectives  74.4 us (5%)
  local copies, waits for them, and re-layouts  35.7 us (3%)
  other arithmetic  18.7 us (1%)
  between operations  15.4 us (1%)
    reduce_scatter x1, waiting for transfers between devices, on_device(): lax.psum_scatter(up_sum, ('dp', 'context'), scatter_dimension=0, tiled=True)  231 us
    reduce_scatter x1, waiting for transfers between devices, on_device(): lax.psum_scatter(down_sum, ('dp', 'context'), scatter_dimension=1, tiled=...  231 us
    reduce_scatter x1, waiting for transfers between devices, on_device(): lax.psum_scatter(gate_sum, ('dp', 'context'), scatter_dimension=0, tiled=...  231 us
    reduce_scatter x1, waiting for transfers between devices, on_device(): lax.psum_scatter(query_sum, ('dp', 'context'), scatter_dimension=0, tiled...  109 us
    reduce_scatter x1, waiting for transfers between devices, on_device(): lax.psum_scatter(out_sum, ('dp', 'context'), scatter_dimension=1, tiled=T...  109 us
    unnamed x1, blocking collectives  61.3 us
    reduce_scatter x1, waiting for transfers between devices, on_device(): lax.psum_scatter(value_sum, ('dp', 'context'), scatter_dimension=0, tiled...  53.5 us
    psum x1, waiting for transfers between devices, on_device(): lax.psum(jnp.dot(attn_b, output_matrix, preferred_element_type=single_flo...  52.6 us
  transfers between devices with their start and end apart: 11, of which 10 were waited for; matrix products, arithmetic and copies ran while one was open for 6% of the time, Pallas kernels for 0%

commit v1 on v0

v1 whole, which is shorter than its diff:
```python
import math
from functools import partial

import jax
import jax.numpy as jnp
from jax import lax
from jax.experimental import pallas as pl
from jax.experimental.pallas import tpu as pltpu
from jax.sharding import PartitionSpec as P

HEAD_WIDTH = 64
EPS = 1e-05
ROPE_BASE = 10000.0
NEG_FILL = -1e30
F32 = jnp.float32
BF16 = jnp.bfloat16


def rope_angles(positions, head_size):
    half_size = head_size // 2
    frequencies = jnp.exp(
        jnp.arange(half_size, dtype=jnp.float32) * (-2.0 * math.log(ROPE_BASE) / head_size)
    )
    return positions.astype(jnp.float32)[:, None] * frequencies[None, :]


def apply_rotary(heads_in, cosine_rows, sine_rows):
    half_size = heads_in.shape[-1] // 2
    first_half = heads_in[..., :half_size]
    second_half = heads_in[..., half_size:]
    return jnp.concatenate(
        [
            first_half * cosine_rows - second_half * sine_rows,
            second_half * cosine_rows + first_half * sine_rows,
        ],
        axis=-1,
    )


def inverse_rotary(heads_in, cosine_rows, sine_rows):
    return apply_rotary(heads_in, cosine_rows, -sine_rows)


def rms_scale(values_in):
    return lax.rsqrt(jnp.mean(values_in * values_in, axis=-1, keepdims=True) + EPS)


def norm_backward(d_normed, inputs_f, inv_rms, gain_in):
    scaled = d_normed * gain_in
    return inv_rms * scaled - inputs_f * (inv_rms * inv_rms * inv_rms) * jnp.mean(
        scaled * inputs_f, axis=-1, keepdims=True
    )


def dot_nn(a, b):
    return lax.dot_general(a, b, (((1,), (0,)), ((), ())), preferred_element_type=F32)


def dot_nt(a, b):
    return lax.dot_general(a, b, (((1,), (1,)), ((), ())), preferred_element_type=F32)


def dot_tn(a, b):
    return lax.dot_general(a, b, (((0,), (0,)), ((), ())), preferred_element_type=F32)


def swap(value, axis, flip):
    count = lax.axis_size(axis)
    return lax.ppermute(value, axis, [(i, i ^ flip) for i in range(count)])


def sum_pair(part):
    total = part.astype(BF16)
    flip = 1
    while flip < lax.axis_size("tensor"):
        other = swap(total, "tensor", flip)
        total = total.astype(F32) + other.astype(F32)
        flip *= 2
    return total


def gather_context(value):
    pieces = []
    for k in range(lax.axis_size("context")):
        if k == 0:
            pieces.append(value)
        elif k % 2 == 0:
            pieces.append(swap(value, "context", k))
        else:
            pieces.append(swap(pieces[k - 1], "context", 1))
    return pieces


def spread_columns(value):
    dp_count, ctx_count = lax.axis_size("dp"), lax.axis_size("context")
    here = lax.axis_index("context")
    tokens, width = value.shape
    blocks = value.reshape(tokens, dp_count, ctx_count, width // (dp_count * ctx_count))
    pieces = []
    for k in range(ctx_count):
        mine = lax.dynamic_index_in_dim(blocks, here ^ k, 2, keepdims=False)
        mine = mine.reshape(tokens, width // ctx_count)
        pieces.append(mine if k == 0 else swap(mine, "context", k))
    return pieces


def ring_sum(chunk_of):
    count = lax.axis_size("dp")
    here = lax.axis_index("dp")
    ring = [(i, (i + 1) % count) for i in range(count)]
    total = chunk_of((here - 1) % count).astype(BF16)
    for step in range(1, count):
        arrived = lax.ppermute(total, "dp", ring)
        total = arrived.astype(F32) + chunk_of((here - 1 - step) % count).astype(F32)
        if step < count - 1:
            total = total.astype(BF16)
    return total


def scatter_gain(value):
    dp_count, ctx_count = lax.axis_size("dp"), lax.axis_size("context")
    dp_here, ctx_here = lax.axis_index("dp"), lax.axis_index("context")
    blocks = value.reshape(dp_count, ctx_count, -1)
    total = lax.dynamic_index_in_dim(blocks, ctx_here, 1, keepdims=False)
    for k in range(1, ctx_count):
        total = total + swap(
            lax.dynamic_index_in_dim(blocks, ctx_here ^ k, 1, keepdims=False), "context", k
        )
    result = lax.dynamic_index_in_dim(total, dp_here, 0, keepdims=False)
    for k in range(1, dp_count):
        result = result + swap(
            lax.dynamic_index_in_dim(total, dp_here ^ k, 0, keepdims=False), "dp", k
        )
    return result


def grad_kernel(count, left_is_wide, *refs):
    narrow_refs, wide_refs, out_ref = refs[:count], refs[count : 2 * count], refs[-1]
    total = None
    for narrow_ref, wide_ref in zip(narrow_refs, wide_refs):
        if left_is_wide:
            term = dot_tn(wide_ref[...], narrow_ref[...])
        else:
            term = dot_tn(narrow_ref[...], wide_ref[...])
        total = term if total is None else total + term
    out_ref[...] = total.astype(out_ref.dtype)


def pick_block(size, largest):
    for block in range(largest, 0, -128):
        if size % block == 0:
            return block
    return size


def grad_product(narrow, wide, left_is_wide=False):
    count = len(narrow)
    tokens, rows = narrow[0].shape
    columns = wide[0].shape[1]
    block = pick_block(columns, 512)
    narrow_spec = pl.BlockSpec((tokens, rows), lambda j: (0, 0))
    wide_spec = pl.BlockSpec((tokens, block), lambda j: (0, j))
    if left_is_wide:
        out_shape, out_spec = (columns, rows), pl.BlockSpec((block, rows), lambda j: (j, 0))
    else:
        out_shape, out_spec = (rows, columns), pl.BlockSpec((rows, block), lambda j: (0, j))
    return pl.pallas_call(
        partial(grad_kernel, count, left_is_wide),
        grid=(columns // block,),
        in_specs=[narrow_spec] * count + [wide_spec] * count,
        out_specs=out_spec,
        out_shape=jax.ShapeDtypeStruct(out_shape, BF16),
        compiler_params=pltpu.CompilerParams(vmem_limit_bytes=32 * 1024 * 1024),
        cost_estimate=pl.CostEstimate(
            flops=2 * count * tokens * rows * columns,
            bytes_accessed=2 * (count * tokens * (rows + columns) + rows * columns),
            transcendentals=0,
        ),
    )(*narrow, *wide)


def row_share(narrow, wide):
    dp_count = lax.axis_size("dp")
    product = grad_product(narrow, wide)
    chunks = product.reshape(dp_count, product.shape[0] // dp_count, product.shape[1])
    return ring_sum(lambda d: lax.dynamic_index_in_dim(chunks, d, 0, keepdims=False))


def column_share(wide, narrow):
    dp_count = lax.axis_size("dp")
    product = grad_product(narrow, wide, left_is_wide=True)
    chunks = product.reshape(product.shape[0], dp_count, product.shape[1] // dp_count)
    return ring_sum(lambda d: lax.dynamic_index_in_dim(chunks, d, 1, keepdims=False))


def attend_piece(query_rows, query_pos, score_scale, state_in, kv_piece, offset):
    run_max, run_sum, accum = state_in
    key_heads, value_heads = kv_piece
    key_count = key_heads.shape[0]
    scores = (
        jnp.einsum("qngd,knd->qngk", query_rows, key_heads, preferred_element_type=F32)
        * score_scale
    )
    key_pos = offset + jnp.arange(key_count, dtype=jnp.int32)
    allowed = (query_pos[:, None] >= key_pos[None, :])[:, None, None, :]
    new_max = jnp.maximum(run_max, jnp.max(jnp.where(allowed, scores, NEG_FILL), axis=-1))
    factor = jnp.exp(run_max - new_max)
    weights = jnp.where(allowed, jnp.exp(scores - new_max[..., None]), 0.0)
    new_sum = run_sum * factor + jnp.sum(weights, axis=-1)
    new_accum = accum * factor[..., None] + jnp.einsum(
        "qngk,knd->qngd", weights.astype(BF16), value_heads, preferred_element_type=F32
    )
    return (new_max, new_sum, new_accum)


def on_device(
    layer_input,
    cotangent,
    attn_gain,
    query_weight,
    key_matrix,
    value_matrix,
    output_matrix,
    feed_gain,
    gate_weight,
    up_weight,
    down_weight,
):
    block_shape = layer_input.shape
    tok_here = block_shape[0] * block_shape[1]
    width = block_shape[2]
    layer_input = layer_input.reshape(tok_here, width)
    cotangent = cotangent.reshape(tok_here, width)
    head_size = HEAD_WIDTH
    q_local = query_weight.shape[1] // head_size
    kv_local = key_matrix.shape[1] // head_size
    group_size = q_local // kv_local
    score_scale = 1.0 / math.sqrt(head_size)
    ctx_count = lax.axis_size("context")
    first_pos = lax.axis_index("context") * tok_here
    query_pos = first_pos + jnp.arange(tok_here, dtype=jnp.int32)
    last_pos = first_pos + tok_here - 1
    angles = rope_angles(query_pos, head_size)
    cosine_rows = jnp.cos(angles)[:, None, :]
    sine_rows = jnp.sin(angles)[:, None, :]

    cot_cols = spread_columns(cotangent)
    inputs_f = layer_input.astype(F32)
    attn_rms = rms_scale(inputs_f)
    first_normed = (inputs_f * attn_rms * attn_gain).astype(BF16)
    query_rows = apply_rotary(
        dot_nn(first_normed, query_weight).reshape(tok_here, q_local, head_size),
        cosine_rows,
        sine_rows,
    ).astype(BF16)
    query_rows = query_rows.reshape(tok_here, kv_local, group_size, head_size)
    rotated_keys = (
        apply_rotary(
            dot_nn(first_normed, key_matrix).reshape(tok_here, kv_local, head_size),
            cosine_rows,
            sine_rows,
        )
        .astype(BF16)
        .reshape(tok_here, kv_local * head_size)
    )
    value_rows = dot_nn(first_normed, value_matrix).astype(BF16)
    kv_own = jnp.concatenate([rotated_keys, value_rows], axis=-1)
    kv_whole = lax.all_gather(kv_own, "context", axis=0, tiled=True)
    kv_stack = kv_whole.reshape(ctx_count, tok_here, 2, kv_local, head_size)
    first_cols = spread_columns(first_normed)

    stat_shape = (tok_here, kv_local, group_size)
    initial_state = (
        jnp.full(stat_shape, NEG_FILL, F32),
        jnp.zeros(stat_shape, F32),
        jnp.zeros(stat_shape + (head_size,), F32),
    )
    block_ids = jnp.arange(ctx_count, dtype=jnp.int32)

    def scan_piece(state_in, inputs):
        kv_block, block_index = inputs
        offset = block_index * tok_here
        state = lax.cond(
            offset <= last_pos,
            lambda s: attend_piece(
                query_rows, query_pos, score_scale, s, (kv_block[:, 0], kv_block[:, 1]), offset
            ),
            lambda s: s,
            state_in,
        )
        return (state, None)

    (run_max, run_sum, accum), _ = lax.scan(scan_piece, initial_state, (kv_stack, block_ids))
    logsum_total = run_max + jnp.log(run_sum)
    attention_float = accum / run_sum[..., None]
    attn_b = attention_float.reshape(tok_here, q_local * head_size).astype(BF16)
    resid = inputs_f + sum_pair(dot_nn(attn_b, output_matrix))
    feed_rms = rms_scale(resid)
    normed_two = (resid * feed_rms * feed_gain).astype(BF16)
    gate_values = dot_nn(normed_two, gate_weight)
    up_values = dot_nn(normed_two, up_weight)
    sigmoid_gate = jax.nn.sigmoid(gate_values)
    activated = gate_values * sigmoid_gate
    hidden = (activated * up_values).astype(BF16)
    hidden_all = gather_context(hidden)
    down_share = column_share(hidden_all, cot_cols)
    d_hidden = dot_nt(cotangent, down_weight)
    d_gate = (
        d_hidden * up_values * (sigmoid_gate * (1.0 + gate_values * (1.0 - sigmoid_gate)))
    ).astype(BF16)
    d_up = (d_hidden * activated).astype(BF16)
    two_cols = spread_columns(normed_two)
    gate_share = row_share(two_cols, gather_context(d_gate))
    up_share = row_share(two_cols, gather_context(d_up))
    d_normed_two = sum_pair(dot_nt(d_gate, gate_weight) + dot_nt(d_up, up_weight))
    layer_output = (resid + sum_pair(dot_nn(hidden, down_weight))).astype(BF16)
    feed_gain_sum = jnp.sum(d_normed_two * resid * feed_rms, axis=0)
    d_resid = cotangent.astype(F32) + norm_backward(d_normed_two, resid, feed_rms, feed_gain)
    d_resid_b = d_resid.astype(BF16)
    out_share = column_share(gather_context(attn_b), spread_columns(d_resid_b))
    attention_grad = dot_nt(d_resid_b, output_matrix).reshape(
        tok_here, kv_local, group_size, head_size
    )
    d_attn_b = attention_grad.astype(BF16)
    row_delta = jnp.sum(attention_grad * attention_float, axis=-1)

    def back_piece(query_delta, inputs):
        kv_block, block_index = inputs
        key_block, value_block = kv_block[:, 0], kv_block[:, 1]
        offset = block_index * tok_here

        def compute(delta_in):
            scores = (
                jnp.einsum("qngd,knd->qngk", query_rows, key_block, preferred_element_type=F32)
                * score_scale
            )
            key_pos = offset + jnp.arange(tok_here, dtype=jnp.int32)
            allowed = (query_pos[:, None] >= key_pos[None, :])[:, None, None, :]
            probs = jnp.where(allowed, jnp.exp(scores - logsum_total[..., None]), 0.0)
            d_probs = jnp.einsum(
                "qngd,knd->qngk", d_attn_b, value_block, preferred_element_type=F32
            )
            d_scores_b = (probs * (d_probs - row_delta[..., None]) * score_scale).astype(BF16)
            delta_out = delta_in + jnp.einsum(
                "qngk,knd->qngd", d_scores_b, key_block, preferred_element_type=F32
            )
            d_key = jnp.einsum(
                "qngk,qngd->knd", d_scores_b, query_rows, preferred_element_type=F32
            )
            d_value = jnp.einsum(
                "qngk,qngd->knd", probs.astype(BF16), d_attn_b, preferred_element_type=F32
            )
            return (delta_out, d_key, d_value)

        def skip_piece(delta_in):
            zero_block = jnp.zeros(key_block.shape, F32)
            return (delta_in, zero_block, zero_block)

        delta_next, d_key, d_value = lax.cond(offset <= last_pos, compute, skip_piece, query_delta)
        return (delta_next, jnp.concatenate([d_key, d_value], axis=1).astype(BF16))

    zero_query = jnp.zeros((tok_here, kv_local, group_size, head_size), F32)
    query_delta, kv_parts = lax.scan(back_piece, zero_query, (kv_stack, block_ids))
    kv_parts = kv_parts.reshape(ctx_count, tok_here, 2 * kv_local * head_size)
    ctx_here = lax.axis_index("context")
    kv_back = lax.dynamic_index_in_dim(kv_parts, ctx_here, 0, keepdims=False).astype(F32)
    for k in range(1, ctx_count):
        kv_back = kv_back + swap(
            lax.dynamic_index_in_dim(kv_parts, ctx_here ^ k, 0, keepdims=False), "context", k
        ).astype(F32)
    key_local = kv_back[:, : kv_local * head_size].reshape(tok_here, kv_local, head_size)
    d_query_b = (
        inverse_rotary(
            query_delta.reshape(tok_here, q_local, head_size), cosine_rows, sine_rows
        )
        .reshape(tok_here, q_local * head_size)
        .astype(BF16)
    )
    d_key_b = (
        inverse_rotary(key_local, cosine_rows, sine_rows)
        .reshape(tok_here, kv_local * head_size)
        .astype(BF16)
    )
    d_value_b = kv_back[:, kv_local * head_size :].astype(BF16)
    d_qkv = jnp.concatenate([d_query_b, d_key_b, d_value_b], axis=-1)
    qkv_share = row_share(first_cols, gather_context(d_qkv))
    d_normed_one = sum_pair(
        dot_nt(d_query_b, query_weight)
        + dot_nt(d_key_b, key_matrix)
        + dot_nt(d_value_b, value_matrix)
    )
    attn_gain_sum = jnp.sum(d_normed_one * inputs_f * attn_rms, axis=0)
    input_grad = (d_resid + norm_backward(d_normed_one, inputs_f, attn_rms, attn_gain)).astype(BF16)
    q_width, kv_width = q_local * head_size, kv_local * head_size
    return (
        layer_output.reshape(block_shape),
        input_grad.reshape(block_shape),
        scatter_gain(attn_gain_sum),
        qkv_share[:, :q_width],
        qkv_share[:, q_width : q_width + kv_width],
        qkv_share[:, q_width + kv_width :],
        out_share,
        scatter_gain(feed_gain_sum),
        gate_share,
        up_share,
        down_share,
    )


def solution(mesh):
    in_specs = (
        P("context", "dp", None),
        P("context", "dp", None),
        P(),
        P(None, "tensor"),
        P(None, "tensor"),
        P(None, "tensor"),
        P("tensor", None),
        P(),
        P(None, "tensor"),
        P(None, "tensor"),
        P("tensor", None),
    )
    out_specs = (
        P("context", "dp", None),
        P("context", "dp", None),
        P(("dp", "context")),
        P(("dp", "context"), "tensor"),
        P(("dp", "context"), "tensor"),
        P(("dp", "context"), "tensor"),
        P("tensor", ("dp", "context")),
        P(("dp", "context")),
        P(("dp", "context"), "tensor"),
        P(("dp", "context"), "tensor"),
        P("tensor", ("dp", "context")),
    )
    return jax.shard_map(
        on_device, mesh=mesh, in_specs=in_specs, out_specs=out_specs, check_vma=False
    )
```

time: 1370 us -> 571 us (0.42)
  waiting for transfers between devices: 1080 us -> 248 us
  matrix products: 135 us -> 66.5 us
  blocking collectives: 74.4 us -> 8.65 us
  starting transfers between devices: 1.05 us -> 65.5 us
  local copies, waits for them, and re-layouts: 35.7 us -> 98 us
  Pallas kernels: 0 us -> 33.2 us
  other arithmetic: 18.7 us -> 35.4 us
    reduce_scatter x8 -> x0, waiting for transfers between devices: 989 us -> none  [the longest x1 231 us: on_device(): lax.psum_scatter(up_sum, ('dp', 'context'), scatter_dimension=0, tiled=True)]
    ppermute x0 -> x61, waiting for transfers between devices: none -> 248 us  [the longest x15 141 us: ring_sum(): arrived = lax.ppermute(total, 'dp', ring)]
    psum x3 -> x0, waiting for transfers between devices: 91.3 us -> none  [the longest x1 52.6 us: on_device(): lax.psum(jnp.dot(attn_b, output_matrix, preferred_element_type=single_flo...]
    dot_general x28 -> x21, matrix products: 135 us -> 66.5 us  [the longest x7 30.6 us: dot_nt(): lax.dot_general(a, b, (((1,), (1,)), ((), ())), preferred_element_type=F32)]
    ppermute x0 -> x61, starting transfers between devices: none -> 65.5 us  [the longest x46 57.8 us: swap(): return lax.ppermute(value, axis, [(i, i ^ flip) for i in range(count)])]
    unnamed x1 -> x0, blocking collectives: 61.3 us -> none
    dynamic_slice x9 -> x19, local copies, waits for them, and re-layouts: 8.27 us -> 44.8 us  [the longest x4 23.5 us: spread_columns(): mine = lax.dynamic_index_in_dim(blocks, here ^ k, 2, keepdims=False)]
    pallas_call x0 -> x5, Pallas kernels: none -> 33.2 us  [grad_product(): pl.pallas_call(partial(grad_kernel, count, left_is_wide), grid=(columns /...]
  transfers between devices with their start and end apart: 11 -> 61, of which waited for: 10 -> 18; matrix products, arithmetic and copies ran while one was open for 6% -> 30% of each run, Pallas kernels for 0% -> 6%
where the time goes in v1:
time: 571 us; the launch traced here: 563 us
  waiting for transfers between devices  248 us (43%)
  local copies, waits for them, and re-layouts  98 us (17%)
  matrix products  66.5 us (12%)
  starting transfers between devices  65.5 us (11%)
  other arithmetic  35.4 us (6%)
  Pallas kernels  33.2 us (6%)
  blocking collectives  8.65 us (2%)
  loops' own time  5.77 us (1%)
    ppermute x15, waiting for transfers between devices, ring_sum(): arrived = lax.ppermute(total, 'dp', ring)  141 us
    ppermute x46, waiting for transfers between devices, swap(): return lax.ppermute(value, axis, [(i, i ^ flip) for i in range(count)])  107 us
    ppermute x46, starting transfers between devices, swap(): return lax.ppermute(value, axis, [(i, i ^ flip) for i in range(count)])  57.8 us
    pallas_call x5, Pallas kernels, grad_product(): pl.pallas_call(partial(grad_kernel, count, left_is_wide), grid=(columns /...  33.2 us
    dot_general x7, matrix products, dot_nt(): lax.dot_general(a, b, (((1,), (1,)), ((), ())), preferred_element_type=F32)  30.6 us
    dot_general x7, matrix products, dot_nn(): lax.dot_general(a, b, (((1,), (0,)), ((), ())), preferred_element_type=F32)  29.7 us
    unnamed x106, local copies, waits for them, and re-layouts  27.5 us
    dynamic_slice x4, local copies, waits for them, and re-layouts, spread_columns(): mine = lax.dynamic_index_in_dim(blocks, here ^ k, 2, keepdims=False)  23.5 us
  transfers between devices with their start and end apart: 61, of which 18 were waited for; matrix products, arithmetic and copies ran while one was open for 30% of the time, Pallas kernels for 6%

profile of v1, /device:TPU:0, one launch (start us, length us, event | category | flops | bytes accessed | tf_op | source)
XLA Modules:
  0.0 562.9 jit_solution(8139014138246531443)
XLA Ops:
  5.0 8.6 %all_gather.3 = bf16[1024,256]{0,1:T(8,128)(2,1)S(1)} all-gather(bf16[256,256]{0,1:T(8,128)(2,1)S(1)} %pad_maximum_fusion.3), channel_id=1, replica_groups=mesh['tensor'=2,'dp'=4,'context'=4] {'context'}, dimensions={0}, use_global_device_ids=true | all-gather | bytes 655360 | tf_op jit(solution)/shard_map/all_gather | solution.py:268
  14.2 6.5 %copy.62 = bf16[2048,1024]{0,1:T(8,128)(2,1)} copy(bf16[2048,1024]{1,0:T(8,128)(2,1)} %param.22) | data formatting | bytes 8388608 | tf_op args[3]
  20.6 3.5 fusion.83
  24.5 8.1 %while.31 = (s32[]{:T(128)}, f32[256,2,8]{0,2,1:T(8,128)S(1)}, f32[256,2,8]{0,2,1:T(8,128)S(1)}, f32[256,2,8,64]{0,3,2,1:T(8,128)S(1)}, s32[4]{0:T(128)S(1)}, /*...) while((s32[]{:T(128)}, f32[256,2,8]{0,2,1:T(8,128)S(1)}, ...), condition=%wide.region_6.7_spmd.clone, body=%wide.region_1.6_spmd.clone.sunk | while | flops 280568320 | bytes 16128287 | solution.py:293
  25.8 3.0 conditional.6
  35.2 7.1 %collective-permute-start.26 = (bf16[256,1024]{1,0:T(8,128)(2,1)S(1)}, bf16[256,1024]{1,0:T(8,128)(2,1)S(1)}, u32[]{:S(2)}, u32[]{:S(2)}) collective-permute-start(bf16[256,1024]{1,0:T(8,128)(2,1)S(1)} %copy.81.refs_4_), channel_id=1, source_target_pairs={{0,2},{1,3},{2,0},{3,1},{4,6},{5,7},{6,4},{7,5},{8,10},{9,11},{10,... | collective-permute-start | bytes 1572872 | tf_op jit(solution)/shard_map/ppermute | solution.py:69
  42.3 3.0 collective-permute-start.25
  45.3 4.6 convolution_convert_fusion.1
  51.4 2.7 reshape_reshape.3
  54.1 9.8 %dynamic-slice_reduce_fusion = (bf16[256,4,128]{2,1,0:T(4,128)(2,1)}, bf16[256,4,128]{2,1,0:T(4,128)(2,1)S(1)}, bf16[256,4,128]{2,1,0:T(4,128)(2,1)S(1)}, bf16[256,4,128]{2,1,0:T(4,128)(2,1)}) fusion(bf16[256,4,4,128]{3,2,1,0:T(4,128)(2,1)} %reshape_reshape.3, s32[]{:T(128)S(6)} %select_n.156, s32[]{:T(128)S(6)} %select_n.155, s32[]{:T(128)S(6)} %select_n.154, ...), kind=kLoop, calls=%fused_computation.139 | loop fusion | bytes 2097168 | tf_op jit(solution)/shard_map/jit(dynamic_index_in_dim)/dynamic_slice | solution.py:101
  63.9 3.7 reshape.477
  69.1 6.7 %fusion.74 = f32[256,2816]{1,0:T(8,128)S(1)} fusion(bf16[2816,2048]{1,0:T(8,128)(2,1)} %param.29, bf16[256,1,2048]{2,0,1:T(8,128)(2,1)} %param.20), kind=kOutput, calls=%fused_computation.115 | convolution fusion | flops 2952790016 | bytes 15466496 | tf_op jit(solution)/shard_map/dot_general | solution.py:60
  75.8 2.1 multiply_reduce_fusion.2
  78.3 6.8 %fusion.107 = f32[256,2816]{1,0:T(8,128)S(1)} fusion(bf16[256,2048]{1,0:T(8,128)(2,1)S(1)} %multiply_convert_fusion.3, bf16[2048,2816]{1,0:T(8,128)(2,1)} %param.28), kind=kOutput, calls=%fused_computation.254 | convolution fusion | flops 2952790016 | bytes 15466496 | tf_op jit(solution)/shard_map/dot_general | solution.py:56
  86.1 6.0 %multiply_convert_fusion = (bf16[256,2816]{1,0:T(8,128)(2,1)}, bf16[256,2816]{1,0:T(8,128)(2,1)}, bf16[256,2816]{1,0:T(8,128)(2,1)S(1)}) fusion(f32[256,2816]{1,0:T(8,128)S(1)} %fusion.74, f32[256,2816]{1,0:T(8,128)S(1)} %fusion.107, bf16[256,2048]{1,0:T(8,128)(2,1)S(1)} %multiply_convert_fusion.3, bf16[2048,2816]{1,0:T(8,128)(2,1)S(1)} %bitcast.467), kind=kOutput, calls=%fused_computation.52 | convolution fusion | flops 2963603456 | bytes 22675456 | tf_op jit(solution)/shard_map/dot_general | solution.py:56
  92.1 7.0 %fusion.108 = f32[256,2048]{1,0:T(8,128)S(1)} fusion(bf16[256,2816]{1,0:T(8,128)(2,1)} %get-tuple-element.423.refs_4_, bf16[2048,2816]{1,0:T(8,128)(2,1)} %param.27), kind=kOutput, calls=%fused_computation.255 | convolution fusion | flops 2952790016 | bytes 15073280 | tf_op jit(solution)/shard_map/dot_general | solution.py:60
  99.1 7.9 %fusion.46 = bf16[256,2048]{1,0:T(8,128)(2,1)S(1)} fusion(f32[256,2048]{1,0:T(8,128)S(1)} %fusion.108, bf16[256,2816]{1,0:T(8,128)(2,1)} %get-tuple-element.422.refs_4_, bf16[2048,2816]{1,0:T(8,128)(2,1)} %param.28), kind=kOutput, calls=%fused_computation.60 | convolution fusion | flops 2953838592 | bytes 16121856 | tf_op jit(solution)/shard_map/dot_general | solution.py:60
  108.0 7.6 %convolution_convert_fusion = bf16[256,2048]{1,0:T(8,128)(2,1)S(1)} fusion(bf16[256,2816]{1,0:T(8,128)(2,1)S(1)} %get-tuple-element.424.refs_4_, bf16[2816,2048]{1,0:T(8,128)(2,1)} %param.29), kind=kOutput, calls=%fused_computation.61 | convolution fusion | flops 2953314304 | bytes 14024704 | tf_op jit(solution)/shard_map/dot_general | solution.py:56
  118.5 14.7 %collective-permute-done.2 = bf16[256,2048]{1,0:T(8,128)(2,1)S(1)} collective-permute-done((bf16[256,2048]{1,0:T(8,128)(2,1)S(1)}, bf16[256,2048]{1,0:T(8,128)(2,1)S(1)}, u32[]{:S(2)}, u32[]{:S(2)}) %collective-permute-start.2) | collective-permute-done | bytes 1048608 | tf_op jit(solution)/shard_map/ppermute | solution.py:69
  134.0 20.3 %collective-permute-done.1 = bf16[256,2048]{1,0:T(8,128)(2,1)S(1)} collective-permute-done((bf16[256,2048]{1,0:T(8,128)(2,1)S(1)}, bf16[256,2048]{1,0:T(8,128)(2,1)S(1)}, u32[]{:S(2)}, u32[]{:S(2)}) %collective-permute-start.1) | collective-permute-done | bytes 1048608 | tf_op jit(solution)/shard_map/ppermute | solution.py:69
  154.3 2.8 fusion.104
  158.1 2.1 multiply_reduce_fusion.3
  160.2 2.7 reshape.454
  164.0 13.6 %while.32 = (s32[]{:T(128)}, f32[256,2,8,64]{0,3,2,1:T(8,128)}, bf16[4,256,4,64]{1,3,2,0:T(8,128)(2,1)}, s32[4]{0:T(128)S(1)}, s32[]{:T(128)}, /*index=5*/bf16[4...) while((s32[]{:T(128)}, f32[256,2,8,64]{0,3,2,1:T(8,128)}, ...), condition=%wide.region_13.14_spmd.clone, body=%wide.region_10.13_spmd.clone.sunk | while | flops 683278848 | bytes 34659176 | solution.py:363
  165.2 5.7 %conditional.7 = (f32[256,2,8,64]{0,3,2,1:T(8,128)}, bf16[1,256,2,64]{1,3,2,0:T(8,128)(2,1)S(1)}, bf16[1,256,2,64]{1,3,2,0:T(8,128)(2,1)S(1)}) conditional(s32[]{:T(128)} %convert_element_type.612, f32[256,2,8,64]{0,3,2,1:T(8,128)} %get-tuple-element.674, (s32[]{:T(128)}, s32[]{:T(128)}, bf16[4,256,2,2,64]{1,4,3,2,0:T(8,128)(2,1)}, s32[]{:T(128)}, ...), branch_computations={%region_11.11_spmd, %region_12.12_spmd} | conditional | flops 683016704 | bytes 34395256 | solution.py:359
  179.4 4.5 collective-permute-start.3
  184.6 11.6 %collective-permute-start.4 = (bf16[256,256]{1,0:T(8,128)(2,1)}, bf16[256,256]{1,0:T(8,128)(2,1)}, u32[]{:S(2)}, u32[]{:S(2)}) collective-permute-start(bf16[256,256]{1,0:T(8,128)(2,1)} %bitcast.46), channel_id=1, source_target_pairs={{0,2},{1,3},{2,0},{3,1},{4,6},{5,7},{6,4},{7,5},{8,10},{9,11},{10,... | collective-permute-start | bytes 393224 | tf_op jit(solution)/shard_map/ppermute | solution.py:69
  199.2 5.1 fusion.109
  204.3 6.7 %dynamic-slice_reduce_fusion.8 = (bf16[256,4,128]{2,1,0:T(4,128)(2,1)S(1)}, bf16[256,4,128]{2,1,0:T(4,128)(2,1)S(1)}, bf16[256,4,128]{2,1,0:T(4,128)(2,1)S(1)}, bf16[256,4,128]{2,1,0:T(4,128)(2,1)S(1)}) fusion(bf16[256,4,4,128]{3,2,1,0:T(4,128)(2,1)S(1)} %copy-done.17, s32[]{:T(128)S(6)} %select_n.156, s32[]{:T(128)S(6)} %select_n.155, s32[]{:T(128)S(6)} %select_n.154, ...), kind=kLoop, calls=%fused_computation.147 | loop fusion | bytes 2097168 | tf_op jit(solution)/shard_map/jit(dynamic_index_in_dim)/dynamic_slice | solution.py:101
  213.5 2.0 collective-permute-start.23
  221.6 2.0 collective-permute-start.53
  225.1 3.1 collective-permute-done.24.refs_3_
  231.1 2.5 shard_map.195
  234.3 3.2 constant_dynamic-slice_fusion.12
  239.6 8.3 %collective-permute-done.28 = bf16[1024,128]{1,0:T(8,128)(2,1)S(1)} collective-permute-done((bf16[1024,128]{1,0:T(8,128)(2,1)S(1)}, bf16[1024,128]{1,0:T(8,128)(2,1)S(1)}, u32[]{:S(2)}, u32[]{:S(2)}) %collective-permute-start.28) | collective-permute-done | bytes 262176 | tf_op jit(solution)/shard_map/ppermute | solution.py:113
  254.5 4.0 collective-permute-done.29
  259.5 1.9 fusion.80
  261.4 6.7 %dynamic-slice_reduce_fusion.4 = (bf16[256,4,128]{2,1,0:T(4,128)(2,1)S(1)}, bf16[256,4,128]{2,1,0:T(4,128)(2,1)S(1)}, bf16[256,4,128]{2,1,0:T(4,128)(2,1)S(1)}, bf16[256,4,128]{2,1,0:T(4,128)(2,1)S(1)}) fusion(bf16[256,4,4,128]{3,2,1,0:T(4,128)(2,1)S(1)} %reshape.461, s32[]{:T(128)S(6)} %select_n.156, s32[]{:T(128)S(6)} %select_n.155, s32[]{:T(128)S(6)} %select_n.154, ...), kind=kLoop, calls=%fused_computation.143 | loop fusion | bytes 2097168 | tf_op jit(solution)/shard_map/jit(dynamic_index_in_dim)/dynamic_slice | solution.py:101
  275.7 2.1 convert_add_fusion.14
  277.8 4.1 collective-permute-done.14.refs_2_
  282.4 2.3 fusion.59
  284.7 15.0 %collective-permute-done.15.refs_3_ = bf16[256,512]{1,0:T(8,128)(2,1)S(1)} collective-permute-done((bf16[256,512]{1,0:T(8,128)(2,1)S(1)}, bf16[256,512]{1,0:T(8,128)(2,1)S(1)}, u32[]{:S(2)}, u32[]{:S(2)}) %collective-permute-start.15) | collective-permute-done | bytes 262176 | tf_op jit(solution)/shard_map/ppermute | solution.py:69
  302.6 31.7 %collective-permute-done.32 = f32[4,128]{1,0:T(4,128)S(1)} collective-permute-done((f32[4,128]{1,0:T(4,128)S(1)}, f32[4,128]{1,0:T(4,128)S(1)}, u32[]{:S(2)}, u32[]{:S(2)}) %collective-permute-start.32) | collective-permute-done | bytes 2080 | tf_op jit(solution)/shard_map/ppermute | solution.py:69
  335.5 3.3 fusion.71
  341.7 3.1 collective-permute-start.35
  344.8 2.3 collective-permute-start.36
  347.2 2.7 shard_map.194
  350.0 2.0 collective-permute-start.11
  352.0 2.3 collective-permute-start.12
  355.0 2.4 collective-permute-done.12
  358.6 14.9 %collective-permute-done.41.refs_6_ = bf16[256,2816]{1,0:T(8,128)(2,1)} collective-permute-done((bf16[256,2816]{1,0:T(8,128)(2,1)}, bf16[256,2816]{1,0:T(8,128)(2,1)}, u32[]{:S(2)}, u32[]{:S(2)}) %collective-permute-start.41) | collective-permute-done | bytes 1441824 | tf_op jit(solution)/shard_map/ppermute | solution.py:69
  374.5 8.7 %shard_map.198 = bf16[2816,512]{1,0:T(8,128)(2,1)S(1)} custom-call(bf16[256,512]{1,0:T(8,128)(2,1)S(1)} %bitcast.411, bf16[256,512]{1,0:T(8,128)(2,1)} %collective-permute-done.52.refs_1_, bf16[256,512]{1,0:T(8,128)(2,1)} %collective-permute-done.53.refs_2_, bf16[256,512]{1,0:T(8,128)(2,1)S(1)} %collective-permute-done.54.refs_3_, ...), custom_call_target="tpu_custom_call" | custom-call | flops 2952790016 | bytes 9699328 | tf_op jit(solution)/shard_map/pallas_call | solution.py:167
  384.8 6.0 %reshape.472 = bf16[2816,4,128]{2,1,0:T(4,128)(2,1)} reshape(bf16[2816,512]{1,0:T(8,128)(2,1)} %copy-done.1) | data formatting | bytes 5767168 | tf_op jit(solution)/shard_map/reshape | solution.py:192
  391.9 10.0 %constant_dynamic-slice_fusion = (bf16[2816,1,128]{2,1,0:T(2,128)(2,1)S(1)}, bf16[2816,1,128]{2,1,0:T(2,128)(2,1)S(1)}, bf16[2816,1,128]{2,1,0:T(2,128)(2,1)S(1)}, bf16[2816,1,128]{2,1,0:T(2,128)(2,1)S(1)}) fusion(bf16[2816,4,128]{2,1,0:T(4,128)(2,1)} %reshape.472, s32[]{:T(128)S(6)} %select_n.168, s32[]{:T(128)S(6)} %select_n.166, s32[]{:T(128)S(6)} %select_n.164, ...), kind=kLoop, calls=%fused_computation.194 | loop fusion | bytes 5767184 | tf_op jit(solution)/shard_map/jit(dynamic_index_in_dim)/dynamic_slice | solution.py:193
  403.2 9.6 %shard_map.197 = bf16[512,2816]{1,0:T(8,128)(2,1)S(1)} custom-call(bf16[256,512]{1,0:T(8,128)(2,1)S(1)} %bitcast.412, bf16[256,512]{1,0:T(8,128)(2,1)S(1)} %collective-permute-done.37.refs_1_, bf16[256,512]{1,0:T(8,128)(2,1)S(1)} %collective-permute-done.38.refs_2_, bf16[256,512]{1,0:T(8,128)(2,1)S(1)} %collective-permute-done.39.refs_3_, ...), custom_call_target="tpu_custom_call" | custom-call | flops 2952790016 | bytes 9699328 | tf_op jit(solution)/shard_map/pallas_call | solution.py:167
  412.9 3.5 collective-permute-start.49
  416.5 9.6 %shard_map.196 = bf16[512,2816]{1,0:T(8,128)(2,1)S(1)} custom-call(bf16[256,512]{1,0:T(8,128)(2,1)S(1)} %bitcast.413, bf16[256,512]{1,0:T(8,128)(2,1)S(1)} %collective-permute-done.37.refs_1_, bf16[256,512]{1,0:T(8,128)(2,1)S(1)} %collective-permute-done.38.refs_2_, bf16[256,512]{1,0:T(8,128)(2,1)S(1)} %collective-permute-done.39.refs_3_, ...), custom_call_target="tpu_custom_call" | custom-call | flops 2952790016 | bytes 9699328 | tf_op jit(solution)/shard_map/pallas_call | solution.py:167
  426.7 25.6 %collective-permute-done.21 = bf16[128,1280]{1,0:T(8,128)(2,1)S(1)} collective-permute-done((bf16[128,1280]{1,0:T(8,128)(2,1)S(1)}, bf16[128,1280]{1,0:T(8,128)(2,1)S(1)}, u32[]{:S(2)}, u32[]{:S(2)}) %collective-permute-start.21) | collective-permute-done | bytes 327712 | tf_op jit(solution)/shard_map/ppermute | solution.py:113
  454.7 13.1 %collective-permute-done.43 = bf16[128,2816]{1,0:T(8,128)(2,1)S(1)} collective-permute-done((bf16[128,2816]{1,0:T(8,128)(2,1)S(1)}, bf16[128,2816]{1,0:T(8,128)(2,1)S(1)}, u32[]{:S(2)}, u32[]{:S(2)}) %collective-permute-start.43) | collective-permute-done | bytes 720928 | tf_op jit(solution)/shard_map/ppermute | solution.py:113
  468.0 15.2 %collective-permute-done.50 = bf16[128,2816]{1,0:T(8,128)(2,1)S(1)} collective-permute-done((bf16[128,2816]{1,0:T(8,128)(2,1)S(1)}, bf16[128,2816]{1,0:T(8,128)(2,1)S(1)}, u32[]{:S(2)}, u32[]{:S(2)}) %collective-permute-start.50) | collective-permute-done | bytes 720928 | tf_op jit(solution)/shard_map/ppermute | solution.py:113
  483.5 15.2 %collective-permute-done.59 = bf16[2816,128]{1,0:T(8,128)(2,1)S(1)} collective-permute-done((bf16[2816,128]{1,0:T(8,128)(2,1)S(1)}, bf16[2816,128]{1,0:T(8,128)(2,1)S(1)}, u32[]{:S(2)}, u32[]{:S(2)}) %collective-permute-start.59) | collective-permute-done | bytes 720928 | tf_op jit(solution)/shard_map/ppermute | solution.py:113
  498.9 15.2 %collective-permute-done.44 = bf16[128,2816]{1,0:T(8,128)(2,1)S(1)} collective-permute-done((bf16[128,2816]{1,0:T(8,128)(2,1)S(1)}, bf16[128,2816]{1,0:T(8,128)(2,1)S(1)}, u32[]{:S(2)}, u32[]{:S(2)}) %collective-permute-start.44) | collective-permute-done | bytes 720928 | tf_op jit(solution)/shard_map/ppermute | solution.py:113
  514.4 15.2 %collective-permute-done.51 = bf16[128,2816]{1,0:T(8,128)(2,1)S(1)} collective-permute-done((bf16[128,2816]{1,0:T(8,128)(2,1)S(1)}, bf16[128,2816]{1,0:T(8,128)(2,1)S(1)}, u32[]{:S(2)}, u32[]{:S(2)}) %collective-permute-start.51) | collective-permute-done | bytes 720928 | tf_op jit(solution)/shard_map/ppermute | solution.py:113
  530.8 29.4 %collective-permute-done.45 = bf16[128,2816]{1,0:T(8,128)(2,1)S(1)} collective-permute-done((bf16[128,2816]{1,0:T(8,128)(2,1)S(1)}, bf16[128,2816]{1,0:T(8,128)(2,1)S(1)}, u32[]{:S(2)}, u32[]{:S(2)}) %collective-permute-start.45) | collective-permute-done | bytes 720928 | tf_op jit(solution)/shard_map/ppermute | solution.py:113
  (330 shorter events, 93.1 us)
Async XLA Ops:
  35.2 83.2 %collective-permute-start.26 = (bf16[256,1024]{1,0:T(8,128)(2,1)S(1)}, bf16[256,1024]{1,0:T(8,128)(2,1)S(1)}, u32[]{:S(2)}, u32[]{:S(2)}) collective-permute-start(bf16[256,1024]{1,0:T(8,128)(2,1)S(1)} %copy.81.refs_4_), channel_id=1, source_target_pairs={{0,2},{1,3},{2,0},{3,1},{4,6},{5,7},{6,4},{7,5},{8,10},{9,11},{10,... | collective-permute-start | bytes 1572872 | tf_op jit(solution)/shard_map/ppermute | solution.py:69
  42.3 178.3 %collective-permute-start.25 = (bf16[256,1024]{1,0:T(8,128)(2,1)S(1)}, bf16[256,1024]{1,0:T(8,128)(2,1)S(1)}, u32[]{:S(2)}, u32[]{:S(2)}) collective-permute-start(bf16[256,1024]{1,0:T(8,128)(2,1)S(1)} %copy.81.refs_4_), channel_id=1, source_target_pairs={{0,1},{1,0},{2,3},{3,2},{4,5},{5,4},{6,7},{7,6},{8,9},{9,8},{10,11... | collective-permute-start | bytes 1572872 | tf_op jit(solution)/shard_map/ppermute | solution.py:69
  49.9 26.0 %collective-permute-start = (bf16[256,2048]{1,0:T(8,128)(2,1)}, bf16[256,2048]{1,0:T(8,128)(2,1)}, u32[]{:S(2)}, u32[]{:S(2)}) collective-permute-start(bf16[256,2048]{1,0:T(8,128)(2,1)} %convolution_convert_fusion.1), channel_id=1, source_target_pairs={{0,16},{16,0},{1,17},{17,1},{2,18},{18,2},{3,19},{19,3},{4,20},{20... | collective-permute-start | bytes 3145736 | tf_op jit(solution)/shard_map/ppermute | solution.py:69
  107.0 26.1 %collective-permute-start.2 = (bf16[256,2048]{1,0:T(8,128)(2,1)S(1)}, bf16[256,2048]{1,0:T(8,128)(2,1)S(1)}, u32[]{:S(2)}, u32[]{:S(2)}) collective-permute-start(bf16[256,2048]{1,0:T(8,128)(2,1)S(1)} %fusion.46), channel_id=1, source_target_pairs={{0,16},{16,0},{1,17},{17,1},{2,18},{18,2},{3,19},{19,3},{4,20},{20... | collective-permute-start | bytes 3145736 | tf_op jit(solution)/shard_map/ppermute | solution.py:69
  115.6 38.8 %collective-permute-start.1 = (bf16[256,2048]{1,0:T(8,128)(2,1)S(1)}, bf16[256,2048]{1,0:T(8,128)(2,1)S(1)}, u32[]{:S(2)}, u32[]{:S(2)}) collective-permute-start(bf16[256,2048]{1,0:T(8,128)(2,1)S(1)} %convolution_convert_fusion), channel_id=1, source_target_pairs={{0,16},{16,0},{1,17},{17,1},{2,18},{18,2},{3,19},{19,3},{4,20},{20... | collective-permute-start | bytes 3145736 | tf_op jit(solution)/shard_map/ppermute | solution.py:69
  118.4 35.9 %copy-start.22 = (bf16[256,1,2048]{2,0,1:T(8,128)(2,1)S(1)}, bf16[256,1,2048]{2,0,1:T(8,128)(2,1)}, u32[]{:S(2)}) copy-start(bf16[256,1,2048]{2,0,1:T(8,128)(2,1)} %param.20) | copy-start | bytes 3145732
  118.4 102.4 %collective-permute-start.27 = (bf16[256,1024]{1,0:T(8,128)(2,1)S(1)}, bf16[256,1024]{1,0:T(8,128)(2,1)S(1)}, u32[]{:S(2)}, u32[]{:S(2)}) collective-permute-start(bf16[256,1024]{1,0:T(8,128)(2,1)S(1)} %collective-permute-done.26.refs_6_), channel_id=1, source_target_pairs={{0,1},{1,0},{2,3},{3,2},{4,5},{5,4},{6,7},{7,6},{8,9},{9,8},{10,11... | collective-permute-start | bytes 1572872 | tf_op jit(solution)/shard_map/ppermute | solution.py:69
  179.4 33.9 %collective-permute-start.3 = (bf16[256,256]{1,0:T(8,128)(2,1)}, bf16[256,256]{1,0:T(8,128)(2,1)}, u32[]{:S(2)}, u32[]{:S(2)}) collective-permute-start(bf16[256,256]{1,0:T(8,128)(2,1)} %bitcast.45), channel_id=1, source_target_pairs={{0,1},{1,0},{2,3},{3,2},{4,5},{5,4},{6,7},{7,6},{8,9},{9,8},{10,11... | collective-permute-start | bytes 393224 | tf_op jit(solution)/shard_map/ppermute | solution.py:69
  184.6 28.8 %collective-permute-start.4 = (bf16[256,256]{1,0:T(8,128)(2,1)}, bf16[256,256]{1,0:T(8,128)(2,1)}, u32[]{:S(2)}, u32[]{:S(2)}) collective-permute-start(bf16[256,256]{1,0:T(8,128)(2,1)} %bitcast.46), channel_id=1, source_target_pairs={{0,2},{1,3},{2,0},{3,1},{4,6},{5,7},{6,4},{7,5},{8,10},{9,11},{10,... | collective-permute-start | bytes 393224 | tf_op jit(solution)/shard_map/ppermute | solution.py:69
  197.0 18.5 %collective-permute-start.5 = (bf16[256,256]{1,0:T(8,128)(2,1)}, bf16[256,256]{1,0:T(8,128)(2,1)}, u32[]{:S(2)}, u32[]{:S(2)}) collective-permute-start(bf16[256,256]{1,0:T(8,128)(2,1)} %bitcast.47), channel_id=1, source_target_pairs={{0,3},{1,2},{2,1},{3,0},{4,7},{5,6},{6,5},{7,4},{8,11},{9,10},{10,... | collective-permute-start | bytes 393224 | tf_op jit(solution)/shard_map/ppermute | solution.py:69
  213.3 10.3 %collective-permute-start.22 = (bf16[256,512]{1,0:T(8,128)(2,1)}, bf16[256,512]{1,0:T(8,128)(2,1)S(1)}, u32[]{:S(2)}, u32[]{:S(2)}) collective-permute-start(bf16[256,512]{1,0:T(8,128)(2,1)} %bitcast.386), channel_id=1, source_target_pairs={{0,1},{1,0},{2,3},{3,2},{4,5},{5,4},{6,7},{7,6},{8,9},{9,8},{10,11... | collective-permute-start | bytes 786440 | tf_op jit(solution)/shard_map/ppermute | solution.py:69
  213.5 10.9 %collective-permute-start.23 = (bf16[256,512]{1,0:T(8,128)(2,1)}, bf16[256,512]{1,0:T(8,128)(2,1)S(1)}, u32[]{:S(2)}, u32[]{:S(2)}) collective-permute-start(bf16[256,512]{1,0:T(8,128)(2,1)} %bitcast.385), channel_id=1, source_target_pairs={{0,2},{1,3},{2,0},{3,1},{4,6},{5,7},{6,4},{7,5},{8,10},{9,11},{10,... | collective-permute-start | bytes 786440 | tf_op jit(solution)/shard_map/ppermute | solution.py:69
  215.5 12.6 %collective-permute-start.24 = (bf16[256,512]{1,0:T(8,128)(2,1)}, bf16[256,512]{1,0:T(8,128)(2,1)}, u32[]{:S(2)}, u32[]{:S(2)}) collective-permute-start(bf16[256,512]{1,0:T(8,128)(2,1)} %bitcast.384), channel_id=1, source_target_pairs={{0,3},{1,2},{2,1},{3,0},{4,7},{5,6},{6,5},{7,4},{8,11},{9,10},{10,... | collective-permute-start | bytes 786440 | tf_op jit(solution)/shard_map/ppermute | solution.py:69
  220.6 40.8 %collective-permute-start.52 = (bf16[256,512]{1,0:T(8,128)(2,1)}, bf16[256,512]{1,0:T(8,128)(2,1)}, u32[]{:S(2)}, u32[]{:S(2)}) collective-permute-start(bf16[256,512]{1,0:T(8,128)(2,1)} %bitcast.447), channel_id=1, source_target_pairs={{0,1},{1,0},{2,3},{3,2},{4,5},{5,4},{6,7},{7,6},{8,9},{9,8},{10,11... | collective-permute-start | bytes 786440 | tf_op jit(solution)/shard_map/ppermute | solution.py:69
  221.6 49.9 %collective-permute-start.53 = (bf16[256,512]{1,0:T(8,128)(2,1)}, bf16[256,512]{1,0:T(8,128)(2,1)}, u32[]{:S(2)}, u32[]{:S(2)}) collective-permute-start(bf16[256,512]{1,0:T(8,128)(2,1)} %bitcast.446), channel_id=1, source_target_pairs={{0,2},{1,3},{2,0},{3,1},{4,6},{5,7},{6,4},{7,5},{8,10},{9,11},{10,... | collective-permute-start | bytes 786440 | tf_op jit(solution)/shard_map/ppermute | solution.py:69
  224.3 76.2 %collective-permute-start.56 = (bf16[256,2816]{1,0:T(8,128)(2,1)}, bf16[256,2816]{1,0:T(8,128)(2,1)}, u32[]{:S(2)}, u32[]{:S(2)}) collective-permute-start(bf16[256,2816]{1,0:T(8,128)(2,1)} %copy-done.8), channel_id=1, source_target_pairs={{0,2},{1,3},{2,0},{3,1},{4,6},{5,7},{6,4},{7,5},{8,10},{9,11},{10,... | collective-permute-start | bytes 4325384 | tf_op jit(solution)/shard_map/ppermute | solution.py:69
  237.5 10.4 %collective-permute-start.28 = (bf16[1024,128]{1,0:T(8,128)(2,1)S(1)}, bf16[1024,128]{1,0:T(8,128)(2,1)S(1)}, u32[]{:S(2)}, u32[]{:S(2)}) collective-permute-start(bf16[1024,128]{1,0:T(8,128)(2,1)S(1)} %bitcast.445), channel_id=1, source_target_pairs={{0,4},{4,8},{8,12},{12,0},{1,5},{5,9},{9,13},{13,1},{2,6},{6,10},{... | collective-permute-start | bytes 786440 | tf_op jit(solution)/shard_map/ppermute | solution.py:113
  248.7 9.8 %collective-permute-start.29 = (bf16[1024,128]{1,0:T(8,128)(2,1)}, bf16[1024,128]{1,0:T(8,128)(2,1)}, u32[]{:S(2)}, u32[]{:S(2)}) collective-permute-start(bf16[1024,128]{1,0:T(8,128)(2,1)} %fusion.81), channel_id=1, source_target_pairs={{0,4},{4,8},{8,12},{12,0},{1,5},{5,9},{9,13},{13,1},{2,6},{6,10},{... | collective-permute-start | bytes 786440 | tf_op jit(solution)/shard_map/ppermute | solution.py:113
  250.1 31.7 %collective-permute-start.6 = (bf16[256,2048]{1,0:T(8,128)(2,1)}, bf16[256,2048]{1,0:T(8,128)(2,1)}, u32[]{:S(2)}, u32[]{:S(2)}) collective-permute-start(bf16[256,2048]{1,0:T(8,128)(2,1)} %fusion.47), channel_id=1, source_target_pairs={{0,16},{16,0},{1,17},{17,1},{2,18},{18,2},{3,19},{19,3},{4,20},{20... | collective-permute-start | bytes 3145736 | tf_op jit(solution)/shard_map/ppermute | solution.py:69
  258.5 14.0 %collective-permute-start.54 = (bf16[256,512]{1,0:T(8,128)(2,1)}, bf16[256,512]{1,0:T(8,128)(2,1)S(1)}, u32[]{:S(2)}, u32[]{:S(2)}) collective-permute-start(bf16[256,512]{1,0:T(8,128)(2,1)} %bitcast.453), channel_id=1, source_target_pairs={{0,3},{1,2},{2,1},{3,0},{4,7},{5,6},{6,5},{7,4},{8,11},{9,10},{10,... | collective-permute-start | bytes 786440 | tf_op jit(solution)/shard_map/ppermute | solution.py:69
  261.4 12.5 %collective-permute-start.30 = (bf16[1024,128]{1,0:T(8,128)(2,1)}, bf16[1024,128]{1,0:T(8,128)(2,1)}, u32[]{:S(2)}, u32[]{:S(2)}) collective-permute-start(bf16[1024,128]{1,0:T(8,128)(2,1)} %fusion.80), channel_id=1, source_target_pairs={{0,4},{4,8},{8,12},{12,0},{1,5},{5,9},{9,13},{13,1},{2,6},{6,10},{... | collective-permute-start | bytes 786440 | tf_op jit(solution)/shard_map/ppermute | solution.py:113
  271.5 6.3 %collective-permute-start.13 = (bf16[256,512]{1,0:T(8,128)(2,1)}, bf16[256,512]{1,0:T(8,128)(2,1)S(1)}, u32[]{:S(2)}, u32[]{:S(2)}) collective-permute-start(bf16[256,512]{1,0:T(8,128)(2,1)} %bitcast.451), channel_id=1, source_target_pairs={{0,1},{1,0},{2,3},{3,2},{4,5},{5,4},{6,7},{7,6},{8,9},{9,8},{10,11... | collective-permute-start | bytes 786440 | tf_op jit(solution)/shard_map/ppermute | solution.py:69
  272.5 9.4 %collective-permute-start.14 = (bf16[256,512]{1,0:T(8,128)(2,1)}, bf16[256,512]{1,0:T(8,128)(2,1)S(1)}, u32[]{:S(2)}, u32[]{:S(2)}) collective-permute-start(bf16[256,512]{1,0:T(8,128)(2,1)} %bitcast.450), channel_id=1, source_target_pairs={{0,2},{1,3},{2,0},{3,1},{4,6},{5,7},{6,4},{7,5},{8,10},{9,11},{10,... | collective-permute-start | bytes 786440 | tf_op jit(solution)/shard_map/ppermute | solution.py:69
  273.9 28.3 %collective-permute-start.17 = (bf16[256,1280]{1,0:T(8,128)(2,1)S(1)}, bf16[256,1280]{1,0:T(8,128)(2,1)S(1)}, u32[]{:S(2)}, u32[]{:S(2)}) collective-permute-start(bf16[256,1280]{1,0:T(8,128)(2,1)S(1)} %pad_maximum_fusion.refs_4_), channel_id=1, source_target_pairs={{0,2},{1,3},{2,0},{3,1},{4,6},{5,7},{6,4},{7,5},{8,10},{9,11},{10,... | collective-permute-start | bytes 1966088 | tf_op jit(solution)/shard_map/ppermute | solution.py:69
  275.7 59.8 %copy-start.19 = (f32[256,2048]{1,0:T(8,128)S(1)}, f32[256,2048]{1,0:T(8,128)}, u32[]{:S(2)}) copy-start(f32[256,2048]{1,0:T(8,128)} %get-tuple-element.413) | copy-start | bytes 6291460
  277.8 22.0 %collective-permute-start.15 = (bf16[256,512]{1,0:T(8,128)(2,1)S(1)}, bf16[256,512]{1,0:T(8,128)(2,1)S(1)}, u32[]{:S(2)}, u32[]{:S(2)}) collective-permute-start(bf16[256,512]{1,0:T(8,128)(2,1)S(1)} %bitcast.449), channel_id=1, source_target_pairs={{0,3},{1,2},{2,1},{3,0},{4,7},{5,6},{6,5},{7,4},{8,11},{9,10},{10,... | collective-permute-start | bytes 786440 | tf_op jit(solution)/shard_map/ppermute | solution.py:69
  281.8 58.3 %collective-permute-start.55 = (bf16[256,2816]{1,0:T(8,128)(2,1)}, bf16[256,2816]{1,0:T(8,128)(2,1)S(1)}, u32[]{:S(2)}, u32[]{:S(2)}) collective-permute-start(bf16[256,2816]{1,0:T(8,128)(2,1)} %copy-done.8), channel_id=1, source_target_pairs={{0,1},{1,0},{2,3},{3,2},{4,5},{5,4},{6,7},{7,6},{8,9},{9,8},{10,11... | collective-permute-start | bytes 4325384 | tf_op jit(solution)/shard_map/ppermute | solution.py:69
  281.9 18.3 %collective-permute-start.37 = (bf16[256,512]{1,0:T(8,128)(2,1)S(1)}, bf16[256,512]{1,0:T(8,128)(2,1)S(1)}, u32[]{:S(2)}, u32[]{:S(2)}) collective-permute-start(bf16[256,512]{1,0:T(8,128)(2,1)S(1)} %bitcast.452), channel_id=1, source_target_pairs={{0,1},{1,0},{2,3},{3,2},{4,5},{5,4},{6,7},{7,6},{8,9},{9,8},{10,11... | collective-permute-start | bytes 786440 | tf_op jit(solution)/shard_map/ppermute | solution.py:69
  299.8 40.7 %collective-permute-start.47 = (bf16[256,2816]{1,0:T(8,128)(2,1)}, bf16[256,2816]{1,0:T(8,128)(2,1)}, u32[]{:S(2)}, u32[]{:S(2)}) collective-permute-start(bf16[256,2816]{1,0:T(8,128)(2,1)} %get-tuple-element.422.refs_4_), channel_id=1, source_target_pairs={{0,2},{1,3},{2,0},{3,1},{4,6},{5,7},{6,4},{7,5},{8,10},{9,11},{10,... | collective-permute-start | bytes 4325384 | tf_op jit(solution)/shard_map/ppermute | solution.py:69
  300.2 2.0 collective-permute-start.31
  300.5 33.8 %collective-permute-start.32 = (f32[4,128]{1,0:T(4,128)S(1)}, f32[4,128]{1,0:T(4,128)S(1)}, u32[]{:S(2)}, u32[]{:S(2)}) collective-permute-start(f32[4,128]{1,0:T(4,128)S(1)} %bitcast.464), channel_id=1, source_target_pairs={{0,2},{1,3},{2,0},{3,1},{4,6},{5,7},{6,4},{7,5},{8,10},{9,11},{10,... | collective-permute-start | bytes 6152 | tf_op jit(solution)/shard_map/ppermute | solution.py:69
  302.2 32.4 %collective-permute-start.33 = (f32[4,128]{1,0:T(4,128)S(1)}, f32[4,128]{1,0:T(4,128)S(1)}, u32[]{:S(2)}, u32[]{:S(2)}) collective-permute-start(f32[4,128]{1,0:T(4,128)S(1)} %bitcast.463), channel_id=1, source_target_pairs={{0,3},{1,2},{2,1},{3,0},{4,7},{5,6},{6,5},{7,4},{8,11},{9,10},{10,... | collective-permute-start | bytes 6152 | tf_op jit(solution)/shard_map/ppermute | solution.py:69
  302.2 36.5 %collective-permute-start.7 = (f32[4,128]{1,0:T(4,128)S(1)}, f32[4,128]{1,0:T(4,128)S(1)}, u32[]{:S(2)}, u32[]{:S(2)}) collective-permute-start(f32[4,128]{1,0:T(4,128)S(1)} %bitcast.462), channel_id=1, source_target_pairs={{0,1},{1,0},{2,3},{3,2},{4,5},{5,4},{6,7},{7,6},{8,9},{9,8},{10,11... | collective-permute-start | bytes 6152 | tf_op jit(solution)/shard_map/ppermute | solution.py:69
  334.3 5.3 collective-permute-start.8
  334.6 5.2 collective-permute-start.9
  338.8 34.8 %collective-permute-start.41 = (bf16[256,2816]{1,0:T(8,128)(2,1)}, bf16[256,2816]{1,0:T(8,128)(2,1)}, u32[]{:S(2)}, u32[]{:S(2)}) collective-permute-start(bf16[256,2816]{1,0:T(8,128)(2,1)} %get-tuple-element.423.refs_4_), channel_id=1, source_target_pairs={{0,2},{1,3},{2,0},{3,1},{4,6},{5,7},{6,4},{7,5},{8,10},{9,11},{10,... | collective-permute-start | bytes 4325384 | tf_op jit(solution)/shard_map/ppermute | solution.py:69
  339.6 2.1 collective-permute-start.16
  339.8 5.0 collective-permute-start.18
  340.2 34.0 %collective-permute-start.57 = (bf16[256,2816]{1,0:T(8,128)(2,1)}, bf16[256,2816]{1,0:T(8,128)(2,1)S(1)}, u32[]{:S(2)}, u32[]{:S(2)}) collective-permute-start(bf16[256,2816]{1,0:T(8,128)(2,1)} %collective-permute-done.56.refs_6_), channel_id=1, source_target_pairs={{0,1},{1,0},{2,3},{3,2},{4,5},{5,4},{6,7},{7,6},{8,9},{9,8},{10,11... | collective-permute-start | bytes 4325384 | tf_op jit(solution)/shard_map/ppermute | solution.py:69
  340.4 9.5 %collective-permute-start.34 = (f32[128]{0:T(128)S(1)}, f32[128]{0:T(128)S(1)}, u32[]{:S(2)}, u32[]{:S(2)}) collective-permute-start(f32[128]{0:T(128)S(1)} %get-tuple-element.460), channel_id=1, source_target_pairs={{0,4},{4,0},{8,12},{12,8},{1,5},{5,1},{9,13},{13,9},{2,6},{6,2},{1... | collective-permute-start | bytes 1544 | tf_op jit(solution)/shard_map/ppermute | solution.py:69
  341.7 8.3 %collective-permute-start.35 = (f32[128]{0:T(128)S(1)}, f32[128]{0:T(128)S(1)}, u32[]{:S(2)}, u32[]{:S(2)}) collective-permute-start(f32[128]{0:T(128)S(1)} %get-tuple-element.462), channel_id=1, source_target_pairs={{0,8},{4,12},{8,0},{12,4},{1,9},{5,13},{9,1},{13,5},{2,10},{6,14},... | collective-permute-start | bytes 1544 | tf_op jit(solution)/shard_map/ppermute | solution.py:69
  344.8 7.2 %collective-permute-start.36 = (f32[128]{0:T(128)S(1)}, f32[128]{0:T(128)S(1)}, u32[]{:S(2)}, u32[]{:S(2)}) collective-permute-start(f32[128]{0:T(128)S(1)} %get-tuple-element.461), channel_id=1, source_target_pairs={{0,12},{4,8},{8,4},{12,0},{1,13},{5,9},{9,5},{13,1},{2,14},{6,10},... | collective-permute-start | bytes 1544 | tf_op jit(solution)/shard_map/ppermute | solution.py:69
  347.2 27.4 %copy-start.9 = (bf16[256,2816]{1,0:T(8,128)(2,1)S(1)}, bf16[256,2816]{1,0:T(8,128)(2,1)}, u32[]{:S(2)}) copy-start(bf16[256,2816]{1,0:T(8,128)(2,1)} %copy-done.8) | copy-start | bytes 4325380
  349.9 4.5 collective-permute-start.10
  350.0 4.5 collective-permute-start.11
  352.0 5.3 collective-permute-start.12
  354.4 47.7 %collective-permute-start.46 = (bf16[256,2816]{1,0:T(8,128)(2,1)}, bf16[256,2816]{1,0:T(8,128)(2,1)}, u32[]{:S(2)}, u32[]{:S(2)}) collective-permute-start(bf16[256,2816]{1,0:T(8,128)(2,1)} %get-tuple-element.422.refs_4_), channel_id=1, source_target_pairs={{0,1},{1,0},{2,3},{3,2},{4,5},{5,4},{6,7},{7,6},{8,9},{9,8},{10,11... | collective-permute-start | bytes 4325384 | tf_op jit(solution)/shard_map/ppermute | solution.py:69
  354.5 48.7 %collective-permute-start.48 = (bf16[256,2816]{1,0:T(8,128)(2,1)}, bf16[256,2816]{1,0:T(8,128)(2,1)}, u32[]{:S(2)}, u32[]{:S(2)}) collective-permute-start(bf16[256,2816]{1,0:T(8,128)(2,1)} %collective-permute-done.47.refs_6_), channel_id=1, source_target_pairs={{0,1},{1,0},{2,3},{3,2},{4,5},{5,4},{6,7},{7,6},{8,9},{9,8},{10,11... | collective-permute-start | bytes 4325384 | tf_op jit(solution)/shard_map/ppermute | solution.py:69
  357.4 16.3 %collective-permute-start.19 = (bf16[128,1280]{1,0:T(8,128)(2,1)S(1)}, bf16[128,1280]{1,0:T(8,128)(2,1)S(1)}, u32[]{:S(2)}, u32[]{:S(2)}) collective-permute-start(bf16[128,1280]{1,0:T(8,128)(2,1)S(1)} %dynamic-slice_bitcast_fusion.4), channel_id=1, source_target_pairs={{0,4},{4,8},{8,12},{12,0},{1,5},{5,9},{9,13},{13,1},{2,6},{6,10},{... | collective-permute-start | bytes 983048 | tf_op jit(solution)/shard_map/ppermute | solution.py:113
  373.5 42.9 %collective-permute-start.40 = (bf16[256,2816]{1,0:T(8,128)(2,1)}, bf16[256,2816]{1,0:T(8,128)(2,1)}, u32[]{:S(2)}, u32[]{:S(2)}) collective-permute-start(bf16[256,2816]{1,0:T(8,128)(2,1)} %get-tuple-element.423.refs_4_), channel_id=1, source_target_pairs={{0,1},{1,0},{2,3},{3,2},{4,5},{5,4},{6,7},{7,6},{8,9},{9,8},{10,11... | collective-permute-start | bytes 4325384 | tf_op jit(solution)/shard_map/ppermute | solution.py:69
  373.6 42.8 %collective-permute-start.42 = (bf16[256,2816]{1,0:T(8,128)(2,1)}, bf16[256,2816]{1,0:T(8,128)(2,1)}, u32[]{:S(2)}, u32[]{:S(2)}) collective-permute-start(bf16[256,2816]{1,0:T(8,128)(2,1)} %collective-permute-done.41.refs_6_), channel_id=1, source_target_pairs={{0,1},{1,0},{2,3},{3,2},{4,5},{5,4},{6,7},{7,6},{8,9},{9,8},{10,11... | collective-permute-start | bytes 4325384 | tf_op jit(solution)/shard_map/ppermute | solution.py:69
  374.1 16.6 %collective-permute-start.38 = (bf16[256,512]{1,0:T(8,128)(2,1)}, bf16[256,512]{1,0:T(8,128)(2,1)S(1)}, u32[]{:S(2)}, u32[]{:S(2)}) collective-permute-start(bf16[256,512]{1,0:T(8,128)(2,1)} %bitcast.381), channel_id=1, source_target_pairs={{0,2},{1,3},{2,0},{3,1},{4,6},{5,7},{6,4},{7,5},{8,10},{9,11},{10,... | collective-permute-start | bytes 786440 | tf_op jit(solution)/shard_map/ppermute | solution.py:69
  390.8 11.2 %collective-permute-start.39 = (bf16[256,512]{1,0:T(8,128)(2,1)S(1)}, bf16[256,512]{1,0:T(8,128)(2,1)S(1)}, u32[]{:S(2)}, u32[]{:S(2)}) collective-permute-start(bf16[256,512]{1,0:T(8,128)(2,1)S(1)} %bitcast.448), channel_id=1, source_target_pairs={{0,3},{1,2},{2,1},{3,0},{4,7},{5,6},{6,5},{7,4},{8,11},{9,10},{10,... | collective-permute-start | bytes 786440 | tf_op jit(solution)/shard_map/ppermute | solution.py:69
  402.0 24.1 %collective-permute-start.20 = (bf16[128,1280]{1,0:T(8,128)(2,1)S(1)}, bf16[128,1280]{1,0:T(8,128)(2,1)S(1)}, u32[]{:S(2)}, u32[]{:S(2)}) collective-permute-start(bf16[128,1280]{1,0:T(8,128)(2,1)S(1)} %fusion.79), channel_id=1, source_target_pairs={{0,4},{4,8},{8,12},{12,0},{1,5},{5,9},{9,13},{13,1},{2,6},{6,10},{... | collective-permute-start | bytes 983048 | tf_op jit(solution)/shard_map/ppermute | solution.py:113
  402.1 52.1 %collective-permute-start.58 = (bf16[2816,128]{1,0:T(8,128)(2,1)S(1)}, bf16[2816,128]{1,0:T(8,128)(2,1)S(1)}, u32[]{:S(2)}, u32[]{:S(2)}) collective-permute-start(bf16[2816,128]{1,0:T(8,128)(2,1)S(1)} %bitcast.438), channel_id=1, source_target_pairs={{0,4},{4,8},{8,12},{12,0},{1,5},{5,9},{9,13},{13,1},{2,6},{6,10},{... | collective-permute-start | bytes 2162696 | tf_op jit(solution)/shard_map/ppermute | solution.py:113
  412.9 41.0 %collective-permute-start.49 = (bf16[128,2816]{1,0:T(8,128)(2,1)S(1)}, bf16[128,2816]{1,0:T(8,128)(2,1)S(1)}, u32[]{:S(2)}, u32[]{:S(2)}) collective-permute-start(bf16[128,2816]{1,0:T(8,128)(2,1)S(1)} %dynamic-slice_bitcast_fusion.2), channel_id=1, source_target_pairs={{0,4},{4,8},{8,12},{12,0},{1,5},{5,9},{9,13},{13,1},{2,6},{6,10},{... | collective-permute-start | bytes 2162696 | tf_op jit(solution)/shard_map/ppermute | solution.py:113
  426.2 26.2 %collective-permute-start.21 = (bf16[128,1280]{1,0:T(8,128)(2,1)S(1)}, bf16[128,1280]{1,0:T(8,128)(2,1)S(1)}, u32[]{:S(2)}, u32[]{:S(2)}) collective-permute-start(bf16[128,1280]{1,0:T(8,128)(2,1)S(1)} %fusion.78), channel_id=1, source_target_pairs={{0,4},{4,8},{8,12},{12,0},{1,5},{5,9},{9,13},{13,1},{2,6},{6,10},{... | collective-permute-start | bytes 983048 | tf_op jit(solution)/shard_map/ppermute | solution.py:113
  426.6 41.2 %collective-permute-start.43 = (bf16[128,2816]{1,0:T(8,128)(2,1)S(1)}, bf16[128,2816]{1,0:T(8,128)(2,1)S(1)}, u32[]{:S(2)}, u32[]{:S(2)}) collective-permute-start(bf16[128,2816]{1,0:T(8,128)(2,1)S(1)} %dynamic-slice_bitcast_fusion.3), channel_id=1, source_target_pairs={{0,4},{4,8},{8,12},{12,0},{1,5},{5,9},{9,13},{13,1},{2,6},{6,10},{... | collective-permute-start | bytes 2162696 | tf_op jit(solution)/shard_map/ppermute | solution.py:113
  454.1 29.1 %collective-permute-start.50 = (bf16[128,2816]{1,0:T(8,128)(2,1)S(1)}, bf16[128,2816]{1,0:T(8,128)(2,1)S(1)}, u32[]{:S(2)}, u32[]{:S(2)}) collective-permute-start(bf16[128,2816]{1,0:T(8,128)(2,1)S(1)} %fusion.67), channel_id=1, source_target_pairs={{0,4},{4,8},{8,12},{12,0},{1,5},{5,9},{9,13},{13,1},{2,6},{6,10},{... | collective-permute-start | bytes 2162696 | tf_op jit(solution)/shard_map/ppermute | solution.py:113
  454.3 44.4 %collective-permute-start.59 = (bf16[2816,128]{1,0:T(8,128)(2,1)S(1)}, bf16[2816,128]{1,0:T(8,128)(2,1)S(1)}, u32[]{:S(2)}, u32[]{:S(2)}) collective-permute-start(bf16[2816,128]{1,0:T(8,128)(2,1)S(1)} %fusion.65), channel_id=1, source_target_pairs={{0,4},{4,8},{8,12},{12,0},{1,5},{5,9},{9,13},{13,1},{2,6},{6,10},{... | collective-permute-start | bytes 2162696 | tf_op jit(solution)/shard_map/ppermute | solution.py:113
  468.0 46.2 %collective-permute-start.44 = (bf16[128,2816]{1,0:T(8,128)(2,1)S(1)}, bf16[128,2816]{1,0:T(8,128)(2,1)S(1)}, u32[]{:S(2)}, u32[]{:S(2)}) collective-permute-start(bf16[128,2816]{1,0:T(8,128)(2,1)S(1)} %fusion.69), channel_id=1, source_target_pairs={{0,4},{4,8},{8,12},{12,0},{1,5},{5,9},{9,13},{13,1},{2,6},{6,10},{... | collective-permute-start | bytes 2162696 | tf_op jit(solution)/shard_map/ppermute | solution.py:113
  483.4 46.2 %collective-permute-start.51 = (bf16[128,2816]{1,0:T(8,128)(2,1)S(1)}, bf16[128,2816]{1,0:T(8,128)(2,1)S(1)}, u32[]{:S(2)}, u32[]{:S(2)}) collective-permute-start(bf16[128,2816]{1,0:T(8,128)(2,1)S(1)} %fusion.66), channel_id=1, source_target_pairs={{0,4},{4,8},{8,12},{12,0},{1,5},{5,9},{9,13},{13,1},{2,6},{6,10},{... | collective-permute-start | bytes 2162696 | tf_op jit(solution)/shard_map/ppermute | solution.py:113
  498.8 62.6 %collective-permute-start.60 = (bf16[2816,128]{1,0:T(8,128)(2,1)S(1)}, bf16[2816,128]{1,0:T(8,128)(2,1)S(1)}, u32[]{:S(2)}, u32[]{:S(2)}) collective-permute-start(bf16[2816,128]{1,0:T(8,128)(2,1)S(1)} %fusion.64), channel_id=1, source_target_pairs={{0,4},{4,8},{8,12},{12,0},{1,5},{5,9},{9,13},{13,1},{2,6},{6,10},{... | collective-permute-start | bytes 2162696 | tf_op jit(solution)/shard_map/ppermute | solution.py:113
  514.3 45.9 %collective-permute-start.45 = (bf16[128,2816]{1,0:T(8,128)(2,1)S(1)}, bf16[128,2816]{1,0:T(8,128)(2,1)S(1)}, u32[]{:S(2)}, u32[]{:S(2)}) collective-permute-start(bf16[128,2816]{1,0:T(8,128)(2,1)S(1)} %fusion.68), channel_id=1, source_target_pairs={{0,4},{4,8},{8,12},{12,0},{1,5},{5,9},{9,13},{13,1},{2,6},{6,10},{... | collective-permute-start | bytes 2162696 | tf_op jit(solution)/shard_map/ppermute | solution.py:113
  (42 other events, 186.4 us)

commit v2 on v1

v2 whole, which is shorter than its diff:
```python
import math
from functools import partial

import jax
import jax.numpy as jnp
from jax import lax
from jax.experimental import pallas as pl
from jax.experimental.pallas import tpu as pltpu
from jax.sharding import PartitionSpec as P

CONTEXT = ("row", "core")
HEAD_WIDTH = 64
HALF = HEAD_WIDTH // 2
LANES = 128
EPS = 1e-05
ROPE_BASE = 10000.0
NEG_FILL = -1e30
F32 = jnp.float32
BF16 = jnp.bfloat16
MIB = 1024 * 1024
WEIGHT = 3.0


def dot_nn(a, b):
    return lax.dot_general(a, b, (((1,), (0,)), ((), ())), preferred_element_type=F32)


def dot_nt(a, b):
    return lax.dot_general(a, b, (((1,), (1,)), ((), ())), preferred_element_type=F32)


def dot_tn(a, b):
    return lax.dot_general(a, b, (((0,), (0,)), ((), ())), preferred_element_type=F32)


def whole(shape):
    return pl.BlockSpec(shape, lambda *index: (0,) * len(shape))


def shaped(shape, dtype):
    return jax.ShapeDtypeStruct(shape, dtype)


class Chain:
    def __init__(self):
        self.last = []

    def __call__(
        self,
        body,
        out_shape,
        *operands,
        in_specs,
        out_specs,
        grid=(1,),
        scratch=(),
        scalars=0,
        after=(),
        carry=(),
        vmem=40,
        us=1.0,
    ):
        waits = list(carry) + self.last + list(after)
        inputs = scalars + len(in_specs)
        out_shape = list(out_shape) if isinstance(out_shape, (list, tuple)) else [out_shape]
        out_specs = list(out_specs) if isinstance(out_specs, (list, tuple)) else [out_specs]
        outputs, unread = len(out_shape), pl.BlockSpec(memory_space=pl.ANY)

        def stripped(*refs):
            rest = refs[inputs + len(waits) :]
            body(*refs[:inputs], *rest[:outputs], *rest[outputs + len(carry) :])

        outs = pl.pallas_call(
            stripped,
            out_shape=out_shape + [shaped(c.shape, c.dtype) for c in carry],
            grid_spec=pltpu.PrefetchScalarGridSpec(
                num_scalar_prefetch=scalars,
                grid=grid,
                in_specs=list(in_specs) + [unread] * len(waits),
                out_specs=out_specs + [unread] * len(carry),
                scratch_shapes=list(scratch),
            ),
            input_output_aliases={inputs + i: outputs + i for i in range(len(carry))},
            compiler_params=pltpu.CompilerParams(vmem_limit_bytes=vmem * MIB),
            cost_estimate=pl.CostEstimate(
                flops=int(us * WEIGHT * 1.1e9), bytes_accessed=1000, transcendentals=0
            ),
        )(*operands, *waits)
        self.last = [outs[0]]
        return outs[0] if len(outs) == 1 else outs


def swap(value, axis, flip):
    count = lax.axis_size(axis)
    return lax.ppermute(value, axis, [(i, i ^ flip) for i in range(count)])


def exchange_context(pieces):
    return [p if k == 0 else swap(p, CONTEXT, k) for k, p in enumerate(pieces)]


def exchange_chips(pieces):
    return [p if m == 0 else swap(p, CONTEXT, 2 * m) for m, p in enumerate(pieces)]


def gather_chips(value):
    return exchange_chips([value] * (lax.axis_size(CONTEXT) // 2))


def scatter_gains(value):
    dp_count, ctx_count = lax.axis_size("dp"), lax.axis_size(CONTEXT)
    dp_here, ctx_here = lax.axis_index("dp"), lax.axis_index(CONTEXT)
    blocks = value.reshape(value.shape[0], dp_count, ctx_count, -1)
    total = lax.dynamic_index_in_dim(blocks, ctx_here, 2, keepdims=False)
    for k in range(1, ctx_count):
        total = total + swap(
            lax.dynamic_index_in_dim(blocks, ctx_here ^ k, 2, keepdims=False), CONTEXT, k
        )
    result = lax.dynamic_index_in_dim(total, dp_here, 1, keepdims=False)
    for k in range(1, dp_count):
        result = result + swap(
            lax.dynamic_index_in_dim(total, dp_here ^ k, 1, keepdims=False), "dp", k
        )
    return result


def share_shapes(tokens, width):
    dp_count, ctx_count = lax.axis_size("dp"), lax.axis_size(CONTEXT)
    if (width // (dp_count * ctx_count)) % LANES:
        return []
    return [shaped((tokens, 2 * width // ctx_count), BF16)] * (ctx_count // 2)


def write_shares(here, source_ref, share_refs, by_core=False):
    width = source_ref.shape[1]
    dp_count, ctx_count = lax.axis_size("dp"), lax.axis_size(CONTEXT)
    piece = width // (dp_count * ctx_count)
    for m, share_ref in enumerate(share_refs):
        for side in range(2):
            for d in range(dp_count):
                owner = ((here ^ (2 * m)) // 2) * 2 + side if by_core else here ^ (2 * m + side)
                start = pl.multiple_of((d * ctx_count + owner) * piece, LANES)
                to = (side * dp_count + d) * piece
                share_ref[:, to : to + piece] = source_ref[:, pl.ds(start, piece)]


def shares_of(value, written, by_core=False):
    if written:
        return list(written)
    dp_count, ctx_count = lax.axis_size("dp"), lax.axis_size(CONTEXT)
    here = lax.axis_index(CONTEXT)
    tokens, width = value.shape
    blocks = value.reshape(tokens, dp_count, ctx_count, width // (dp_count * ctx_count))
    cuts = [
        lax.dynamic_index_in_dim(
            blocks, (here ^ k) // 2 * 2 + k % 2 if by_core else here ^ k, 2, keepdims=False
        ).reshape(tokens, -1)
        for k in range(ctx_count)
    ]
    return [
        jnp.concatenate(cuts[2 * m : 2 * m + 2], axis=1) for m in range(ctx_count // 2)
    ]


def pick_kernel(here_ref, value_ref, *share_refs):
    write_shares(here_ref[0], value_ref, share_refs)


def pick_shares(chain, here, value, after=()):
    shapes = share_shapes(*value.shape)
    if not shapes:
        return shares_of(value, ())
    return chain(
        pick_kernel,
        shapes,
        here,
        value,
        in_specs=[whole(value.shape)],
        out_specs=[whole(s.shape) for s in shapes],
        scalars=1,
        after=after,
    )


def pick_block(size, largest):
    for block in range(largest, 0, -LANES):
        if size % block == 0:
            return block
    return size


def rows_kernel(count, *refs):
    narrow_refs, wide_refs = refs[:count], refs[count : 2 * count]
    own_ref, other_ref, turned_ref = refs[2 * count :]

    @pl.when(pl.program_id(0) == 0)
    def _():
        for k in range(count):
            turned_ref[k] = narrow_refs[k][...].T

    total = dot_nn(turned_ref[0], wide_refs[0][...])
    for k in range(1, count):
        total += dot_nn(turned_ref[k], wide_refs[k][...])
    half = total.shape[0] // 2
    own_ref[...] = total[:half].astype(BF16)
    other_ref[...] = total[half:].astype(BF16)


def row_products(chain, narrow, wide, after=()):
    dp_count = lax.axis_size("dp")
    count = len(narrow)
    tokens, rows = narrow[0].shape
    columns = wide[0].shape[1]
    block = pick_block(columns, 512)
    out = shaped((rows // 2, columns), BF16)
    own, other = chain(
        partial(rows_kernel, count),
        [out] * 2,
        *narrow,
        *wide,
        grid=(columns // block,),
        in_specs=[whole((tokens, rows))] * count
        + [pl.BlockSpec((tokens, block), lambda j: (0, j))] * count,
        us=5.0,
        out_specs=[pl.BlockSpec((rows // 2, block), lambda j: (0, j))] * 2,
        scratch=[pltpu.VMEM((count, rows, tokens), BF16)],
        after=after,
    )
    shape = (dp_count, rows // (2 * dp_count), columns)
    return own.reshape(shape), swap(other.reshape(shape), CONTEXT, 1)


def scattered_kernel(count, *refs):
    narrow_refs, wide_refs = refs[:count], refs[count : 2 * count]
    out_ref, turned_ref = refs[2 * count :]

    @pl.when(pl.program_id(0) == 0)
    def _():
        for k in range(count):
            turned_ref[k] = narrow_refs[k][...].T

    total = dot_nn(turned_ref[0], wide_refs[0][...])
    for k in range(1, count):
        total += dot_nn(turned_ref[k], wide_refs[k][...])
    total = total.astype(BF16)
    dp_count, cores, piece = out_ref.shape[:3]
    for side in range(cores):
        for d in range(dp_count):
            start = (side * dp_count + d) * piece
            out_ref[d, side] = total[start : start + piece]


def row_scatter(chain, narrow, wide, after=()):
    dp_count = lax.axis_size("dp")
    count = len(narrow)
    tokens, rows = narrow[0].shape
    columns = wide[0].shape[1]
    block = pick_block(columns, 512)
    piece = rows // (2 * dp_count)
    product = chain(
        partial(scattered_kernel, count),
        shaped((dp_count, 2, piece, columns), BF16),
        *narrow,
        *wide,
        grid=(columns // block,),
        in_specs=[whole((tokens, rows))] * count
        + [pl.BlockSpec((tokens, block), lambda j: (0, j))] * count,
        us=5.0,
        out_specs=pl.BlockSpec((dp_count, 2, piece, block), lambda j: (0, 0, 0, j)),
        scratch=[pltpu.VMEM((count, rows, tokens), BF16)],
        after=after,
    )
    return lax.psum_scatter(
        product.reshape(rows, columns), ("dp", "core"), scatter_dimension=0, tiled=True
    )


def dealt_kernel(block, *refs):
    parts, outs = refs[:-2], refs[-2:]
    at = 0
    for ref in parts:
        for j in range(0, ref.shape[1], 2 * block):
            for side, out_ref in enumerate(outs):
                start = j + side * block
                out_ref[:, at : at + block] = ref[:, start : start + block].astype(F32)
            at += block


def columns_kernel(count, *refs):
    narrow_refs, wide_refs = refs[:count], refs[count : 2 * count]
    own_ref, other_ref = refs[2 * count :]
    total = dot_tn(wide_refs[0][...], narrow_refs[0][...])
    for k in range(1, count):
        total += dot_tn(wide_refs[k][...], narrow_refs[k][...])
    total = total.astype(BF16)
    piece = own_ref.shape[2]
    for side, out_ref in enumerate((own_ref, other_ref)):
        for d in range(out_ref.shape[0]):
            start = (side * out_ref.shape[0] + d) * piece
            out_ref[d] = total[:, start : start + piece]


def column_products(chain, wide, narrow, after=()):
    dp_count = lax.axis_size("dp")
    count = len(narrow)
    tokens, columns = narrow[0].shape
    rows = wide[0].shape[1]
    block = pick_block(rows, 512)
    piece = columns // (2 * dp_count)
    own, other = chain(
        partial(columns_kernel, count),
        [shaped((dp_count, rows, piece), BF16)] * 2,
        *narrow,
        *wide,
        grid=(rows // block,),
        in_specs=[whole((tokens, columns))] * count
        + [pl.BlockSpec((tokens, block), lambda j: (0, j))] * count,
        us=3.0,
        out_specs=[pl.BlockSpec((dp_count, block, piece), lambda j: (0, j, 0))] * 2,
        after=after,
    )
    return own, swap(other, CONTEXT, 1)


def ring_kernel(inputs, block, index_ref, *refs):
    total = refs[0][0].astype(F32)
    for ref in refs[1:inputs]:
        total += ref[0].astype(F32)
    outs = refs[inputs:]
    if len(outs) == 1:
        outs[0][0] = total.astype(outs[0].dtype)
        return
    for j in range(total.shape[1] // block):
        at = j // len(outs) * block
        outs[j % len(outs)][0, :, at : at + block] = total[:, j * block : (j + 1) * block]


class Ring:
    def __init__(self, chain, own, other, block=0):
        self.chain, self.products, self.block = chain, (own, other), block
        self.count = lax.axis_size("dp")
        self.done, self.arrived, self.result = 0, None, None

    def step(self):
        self.done += 1
        last = self.done == self.count
        index = (lax.axis_index("dp") - self.done) % self.count
        shape = (1,) + self.products[0].shape[1:]
        chunk = pl.BlockSpec(shape, lambda i, index_ref: (index_ref[0], 0, 0))
        arrived = [] if self.arrived is None else [self.arrived]
        outs = [shaped(shape, F32 if last else BF16)]
        if last and self.block:
            outs = [shaped(shape[:2] + (shape[2] // 2,), F32)] * 2
        total = self.chain(
            partial(ring_kernel, 2 + len(arrived), self.block),
            outs,
            index.astype(jnp.int32).reshape(1),
            *self.products,
            *arrived,
            in_specs=[chunk] * 2 + [whole(shape)] * len(arrived),
            out_specs=[whole(o.shape) for o in outs],
            scalars=1,
        )
        if last:
            self.result = [t[0] for t in (total if self.block else [total])]
        else:
            ring = [(i, (i + 1) % self.count) for i in range(self.count)]
            self.arrived = lax.ppermute(total, "dp", ring)

    @property
    def open(self):
        return self.result is None


def turns(rings):
    for ring in rings:
        if ring.open:
            ring.step()


def finish(rings):
    while any(ring.open for ring in rings):
        turns(rings)


def rotary_tables(tokens):
    frequencies = jnp.exp(
        jnp.arange(HALF, dtype=F32) * (-2.0 * math.log(ROPE_BASE) / HEAD_WIDTH)
    )
    positions = lax.axis_index(CONTEXT) * tokens + jnp.arange(tokens, dtype=jnp.int32)
    angles = positions.astype(F32)[:, None] * frequencies[None, :]
    cosine, sine = jnp.cos(angles), jnp.sin(angles)
    copies = LANES // HEAD_WIDTH
    return (
        jnp.concatenate([cosine, cosine] * copies, axis=1),
        jnp.concatenate([-sine, sine] * copies, axis=1),
    )


def rotate(values, cosine, sine):
    turned = []
    lane = lax.broadcasted_iota(jnp.int32, cosine.shape, 1)
    first = lane % HEAD_WIDTH < HALF
    for start in range(0, values.shape[1], LANES):
        part = values[:, start : start + LANES]
        partner = jnp.where(
            first, pltpu.roll(part, LANES - HALF, 1), pltpu.roll(part, HALF, 1)
        )
        turned.append(part * cosine + partner * sine)
    return turned[0] if len(turned) == 1 else jnp.concatenate(turned, axis=1)


def rms_of(values):
    return lax.rsqrt(jnp.mean(values * values, axis=-1, keepdims=True) + EPS)


def first_norm_kernel(
    x_ref, gain_ref, key_ref, value_ref, cos_ref, sin_ref, normed_ref, kv_ref
):
    x = x_ref[...].astype(F32)
    normed_ref[...] = (x * rms_of(x) * gain_ref[...]).astype(BF16)
    normed = normed_ref[...]
    kv_width = key_ref.shape[1]
    keys = rotate(dot_nn(normed, key_ref[...]), cos_ref[...], sin_ref[...])
    kv_ref[:, :kv_width] = keys.astype(BF16)
    kv_ref[:, kv_width:] = dot_nn(normed, value_ref[...]).astype(BF16)


def query_kernel(normed_ref, weight_ref, cos_ref, sin_ref, out_ref):
    queries = rotate(dot_nn(normed_ref[...], weight_ref[...]), cos_ref[...], sin_ref[...])
    out_ref[...] = (queries.astype(BF16).astype(F32) * (HEAD_WIDTH**-0.5)).astype(BF16)


def write_bias(here, bias_ref, count):
    tokens = bias_ref.shape[1]
    key = lax.broadcasted_iota(jnp.int32, (tokens, tokens), 0)
    query = lax.broadcasted_iota(jnp.int32, (tokens, tokens), 1)
    for k in range(count):
        allowed = (here ^ k) * tokens + key <= here * tokens + query
        bias_ref[k * tokens : (k + 1) * tokens, :] = jnp.where(allowed, 0.0, NEG_FILL)


def attend_kernel(count, kv_heads, group_blocks, here_ref, *refs):
    q_ref, kv_refs, weight_ref = refs[0], refs[1 : 1 + count], refs[1 + count]
    attn_ref, lse_ref, proj_ref, key_ref, turned_ref, bias_ref, total_ref = refs[2 + count :]
    tokens = q_ref.shape[0]
    step = pl.program_id(0)

    @pl.when(step == 0)
    def _():
        write_bias(here_ref[0], bias_ref, count)
        for k in range(count):
            rows = slice(k * tokens, (k + 1) * tokens)
            values_t = kv_refs[k][:, kv_heads * HEAD_WIDTH :].T
            for g in range(kv_heads):
                cut = slice(g * HEAD_WIDTH, (g + 1) * HEAD_WIDTH)
                key_ref[g, rows, :] = kv_refs[k][:, cut]
                turned_ref[g, :, rows] = values_t[cut, :]

    group = step // group_blocks
    keys, values_t = key_ref[group], turned_ref[group]
    heads = q_ref.shape[1] // HEAD_WIDTH
    outs = []
    for h in range(heads):
        query = q_ref[:, h * HEAD_WIDTH : (h + 1) * HEAD_WIDTH]
        scores = dot_nt(keys, query) + bias_ref[...]
        top = jnp.max(scores, axis=0, keepdims=True)
        expo = jnp.exp(scores - top)
        total = jnp.sum(expo, axis=0, keepdims=True)
        outs.append(dot_nn(values_t, expo.astype(BF16)) / total)
        lse_ref[0, h : h + 1, :] = top + jnp.log(total)
    attn_ref[...] = jnp.concatenate(outs, axis=0).T.astype(BF16)
    term = dot_nn(attn_ref[...], weight_ref[...])

    @pl.when(step == 0)
    def _():
        total_ref[...] = term

    @pl.when(step > 0)
    def _():
        total_ref[...] += term

    @pl.when(step == pl.num_programs(0) - 1)
    def _():
        proj_ref[...] = total_ref[...].astype(BF16)


def attend(chain, here, queries, kv_pieces, output_matrix):
    tokens, q_width = queries.shape
    count = len(kv_pieces)
    kv_heads = kv_pieces[0].shape[1] // (2 * HEAD_WIDTH)
    width = output_matrix.shape[1]
    block = 256
    blocks = q_width // block
    return chain(
        partial(attend_kernel, count, kv_heads, blocks // kv_heads),
        [
            shaped((tokens, q_width), BF16),
            shaped((blocks, block // HEAD_WIDTH, tokens), F32),
            shaped((tokens, width), BF16),
        ],
        here, queries, *kv_pieces, output_matrix,
        grid=(blocks,),
        in_specs=[pl.BlockSpec((tokens, block), lambda j, *_: (0, j))]
        + [whole(p.shape) for p in kv_pieces]
        + [pl.BlockSpec((block, width), lambda j, *_: (j, 0))],
        us=14.0,
        out_specs=[
            pl.BlockSpec((tokens, block), lambda j, *_: (0, j)),
            pl.BlockSpec((1, block // HEAD_WIDTH, tokens), lambda j, *_: (j, 0, 0)),
            whole((tokens, width)),
        ],
        scratch=[
            pltpu.VMEM((kv_heads, count * tokens, HEAD_WIDTH), BF16),
            pltpu.VMEM((kv_heads, HEAD_WIDTH, count * tokens), BF16),
            pltpu.VMEM((count * tokens, tokens), F32),
            pltpu.VMEM((tokens, width), F32),
        ],
        scalars=1,
    )


def attend_back_kernel(count, kv_heads, group_blocks, here_ref, *refs):
    q_ref, attn_ref, lse_ref, grad_ref, weight_ref, cos_ref, sin_ref = refs[:7]
    kv_refs, dq_ref = refs[7 : 7 + count], refs[7 + count]
    dkv_refs = refs[8 + count : 8 + 2 * count]
    key_ref, value_ref, turned_ref, bias_ref, dkey_ref, dvalue_ref = refs[8 + 2 * count :]
    tokens = q_ref.shape[0]
    step = pl.program_id(0)

    @pl.when(step == 0)
    def _():
        write_bias(here_ref[0], bias_ref, count)
        dkey_ref[...] = jnp.zeros_like(dkey_ref)
        dvalue_ref[...] = jnp.zeros_like(dvalue_ref)
        for k in range(count):
            rows = slice(k * tokens, (k + 1) * tokens)
            keys_t = kv_refs[k][:, : kv_heads * HEAD_WIDTH].T
            for g in range(kv_heads):
                cut = slice(g * HEAD_WIDTH, (g + 1) * HEAD_WIDTH)
                value_cut = slice((kv_heads + g) * HEAD_WIDTH, (kv_heads + g + 1) * HEAD_WIDTH)
                key_ref[g, rows, :] = kv_refs[k][:, cut]
                value_ref[g, rows, :] = kv_refs[k][:, value_cut]
                turned_ref[g, :, rows] = keys_t[cut, :]

    group = step // group_blocks
    keys, values, keys_t = key_ref[group], value_ref[group], turned_ref[group]
    d_attn = dot_nt(grad_ref[...], weight_ref[...])
    d_attn_b = d_attn.astype(BF16)
    products = (d_attn * attn_ref[...].astype(F32)).T
    heads = q_ref.shape[1] // HEAD_WIDTH
    d_queries, d_key, d_value = [], None, None
    for h in range(heads):
        cut = slice(h * HEAD_WIDTH, (h + 1) * HEAD_WIDTH)
        query, d_out = q_ref[:, cut], d_attn_b[:, cut]
        delta = jnp.sum(products[cut, :], axis=0, keepdims=True)
        probs = jnp.exp(dot_nt(keys, query) + bias_ref[...] - lse_ref[0, h : h + 1, :])
        d_scores = (probs * (dot_nt(values, d_out) - delta)).astype(BF16)
        value_term = dot_nn(probs.astype(BF16), d_out)
        key_term = dot_nn(d_scores, query)
        d_value = value_term if h == 0 else d_value + value_term
        d_key = key_term if h == 0 else d_key + key_term
        d_queries.append(dot_nn(keys_t, d_scores))
    dkey_ref[group] += d_key
    dvalue_ref[group] += d_value
    d_query = jnp.concatenate(d_queries, axis=0).T * (HEAD_WIDTH**-0.5)
    dq_ref[...] = rotate(d_query, cos_ref[...], -sin_ref[...]).astype(BF16)

    @pl.when(step == pl.num_programs(0) - 1)
    def _():
        for k in range(count):
            rows = slice(k * tokens, (k + 1) * tokens)
            for g in range(kv_heads):
                cut = slice(g * HEAD_WIDTH, (g + 1) * HEAD_WIDTH)
                value_cut = slice((kv_heads + g) * HEAD_WIDTH, (kv_heads + g + 1) * HEAD_WIDTH)
                dkv_refs[k][:, cut] = dkey_ref[g, rows, :].astype(BF16)
                dkv_refs[k][:, value_cut] = dvalue_ref[g, rows, :].astype(BF16)


def attend_back(chain, here, queries, attn_b, lse, grad, output_matrix, tables, kv_pieces):
    tokens, q_width = queries.shape
    count = len(kv_pieces)
    kv_heads = kv_pieces[0].shape[1] // (2 * HEAD_WIDTH)
    width = output_matrix.shape[1]
    block = 256
    blocks = q_width // block
    column = pl.BlockSpec((tokens, block), lambda j, *_: (0, j))
    outs = chain(
        partial(attend_back_kernel, count, kv_heads, blocks // kv_heads),
        [shaped((tokens, q_width), BF16)] + [shaped(p.shape, BF16) for p in kv_pieces],
        here, queries, attn_b, lse, grad, output_matrix, *tables, *kv_pieces,
        grid=(blocks,),
        in_specs=[
            column,
            column,
            pl.BlockSpec((1, block // HEAD_WIDTH, tokens), lambda j, *_: (j, 0, 0)),
            whole((tokens, width)),
            pl.BlockSpec((block, width), lambda j, *_: (j, 0)),
            whole(tables[0].shape),
            whole(tables[1].shape),
        ]
        + [whole(p.shape) for p in kv_pieces],
        us=16.0,
        out_specs=[column] + [whole(p.shape) for p in kv_pieces],
        scratch=[
            pltpu.VMEM((kv_heads, count * tokens, HEAD_WIDTH), BF16),
            pltpu.VMEM((kv_heads, count * tokens, HEAD_WIDTH), BF16),
            pltpu.VMEM((kv_heads, HEAD_WIDTH, count * tokens), BF16),
            pltpu.VMEM((count * tokens, tokens), F32),
            pltpu.VMEM((kv_heads, count * tokens, HEAD_WIDTH), F32),
            pltpu.VMEM((kv_heads, count * tokens, HEAD_WIDTH), F32),
        ],
        scalars=1,
    )
    return outs[0], outs[1:]


def kv_total_kernel(count, *refs):
    cos_ref, sin_ref, out_ref = refs[count:]
    total = refs[0][...].astype(F32)
    for k in range(1, count):
        total += refs[k][...].astype(F32)
    half = total.shape[1] // 2
    out_ref[:, :half] = rotate(total[:, :half], cos_ref[...], -sin_ref[...]).astype(BF16)
    out_ref[:, half:] = total[:, half:].astype(BF16)


def second_norm_kernel(
    here_ref, x_ref, own_ref, other_ref, gain_ref, resid_ref, normed_ref, *share_refs
):
    resid = x_ref[...].astype(F32) + (own_ref[...].astype(F32) + other_ref[...].astype(F32))
    resid_ref[...] = resid
    normed_ref[...] = (resid * rms_of(resid) * gain_ref[...]).astype(BF16)
    write_shares(here_ref[0], normed_ref, share_refs, by_core=True)


def feed_kernel(
    normed_ref, cot_ref, gate_ref, up_ref, down_ref, hidden_ref, d_both_ref
):
    gate = dot_nn(normed_ref[...], gate_ref[...])
    up = dot_nn(normed_ref[...], up_ref[...])
    d_hidden = dot_nt(cot_ref[...], down_ref[...])
    sigmoid = jax.nn.sigmoid(gate)
    active = gate * sigmoid
    hidden_ref[...] = (active * up).astype(BF16)
    d_gate = d_hidden * up * (sigmoid * (1.0 + gate * (1.0 - sigmoid)))
    block = hidden_ref.shape[1]
    d_both_ref[:, :block] = d_gate.astype(BF16)
    d_both_ref[:, block:] = (d_hidden * active).astype(BF16)


def feed_part(chain, normed, cotangent, gate_weight, up_weight, down_weight, first, blocks, block, after=()):
    tokens, width = normed.shape
    column = pl.BlockSpec((width, block), lambda j: (0, first + j))
    return chain(
        feed_kernel,
        [shaped((tokens, blocks * block), BF16), shaped((tokens, 2 * blocks * block), BF16)],
        normed, cotangent, gate_weight, up_weight, down_weight,
        grid=(blocks,),
        in_specs=[
            whole((tokens, width)),
            whole((tokens, width)),
            column,
            column,
            pl.BlockSpec((block, width), lambda j: (first + j, 0)),
        ],
        us=10.0,
        out_specs=[
            pl.BlockSpec((tokens, block), lambda j: (0, j)),
            pl.BlockSpec((tokens, 2 * block), lambda j: (0, j)),
        ],
        after=after,
    )


def part_column(refs, block, visit):
    step, first = pl.program_id(0), 0
    for ref in refs:
        blocks = ref.shape[1] // block
        here = (step >= first) & (step < first + blocks)
        offset = pl.multiple_of((step - first) * block, LANES)
        pl.when(here)(partial(visit, ref, pl.ds(offset, block)))
        first += blocks


def feed_back_kernel(started, block, *refs):
    both_ref, gate_ref, up_ref = refs[:3]
    out_ref, total_ref = refs[-2:]

    @pl.when(pl.program_id(0) == 0)
    def _():
        total_ref[...] = refs[3][...] if started else jnp.zeros_like(total_ref)

    both = both_ref[...]
    total_ref[...] += dot_nt(both[:, :block], gate_ref[...]) + dot_nt(both[:, block:], up_ref[...])

    @pl.when(pl.program_id(0) == pl.num_programs(0) - 1)
    def _():
        out_ref[...] = total_ref[...].astype(out_ref.dtype)


def feed_back(chain, d_both, gate_weight, up_weight, first, block, started, dtype, us, **options):
    tokens, width = d_both.shape[0], gate_weight.shape[0]
    column = pl.BlockSpec((width, block), lambda j: (0, first + j))
    return chain(
        partial(feed_back_kernel, len(started), block),
        shaped((tokens, width), dtype),
        d_both,
        gate_weight,
        up_weight,
        *started,
        grid=(d_both.shape[1] // (2 * block),),
        in_specs=[pl.BlockSpec((tokens, 2 * block), lambda j: (0, j)), column, column]
        + [whole((tokens, width))] * len(started),
        us=us,
        out_specs=whole((tokens, width)),
        scratch=[pltpu.VMEM((tokens, width), F32)],
        **options,
    )


def mixed_kernel(parts, block, *refs):
    hidden_refs = refs[:parts]
    weight_ref, out_ref, total_ref = refs[parts:]

    @pl.when(pl.program_id(0) == 0)
    def _():
        total_ref[...] = jnp.zeros_like(total_ref)

    def visit(ref, columns):
        total_ref[...] += dot_nn(ref[:, columns], weight_ref[...])

    part_column(hidden_refs, block, visit)

    @pl.when(pl.program_id(0) == pl.num_programs(0) - 1)
    def _():
        out_ref[...] = total_ref[...].astype(BF16)


def mix(chain, hidden, down_weight, block):
    tokens, width = hidden[0].shape[0], down_weight.shape[1]
    return chain(
        partial(mixed_kernel, len(hidden), block),
        shaped((tokens, width), BF16),
        *hidden, down_weight,
        grid=(down_weight.shape[0] // block,),
        in_specs=[whole(p.shape) for p in hidden]
        + [pl.BlockSpec((block, width), lambda j: (j, 0))],
        us=8.0,
        out_specs=whole((tokens, width)),
        scratch=[pltpu.VMEM((tokens, width), F32)],
    )


def norm_back(d_normed, inputs, gain):
    scale = rms_of(inputs)
    scaled = d_normed * gain
    back = scale * scaled - inputs * (scale * scale * scale) * jnp.mean(
        scaled * inputs, axis=-1, keepdims=True
    )
    return back, jnp.sum(d_normed * inputs * scale, axis=0, keepdims=True)


def second_back_kernel(
    here_ref,
    cot_ref,
    own_ref,
    other_ref,
    resid_ref,
    gain_ref,
    d_resid_ref,
    rounded_ref,
    gain_grad_ref,
    *share_refs,
):
    d_normed = own_ref[...].astype(F32) + other_ref[...].astype(F32)
    back, gain_grad_ref[...] = norm_back(d_normed, resid_ref[...], gain_ref[...])
    d_resid = cot_ref[...].astype(F32) + back
    d_resid_ref[...] = d_resid
    rounded_ref[...] = d_resid.astype(BF16)
    write_shares(here_ref[0], rounded_ref, share_refs)


def first_back_kernel(dq_ref, dkv_ref, query_ref, key_ref, value_ref, out_ref):
    half = key_ref.shape[1]
    out_ref[...] = (
        dot_nt(dq_ref[...], query_ref[...])
        + dot_nt(dkv_ref[:, :half], key_ref[...])
        + dot_nt(dkv_ref[:, half:], value_ref[...])
    ).astype(BF16)


def output_kernel(resid_ref, own_ref, other_ref, out_ref):
    mixed = own_ref[...].astype(F32) + other_ref[...].astype(F32)
    out_ref[...] = (resid_ref[...] + mixed).astype(BF16)


def last_kernel(own_ref, other_ref, x_ref, gain_ref, d_resid_ref, out_ref, gain_grad_ref):
    d_normed = own_ref[...].astype(F32) + other_ref[...].astype(F32)
    back, gain_grad_ref[...] = norm_back(d_normed, x_ref[...].astype(F32), gain_ref[...])
    out_ref[...] = (d_resid_ref[...] + back).astype(BF16)


def on_device(
    layer_input,
    cotangent,
    attn_gain,
    query_weight,
    key_matrix,
    value_matrix,
    output_matrix,
    feed_gain,
    gate_weight,
    up_weight,
    down_weight,
):
    block_shape = layer_input.shape
    tokens = block_shape[0] * block_shape[1]
    width = block_shape[2]
    x = layer_input.reshape(tokens, width)
    cot = cotangent.reshape(tokens, width)
    q_width, kv_width = query_weight.shape[1], key_matrix.shape[1]
    feed_width = gate_weight.shape[1]
    here = lax.axis_index(CONTEXT).astype(jnp.int32).reshape(1)
    attn_gain, feed_gain = attn_gain.reshape(1, width), feed_gain.reshape(1, width)
    tables = rotary_tables(tokens)
    flat, gain = (tokens, width), (1, width)
    shares = share_shapes(tokens, width)
    share_specs = [whole(s.shape) for s in shares]
    table = whole(tables[0].shape)

    chain = Chain()
    first_normed, kv_own = chain(
        first_norm_kernel,
        [shaped(flat, BF16), shaped((tokens, 2 * kv_width), BF16)],
        x,
        attn_gain,
        key_matrix,
        value_matrix,
        *tables,
        in_specs=[
            whole(flat),
            whole(gain),
            whole(key_matrix.shape),
            whole(value_matrix.shape),
            table,
            table,
        ],
        us=1.5,
        out_specs=[whole(flat), whole((tokens, 2 * kv_width))],
    )
    kv_pieces = exchange_context([kv_own] * lax.axis_size(CONTEXT))
    queries = chain(
        query_kernel,
        shaped((tokens, q_width), BF16),
        first_normed,
        query_weight,
        *tables,
        grid=(q_width // 256,),
        in_specs=[whole(flat), pl.BlockSpec((width, 256), lambda j: (0, j)), table, table],
        us=3.0,
        out_specs=pl.BlockSpec((tokens, 256), lambda j: (0, j)),
    )
    cot_cols = exchange_chips(pick_shares(chain, here, cot))
    attn_b, lse, attn_proj = attend(chain, here, queries, kv_pieces, output_matrix)
    attn_other = swap(attn_proj, "tensor", 1)
    attn_pieces = gather_chips(attn_b)
    first_shares = pick_shares(chain, here, first_normed, after=cot_cols)

    resid, normed_two, *two_shares = chain(
        second_norm_kernel,
        [shaped(flat, F32), shaped(flat, BF16)] + shares,
        here,
        x,
        attn_proj,
        attn_other,
        feed_gain,
        in_specs=[whole(flat)] * 3 + [whole(gain)],
        us=2.0,
        out_specs=[whole(flat)] * 2 + share_specs,
        scalars=1,
        after=attn_pieces,
    )
    two_cols = exchange_chips(shares_of(normed_two, two_shares, by_core=True))

    block = pick_block(feed_width, 256)
    blocks = feed_width // block
    cut = blocks * 5 // 11
    weights = (gate_weight, up_weight)
    feed = partial(feed_part, chain, normed_two, cot, *weights, down_weight)
    hidden_one, both_one = feed(0, cut, block)
    hidden_one_pieces, both_one_pieces = gather_chips(hidden_one), gather_chips(both_one)
    hidden_two, both_two = feed(cut, blocks - cut, block, after=two_cols)
    down_one = Ring(chain, *column_products(chain, hidden_one_pieces, cot_cols))
    d_two, hidden_two, both_two = feed_back(
        chain,
        both_one,
        *weights,
        0,
        block,
        [],
        F32,
        7.0,
        carry=[hidden_two, both_two],
    )
    hidden_two_pieces = gather_chips(hidden_two)
    down_one.step()
    d_two, both_two = feed_back(
        chain, both_two, *weights, cut, block, [d_two], BF16, 8.0, carry=[both_two]
    )
    both_two_pieces = gather_chips(both_two)
    d_two_other = swap(d_two, "tensor", 1)
    down_one.step()
    both_one_share = row_scatter(chain, two_cols, both_one_pieces)
    down_one.step()
    d_resid, d_resid_b, feed_gain_sum, *resid_shares = chain(
        second_back_kernel,
        [shaped(flat, F32), shaped(flat, BF16), shaped(gain, F32)] + shares,
        here,
        cot,
        d_two,
        d_two_other,
        resid,
        feed_gain,
        in_specs=[whole(flat)] * 4 + [whole(gain)],
        us=4.0,
        out_specs=[whole(flat)] * 2 + [whole(gain)] + share_specs,
        scalars=1,
    )
    down_one.step()
    down_two = Ring(chain, *column_products(chain, hidden_two_pieces, cot_cols))
    d_query, d_kv_parts = attend_back(
        chain, here, queries, attn_b, lse, d_resid_b, output_matrix, tables, kv_pieces
    )
    resid_cols = exchange_chips(shares_of(d_resid_b, resid_shares))
    d_kv_pieces = exchange_context(d_kv_parts)
    query_pieces = gather_chips(d_query)
    down_two.step()
    mixed = mix(chain, [hidden_one, hidden_two], down_weight, block)
    down_two.step()
    both_two_share = row_scatter(chain, two_cols, both_two_pieces)
    d_kv = chain(
        partial(kv_total_kernel, len(d_kv_pieces)),
        shaped((tokens, 2 * kv_width), BF16),
        *d_kv_pieces,
        *tables,
        in_specs=[whole((tokens, 2 * kv_width))] * len(d_kv_pieces) + [table] * 2,
        out_specs=whole((tokens, 2 * kv_width)),
    )
    row_block = pick_block(width, 512)
    d_one = chain(
        first_back_kernel,
        shaped(flat, BF16),
        d_query,
        d_kv,
        query_weight,
        key_matrix,
        value_matrix,
        grid=(width // row_block,),
        in_specs=[
            whole((tokens, q_width)),
            whole((tokens, 2 * kv_width)),
            pl.BlockSpec((row_block, q_width), lambda j: (j, 0)),
            pl.BlockSpec((row_block, kv_width), lambda j: (j, 0)),
            pl.BlockSpec((row_block, kv_width), lambda j: (j, 0)),
        ],
        us=2.5,
        out_specs=pl.BlockSpec((tokens, row_block), lambda j: (0, j)),
    )
    d_one_other = swap(d_one, "tensor", 1)
    kv_grad_pieces = gather_chips(d_kv)
    first_cols = exchange_chips(first_shares)
    down_two.step()
    out_ring = Ring(chain, *column_products(chain, attn_pieces, resid_cols))
    down_two.step()
    out_ring.step()
    query_ring = Ring(chain, *row_products(chain, first_cols, query_pieces))
    out_ring.step()
    query_ring.step()
    kv_ring = Ring(chain, *row_products(chain, first_cols, kv_grad_pieces))
    input_grad, attn_gain_sum = chain(
        last_kernel,
        [shaped(flat, BF16), shaped(gain, F32)],
        d_one,
        d_one_other,
        x,
        attn_gain,
        d_resid,
        in_specs=[whole(flat)] * 3 + [whole(gain), whole(flat)],
        us=3.0,
        out_specs=[whole(flat), whole(gain)],
    )
    mixed_other = swap(mixed, "tensor", 1)
    gains = scatter_gains(jnp.concatenate([attn_gain_sum, feed_gain_sum], axis=0))
    kv_ring.step()
    out_ring.step()
    query_ring.step()
    kv_ring.step()
    out_ring.step()
    query_ring.step()
    kv_ring.step()
    layer_output = chain(
        output_kernel,
        shaped(flat, BF16),
        resid,
        mixed,
        mixed_other,
        in_specs=[whole(flat)] * 3,
        us=2.0,
        out_specs=whole(flat),
    )
    finish([down_one, down_two, out_ring, query_ring, kv_ring])
    both = [both_one_share, both_two_share]
    share = both[0].shape[0]
    gate_share, up_share = chain(
        partial(dealt_kernel, block),
        [shaped((share, feed_width), F32)] * 2,
        *both,
        in_specs=[whole(b.shape) for b in both],
        out_specs=[whole((share, feed_width))] * 2,
    )

    return (
        layer_output.reshape(block_shape),
        input_grad.reshape(block_shape),
        gains[0],
        query_ring.result[0],
        kv_ring.result[0][:, :kv_width],
        kv_ring.result[0][:, kv_width:],
        out_ring.result[0],
        gains[1],
        gate_share,
        up_share,
        jnp.concatenate([down_one.result[0], down_two.result[0]], axis=0),
    )


def solution(mesh):
    tensor, dp, context = (mesh.shape[a] for a in ("tensor", "dp", "context"))
    axes = ("tensor", "dp") + CONTEXT
    split = jax.sharding.Mesh(mesh.devices.reshape(tensor, dp, context // 2, 2), axes)
    activation = P(CONTEXT, "dp", None)
    rows, columns = P(None, "tensor"), P("tensor", None)
    vector_share, row_share = P(("dp",) + CONTEXT), P(("dp",) + CONTEXT, "tensor")
    column_share = P("tensor", ("dp",) + CONTEXT)
    in_specs = (activation, activation, P(), rows, rows, rows, columns, P(), rows, rows, columns)
    out_specs = (
        activation,
        activation,
        vector_share,
        row_share,
        row_share,
        row_share,
        column_share,
        vector_share,
        row_share,
        row_share,
        column_share,
    )
    return jax.shard_map(
        on_device, mesh=split, in_specs=in_specs, out_specs=out_specs, check_vma=False
    )
```

time: 571 us -> 354 us (0.62); the launches traced: 563 us -> 353 us
  waiting for transfers between devices: 248 us -> 119 us
  Pallas kernels: 33.2 us -> 130 us
  matrix products: 66.5 us -> 0 us
  local copies, waits for them, and re-layouts: 98 us -> 44.7 us
  other arithmetic: 35.4 us -> 3.33 us
  starting transfers between devices: 65.5 us -> 40.7 us
  between operations: 1.9 us -> 15.2 us
  blocking collectives: 8.65 us -> 0 us
  loops' own time: 5.77 us -> 0 us
    pallas_call x5 -> x45, Pallas kernels: 33.2 us -> 130 us  [__call__(): pl.pallas_call(stripped, out_shape=out_shape + [shaped(c.shape, c.dtype)...]
    dot_general x21 -> x0, matrix products: 66.5 us -> none  [the longest x7 30.6 us: dot_nt(): lax.dot_general(a, b, (((1,), (1,)), ((), ())), preferred_element_type=F32)]
    ppermute x46 -> x32, waiting for transfers between devices: 107 us -> 41.9 us  [swap(): return lax.ppermute(value, axis, [(i, i ^ flip) for i in range(count)])]
    ppermute x15, waiting for transfers between devices: 141 us -> 77.4 us  [step(): self.arrived = lax.ppermute(total, 'dp', ring)]
    dynamic_slice x19 -> x2, local copies, waits for them, and re-layouts: 44.8 us -> 1.48 us  [the longest x1 1.47 us: scatter_gains(): lax.dynamic_index_in_dim(blocks, ctx_here ^ k, 2, keepdims=False)]
    ppermute x46 -> x32, starting transfers between devices: 57.8 us -> 31.1 us  [swap(): return lax.ppermute(value, axis, [(i, i ^ flip) for i in range(count)])]
    unnamed x106 -> x205, local copies, waits for them, and re-layouts: 27.5 us -> 40.7 us
    convert_element_type x15 -> x1, other arithmetic: 9.5 us -> 0.01 us  [rotary_tables(): angles = positions.astype(F32)[:, None] * frequencies[None, :]]
  transfers between devices with their start and end apart: 61 -> 49, of which waited for: 18 -> 22; matrix products, arithmetic and copies ran while one was open for 30% -> 2% of each run, Pallas kernels for 6% -> 31%
where the time goes in v2:
time: 354 us; the launch traced here: 353 us
  Pallas kernels  130 us (37%)
  waiting for transfers between devices  119 us (34%)
  local copies, waits for them, and re-layouts  44.7 us (13%)
  starting transfers between devices  40.7 us (11%)
  between operations  15.2 us (4%)
    pallas_call x45, Pallas kernels, __call__(): pl.pallas_call(stripped, out_shape=out_shape + [shaped(c.shape, c.dtype)...  130 us
    ppermute x15, waiting for transfers between devices, step(): self.arrived = lax.ppermute(total, 'dp', ring)  77.4 us
    ppermute x32, waiting for transfers between devices, swap(): return lax.ppermute(value, axis, [(i, i ^ flip) for i in range(count)])  41.9 us
    unnamed x205, local copies, waits for them, and re-layouts  40.7 us
    ppermute x32, starting transfers between devices, swap(): return lax.ppermute(value, axis, [(i, i ^ flip) for i in range(count)])  31.1 us
    ppermute x15, starting transfers between devices, step(): self.arrived = lax.ppermute(total, 'dp', ring)  9.5 us
  transfers between devices with their start and end apart: 49, of which 22 were waited for; matrix products, arithmetic and copies ran while one was open for 2% of the time, Pallas kernels for 31%

profile of v2, /device:TPU:0, one launch (start us, length us, event | category | flops | bytes accessed | tf_op | source)
XLA Modules:
  0.0 352.9 jit_solution(4691356814475541026)
XLA Ops:
  8.1 1.3 copy-done.21
  13.2 2.5 collective-permute-start.2
  16.4 3.0 shard_map.195.refs_2_.refs_1_
  20.5 2.0 collective-permute-done.1.refs_4_.refs_10_
  22.6 15.3 %shard_map.197 = (bf16[256,1024]{1,0:T(8,128)(2,1)}, f32[4,4,256]{2,1,0:T(4,128)S(1)}, bf16[256,2048]{1,0:T(8,128)(2,1)S(1)}) custom-call(s32[1]{0:T(128)} %bitcast.refs_0_, bf16[256,1024]{1,0:T(8,128)(2,1)S(1)} %shard_map.195.refs_2_.refs_1_, bf16[256,256]{1,0:T(8,128)(2,1)S(1)} %get-tuple-element.58.refs_2_.refs_8_, ...), custom_call_target="tpu_custom_call" | custom-call | flops 46200000512 | bytes 1000 | tf_op jit(solution)/shard_map/pallas_call | solution.py:73
  37.9 2.3 collective-permute-start.3
  40.2 1.5 collective-permute-start.4
  42.3 13.1 %collective-permute-done.4.refs_4_.refs_1_ = bf16[256,1024]{1,0:T(8,128)(2,1)} collective-permute-done((bf16[256,1024]{1,0:T(8,128)(2,1)}, bf16[256,1024]{1,0:T(8,128)(2,1)}, u32[]{:S(2)}, u32[]{:S(2)}) %collective-permute-start.4) | collective-permute-done | bytes 524320 | tf_op jit(solution)/shard_map/ppermute | solution.py:95
  58.0 7.4 %collective-permute-done.5.refs_7_.refs_3_ = bf16[256,1024]{1,0:T(8,128)(2,1)} collective-permute-done((bf16[256,1024]{1,0:T(8,128)(2,1)}, bf16[256,1024]{1,0:T(8,128)(2,1)}, u32[]{:S(2)}, u32[]{:S(2)}) %collective-permute-start.5) | collective-permute-done | bytes 524320 | tf_op jit(solution)/shard_map/ppermute | solution.py:95
  66.7 1.6 collective-permute-start.6
  68.3 8.8 %shard_map.200 = (bf16[256,1280]{1,0:T(8,128)(2,1)S(1)}, bf16[256,2560]{1,0:T(8,128)(2,1)S(1)}) custom-call(bf16[256,2048]{1,0:T(8,128)(2,1)S(1)} %get-tuple-element.65.refs_0_, bf16[256,2048]{1,0:T(8,128)(2,1)S(1)} %bitcast.53, bf16[2048,2816]{1,0:T(8,128)(2,1)} %refs_1_.5, bf16[2048,2816]{1,0:T(8,128)(2,1)} %refs_2_.11, bf16[2816,2048]{1,0:T(8,128)(2,1)} %refs_2_.12, ...), custom_call_target="tpu_custom_call" | custom-call | flops 32999999488 | bytes 1000 | tf_op jit(solution)/shard_map/pallas_call | solution.py:73
  80.3 11.1 %shard_map.201 = (bf16[256,1536]{1,0:T(8,128)(2,1)}, bf16[256,3072]{1,0:T(8,128)(2,1)S(1)}) custom-call(bf16[256,2048]{1,0:T(8,128)(2,1)S(1)} %get-tuple-element.65.refs_0_, bf16[256,2048]{1,0:T(8,128)(2,1)S(1)} %bitcast.54, bf16[2048,2816]{1,0:T(8,128)(2,1)} %refs_1_.5, bf16[2048,2816]{1,0:T(8,128)(2,1)} %refs_2_.11, bf16[2816,2048]{1,0:T(8,128)(2,1)} %refs_2_.12, ...), custom_call_target="tpu_custom_call" | custom-call | flops 32999999488 | bytes 1000 | tf_op jit(solution)/shard_map/pallas_call | solution.py:73
  91.4 3.6 %collective-permute-done.7.refs_3_ = bf16[256,1280]{1,0:T(8,128)(2,1)S(1)} collective-permute-done((bf16[256,1280]{1,0:T(8,128)(2,1)S(1)}, bf16[256,1280]{1,0:T(8,128)(2,1)S(1)}, u32[]{:S(2)}, u32[]{:S(2)}) %collective-permute-start.7) | collective-permute-done | bytes 655392 | tf_op jit(solution)/shard_map/ppermute | solution.py:95
  95.0 3.6 %shard_map.202 = (bf16[4,1280,128]{2,1,0:T(8,128)(2,1)S(1)}, bf16[4,1280,128]{2,1,0:T(8,128)(2,1)S(1)}) custom-call(bf16[256,1024]{1,0:T(8,128)(2,1)S(1)} %copy-done.94, bf16[256,1024]{1,0:T(8,128)(2,1)} %collective-permute-done.4.refs_4_.refs_1_, bf16[256,1280]{1,0:T(8,128)(2,1)S(1)} %get-tuple-element.66.refs_5_.refs_2_.refs_0_, ...), custom_call_target="tpu_custom_call" | custom-call | flops 9900000256 | bytes 1000 | tf_op jit(solution)/shard_map/pallas_call | solution.py:73
  98.7 7.7 %shard_map.203 = (f32[256,2048]{1,0:T(8,128)S(1)}, bf16[256,1536]{1,0:T(8,128)(2,1)}, bf16[256,3072]{1,0:T(8,128)(2,1)S(1)}) custom-call(bf16[256,2560]{1,0:T(8,128)(2,1)S(1)} %get-tuple-element.67.refs_0_.refs_2_, bf16[2048,2816]{1,0:T(8,128)(2,1)} %refs_1_.5, bf16[2048,2816]{1,0:T(8,128)(2,1)} %refs_2_.11, ...), custom_call_target="tpu_custom_call", output_to_operand_aliasing={{1}: (3, {}), {2}: (4, {})} | custom-call | flops 23100000256 | bytes 1000 | tf_op jit(solution)/shard_map/pallas_call | solution.py:73
  106.4 1.6 collective-permute-start.8
  108.2 1.6 collective-permute-start.10
  109.8 9.3 %shard_map.205 = (bf16[256,2048]{1,0:T(8,128)(2,1)}, bf16[256,3072]{1,0:T(8,128)(2,1)S(1)}) custom-call(bf16[256,3072]{1,0:T(8,128)(2,1)S(1)} %get-tuple-element.76.refs_0_, bf16[2048,2816]{1,0:T(8,128)(2,1)} %refs_1_.5, bf16[2048,2816]{1,0:T(8,128)(2,1)} %refs_2_.11, f32[256,2048]{1,0:T(8,128)S(1)} %get-tuple-element.75.refs_3_, ...), custom_call_target="tpu_custom_call", output_to_operand_aliasing={{1}: (4, {})} | custom-call | flops 26400000000 | bytes 1000 | tf_op jit(solution)/shard_map/pallas_call | solution.py:73
  120.3 1.6 collective-permute-start.11
  123.1 4.4 %shard_map.207.refs_4_ = bf16[4,2,128,2560]{3,2,1,0:T(8,128)(2,1)S(1)} custom-call(bf16[256,1024]{1,0:T(8,128)(2,1)S(1)} %get-tuple-element.68.refs_6_.refs_0_, bf16[256,1024]{1,0:T(8,128)(2,1)S(1)} %collective-permute-done.6.refs_7_.refs_1_, bf16[256,2560]{1,0:T(8,128)(2,1)S(1)} %get-tuple-element.67.refs_0_.refs_2_, ...), custom_call_target="tpu_custom_call" | custom-call | flops 16499999744 | bytes 1000 | tf_op jit(solution)/shard_map/pallas_call | solution.py:73
  127.5 2.4 copy-done.1
  130.8 2.5 copy-done.2
  133.3 1.3 copy-done.17
  134.6 1.3 copy-done.74
  137.9 6.1 %collective-permute-done.14.refs_3_ = bf16[256,2048]{1,0:T(8,128)(2,1)} collective-permute-done((bf16[256,2048]{1,0:T(8,128)(2,1)}, bf16[256,2048]{1,0:T(8,128)(2,1)}, u32[]{:S(2)}, u32[]{:S(2)}) %collective-permute-start.14) | collective-permute-done | bytes 1048608 | tf_op jit(solution)/shard_map/ppermute | solution.py:95
  144.1 4.7 %shard_map.209 = (f32[256,2048]{1,0:T(8,128)S(1)}, bf16[256,2048]{1,0:T(8,128)(2,1)S(1)}, f32[1,2048]{1,0:T(1,128)S(1)}, bf16[256,1024]{1,0:T(8,128)(2,1)S(1)}, bf16[256,1024]{1,0:T(8,128)(2,1)}) custom-call(s32[1]{0:T(128)} %bitcast.refs_0_, bf16[256,2048]{1,0:T(8,128)(2,1)S(1)} %bitcast.55, bf16[256,2048]{1,0:T(8,128)(2,1)} %get-tuple-element.77.refs_4_.refs_2_, ...), custom_call_target="tpu_custom_call" | custom-call | flops 13200000000 | bytes 1000 | tf_op jit(solution)/shard_map/pallas_call | solution.py:73
  149.3 6.2 %collective-permute-done.13.refs_3_ = bf16[1,1280,128]{2,1,0:T(8,128)(2,1)S(1)} collective-permute-done((bf16[1,1280,128]{2,1,0:T(8,128)(2,1)S(1)}, bf16[1,1280,128]{2,1,0:T(8,128)(2,1)S(1)}, u32[]{:S(2)}, u32[]{:S(2)}) %collective-permute-start.13) | collective-permute-done | bytes 327712 | tf_op jit(solution)/shard_map/ppermute | solution.py:368
  156.5 4.6 %shard_map.211 = (bf16[4,1536,128]{2,1,0:T(8,128)(2,1)S(1)}, bf16[4,1536,128]{2,1,0:T(8,128)(2,1)S(1)}) custom-call(bf16[256,1024]{1,0:T(8,128)(2,1)S(1)} %copy-done.95, bf16[256,1024]{1,0:T(8,128)(2,1)} %collective-permute-done.4.refs_4_.refs_1_, bf16[256,1536]{1,0:T(8,128)(2,1)} %get-tuple-element.73.refs_2_.refs_1_, ...), custom_call_target="tpu_custom_call" | custom-call | flops 9900000256 | bytes 1000 | tf_op jit(solution)/shard_map/pallas_call | solution.py:73
  161.3 16.6 %shard_map.212 = (bf16[256,1024]{1,0:T(8,128)(2,1)S(1)}, bf16[256,256]{1,0:T(8,128)(2,1)S(1)}, bf16[256,256]{1,0:T(8,128)(2,1)S(1)}, bf16[256,256]{1,0:T(8,128)(2,1)S(1)}, bf16[256,256]{1,0:T(8,128)(2,1)S(1)}) custom-call(s32[1]{0:T(128)} %bitcast.refs_0_, bf16[256,1024]{1,0:T(8,128)(2,1)S(1)} %copy-done.97, ...), custom_call_target="tpu_custom_call" | custom-call | flops 52800000000 | bytes 1000 | tf_op jit(solution)/shard_map/pallas_call | solution.py:73
  178.3 1.6 collective-permute-start.19
  180.1 1.4 copy-done.32
  181.5 4.4 %copy-done.9 = bf16[2816,2048]{1,0:T(8,128)(2,1)S(1)} copy-done((bf16[2816,2048]{1,0:T(8,128)(2,1)S(1)}, bf16[2816,2048]{1,0:T(8,128)(2,1)}, u32[]{:S(2)}) %copy-start.9) | copy-done | bytes 11534360
  185.8 6.6 %shard_map.214.refs_4_.refs_1_ = bf16[256,2048]{1,0:T(8,128)(2,1)S(1)} custom-call(bf16[256,1280]{1,0:T(8,128)(2,1)S(1)} %copy-done.32, bf16[256,1536]{1,0:T(8,128)(2,1)} %get-tuple-element.73.refs_2_.refs_1_, bf16[2816,2048]{1,0:T(8,128)(2,1)S(1)} %copy-done.9, bf16[1,1536,128]{2,1,0:T(8,128)(2,1)S(1)} %shard_map.213.refs_3_), custom_call_target="tpu_custom_call" | custom-call | flops 26400000000 | bytes 1000 | tf_op jit(solution)/shard_map/pallas_call | solution.py:73
  192.4 9.5 %collective-permute-done.22.refs_3_ = bf16[1,1536,128]{2,1,0:T(8,128)(2,1)S(1)} collective-permute-done((bf16[1,1536,128]{2,1,0:T(8,128)(2,1)S(1)}, bf16[1,1536,128]{2,1,0:T(8,128)(2,1)S(1)}, u32[]{:S(2)}, u32[]{:S(2)}) %collective-permute-start.22) | collective-permute-done | bytes 393248 | tf_op jit(solution)/shard_map/ppermute | solution.py:368
  203.3 5.3 %shard_map.216.refs_6_ = bf16[4,2,128,3072]{3,2,1,0:T(8,128)(2,1)S(1)} custom-call(bf16[256,1024]{1,0:T(8,128)(2,1)S(1)} %copy-done.99, bf16[256,1024]{1,0:T(8,128)(2,1)S(1)} %copy-done.40, bf16[256,3072]{1,0:T(8,128)(2,1)S(1)} %get-tuple-element.89.refs_2_, bf16[256,3072]{1,0:T(8,128)(2,1)S(1)} %collective-permute-done.21.refs_3_, ...), custom_call_target="tpu_custom_call" | custom-call | flops 16499999744 | bytes 1000 | tf_op jit(solution)/shard_map/pallas_call | solution.py:73
  208.9 2.9 copy-done
  211.8 1.3 copy-done.13
  213.3 2.3 shard_map.218.refs_4_.refs_0_
  217.1 1.4 copy-done.79
  219.8 3.0 shard_map.220
  223.2 1.6 collective-permute-start.17
  225.3 19.7 %collective-permute-done.28.refs_3_ = bf16[1,1536,128]{2,1,0:T(8,128)(2,1)S(1)} collective-permute-done((bf16[1,1536,128]{2,1,0:T(8,128)(2,1)S(1)}, bf16[1,1536,128]{2,1,0:T(8,128)(2,1)S(1)}, u32[]{:S(2)}, u32[]{:S(2)}) %collective-permute-start.28) | collective-permute-done | bytes 393248 | tf_op jit(solution)/shard_map/ppermute | solution.py:368
  246.1 2.3 collective-permute-done.24.refs_3_
  248.4 2.7 shard_map.223
  252.1 1.6 collective-permute-start.23
  253.7 1.5 collective-permute-start.32
  255.2 13.4 %collective-permute-done.30.refs_3_ = bf16[1,1024,128]{2,1,0:T(8,128)(2,1)S(1)} collective-permute-done((bf16[1,1024,128]{2,1,0:T(8,128)(2,1)S(1)}, bf16[1,1024,128]{2,1,0:T(8,128)(2,1)S(1)}, u32[]{:S(2)}, u32[]{:S(2)}) %collective-permute-start.30) | collective-permute-done | bytes 262176 | tf_op jit(solution)/shard_map/ppermute | solution.py:368
  275.0 4.0 %collective-permute-done.32.refs_1_ = bf16[256,2048]{1,0:T(8,128)(2,1)S(1)} collective-permute-done((bf16[256,2048]{1,0:T(8,128)(2,1)S(1)}, bf16[256,2048]{1,0:T(8,128)(2,1)S(1)}, u32[]{:S(2)}, u32[]{:S(2)}) %collective-permute-start.32) | collective-permute-done | bytes 1048608 | tf_op jit(solution)/shard_map/ppermute | solution.py:95
  279.0 3.1 shard_map.227
  282.8 1.3 reshape.117
  284.1 1.5 constant_dynamic-slice_fusion.6
  286.0 1.7 collective-permute-start.41
  287.7 1.5 collective-permute-start.16
  290.1 3.6 %collective-permute-start.44 = (f32[2,128]{1,0:T(2,128)S(1)}, f32[2,128]{1,0:T(2,128)S(1)}, u32[]{:S(2)}, u32[]{:S(2)}) collective-permute-start(f32[2,128]{1,0:T(2,128)S(1)} %bitcast.84), channel_id=1, source_target_pairs={{0,12},{4,8},{8,4},{12,0},{1,13},{5,9},{9,5},{13,1},{2,14},{6,10},... | collective-permute-start | bytes 3080 | tf_op jit(solution)/shard_map/ppermute | solution.py:95
  296.6 2.0 collective-permute-start.35
  300.8 1.3 collective-permute-start.33
  302.1 5.5 %collective-permute-done.35.refs_3_ = bf16[1,1024,128]{2,1,0:T(8,128)(2,1)S(1)} collective-permute-done((bf16[1,1024,128]{2,1,0:T(8,128)(2,1)S(1)}, bf16[1,1024,128]{2,1,0:T(8,128)(2,1)S(1)}, u32[]{:S(2)}, u32[]{:S(2)}) %collective-permute-start.35) | collective-permute-done | bytes 262176 | tf_op jit(solution)/shard_map/ppermute | solution.py:368
  308.0 5.2 %collective-permute-done.34.refs_3_ = bf16[1,128,1024]{2,1,0:T(8,128)(2,1)S(1)} collective-permute-done((bf16[1,128,1024]{2,1,0:T(8,128)(2,1)S(1)}, bf16[1,128,1024]{2,1,0:T(8,128)(2,1)S(1)}, u32[]{:S(2)}, u32[]{:S(2)}) %collective-permute-start.34) | collective-permute-done | bytes 262176 | tf_op jit(solution)/shard_map/ppermute | solution.py:368
  315.2 5.0 %collective-permute-done.38.refs_3_ = bf16[1,1024,128]{2,1,0:T(8,128)(2,1)S(1)} collective-permute-done((bf16[1,1024,128]{2,1,0:T(8,128)(2,1)S(1)}, bf16[1,1024,128]{2,1,0:T(8,128)(2,1)S(1)}, u32[]{:S(2)}, u32[]{:S(2)}) %collective-permute-start.38) | collective-permute-done | bytes 262176 | tf_op jit(solution)/shard_map/ppermute | solution.py:368
  321.1 4.7 %collective-permute-done.37.refs_3_ = bf16[1,128,1024]{2,1,0:T(8,128)(2,1)S(1)} collective-permute-done((bf16[1,128,1024]{2,1,0:T(8,128)(2,1)S(1)}, bf16[1,128,1024]{2,1,0:T(8,128)(2,1)S(1)}, u32[]{:S(2)}, u32[]{:S(2)}) %collective-permute-start.37) | collective-permute-done | bytes 262176 | tf_op jit(solution)/shard_map/ppermute | solution.py:368
  329.4 1.3 shard_map.235.refs_4_
  330.7 6.5 %collective-permute-done.45.refs_3_ = bf16[1,128,1024]{2,1,0:T(8,128)(2,1)S(1)} collective-permute-done((bf16[1,128,1024]{2,1,0:T(8,128)(2,1)S(1)}, bf16[1,128,1024]{2,1,0:T(8,128)(2,1)S(1)}, u32[]{:S(2)}, u32[]{:S(2)}) %collective-permute-start.45) | collective-permute-done | bytes 262176 | tf_op jit(solution)/shard_map/ppermute | solution.py:368
  338.5 1.8 shard_map.236.refs_4_
  344.3 1.8 shard_map.238
  (299 shorter events, 54.2 us)
Async XLA Ops:
  7.2 334.9 %reduce-scatter.3.cloned.1.call-start = ((), (), s32[]{:S(2)}) async-start(), calls=%async_computation.2 | async-start | bytes 5898240 | tf_op jit(solution)/shard_map/reduce_scatter | solution.py:273
  13.2 7.3 %collective-permute-start.2 = (bf16[256,256]{1,0:T(8,128)(2,1)S(1)}, bf16[256,256]{1,0:T(8,128)(2,1)S(1)}, u32[]{:S(2)}, u32[]{:S(2)}) collective-permute-start(bf16[256,256]{1,0:T(8,128)(2,1)S(1)} %get-tuple-element.58.refs_2_.refs_8_), channel_id=1, source_target_pairs={{0,3},{1,2},{2,1},{3,0},{4,7},{5,6},{6,5},{7,4},{8,11},{9,10},{10,... | collective-permute-start | bytes 393224 | tf_op jit(solution)/shard_map/ppermute | solution.py:95
  15.7 6.9 %collective-permute-start.1 = (bf16[256,256]{1,0:T(8,128)(2,1)S(1)}, bf16[256,256]{1,0:T(8,128)(2,1)S(1)}, u32[]{:S(2)}, u32[]{:S(2)}) collective-permute-start(bf16[256,256]{1,0:T(8,128)(2,1)S(1)} %get-tuple-element.58.refs_2_.refs_8_), channel_id=1, source_target_pairs={{0,2},{1,3},{2,0},{3,1},{4,6},{5,7},{6,4},{7,5},{8,10},{9,11},{10,... | collective-permute-start | bytes 393224 | tf_op jit(solution)/shard_map/ppermute | solution.py:95
  16.3 6.2 %collective-permute-start = (bf16[256,256]{1,0:T(8,128)(2,1)S(1)}, bf16[256,256]{1,0:T(8,128)(2,1)S(1)}, u32[]{:S(2)}, u32[]{:S(2)}) collective-permute-start(bf16[256,256]{1,0:T(8,128)(2,1)S(1)} %get-tuple-element.58.refs_2_.refs_8_), channel_id=1, source_target_pairs={{0,1},{1,0},{2,3},{3,2},{4,5},{5,4},{6,7},{7,6},{8,9},{9,8},{10,11... | collective-permute-start | bytes 393224 | tf_op jit(solution)/shard_map/ppermute | solution.py:95
  37.9 27.5 %collective-permute-start.3 = (bf16[256,2048]{1,0:T(8,128)(2,1)S(1)}, bf16[256,2048]{1,0:T(8,128)(2,1)S(1)}, u32[]{:S(2)}, u32[]{:S(2)}) collective-permute-start(bf16[256,2048]{1,0:T(8,128)(2,1)S(1)} %get-tuple-element.60.refs_2_), channel_id=1, source_target_pairs={{0,16},{16,0},{1,17},{17,1},{2,18},{18,2},{3,19},{19,3},{4,20},{20... | collective-permute-start | bytes 3145736 | tf_op jit(solution)/shard_map/ppermute | solution.py:95
  40.2 15.1 %collective-permute-start.4 = (bf16[256,1024]{1,0:T(8,128)(2,1)}, bf16[256,1024]{1,0:T(8,128)(2,1)}, u32[]{:S(2)}, u32[]{:S(2)}) collective-permute-start(bf16[256,1024]{1,0:T(8,128)(2,1)} %get-tuple-element.62), channel_id=1, source_target_pairs={{0,2},{1,3},{2,0},{3,1},{4,6},{5,7},{6,4},{7,5},{8,10},{9,11},{10,... | collective-permute-start | bytes 1572872 | tf_op jit(solution)/shard_map/ppermute | solution.py:95
  41.8 23.6 %collective-permute-start.5 = (bf16[256,1024]{1,0:T(8,128)(2,1)}, bf16[256,1024]{1,0:T(8,128)(2,1)}, u32[]{:S(2)}, u32[]{:S(2)}) collective-permute-start(bf16[256,1024]{1,0:T(8,128)(2,1)} %get-tuple-element.61.refs_2_.refs_6_), channel_id=1, source_target_pairs={{0,2},{1,3},{2,0},{3,1},{4,6},{5,7},{6,4},{7,5},{8,10},{9,11},{10,... | collective-permute-start | bytes 1572872 | tf_op jit(solution)/shard_map/ppermute | solution.py:95
  42.3 23.1 %copy-start.22 = (bf16[256,1,2048]{2,0,1:T(8,128)(2,1)S(1)}, bf16[256,1,2048]{2,0,1:T(8,128)(2,1)}, u32[]{:S(2)}) copy-start(bf16[256,1,2048]{2,0,1:T(8,128)(2,1)} %param.11) | copy-start | bytes 3145732
  42.3 23.1 %copy-start.59 = (f32[2048]{0:T(1024)S(1)}, f32[2048]{0:T(1024)}, u32[]{:S(2)}) copy-start(f32[2048]{0:T(1024)} %param.18) | copy-start | bytes 24580
  66.7 56.4 %copy-start.98 = (bf16[256,1024]{1,0:T(8,128)(2,1)}, bf16[256,1024]{1,0:T(8,128)(2,1)S(1)}, u32[]{:S(2)}) copy-start(bf16[256,1024]{1,0:T(8,128)(2,1)S(1)} %get-tuple-element.68.refs_6_.refs_0_) | copy-start | bytes 1572868
  66.7 13.6 %collective-permute-start.6 = (bf16[256,1024]{1,0:T(8,128)(2,1)S(1)}, bf16[256,1024]{1,0:T(8,128)(2,1)S(1)}, u32[]{:S(2)}, u32[]{:S(2)}) collective-permute-start(bf16[256,1024]{1,0:T(8,128)(2,1)S(1)} %get-tuple-element.69), channel_id=1, source_target_pairs={{0,2},{1,3},{2,0},{3,1},{4,6},{5,7},{6,4},{7,5},{8,10},{9,11},{10,... | collective-permute-start | bytes 1572872 | tf_op jit(solution)/shard_map/ppermute | solution.py:95
  77.2 17.8 %copy-start.31 = (bf16[256,1280]{1,0:T(8,128)(2,1)}, bf16[256,1280]{1,0:T(8,128)(2,1)S(1)}, u32[]{:S(2)}) copy-start(bf16[256,1280]{1,0:T(8,128)(2,1)S(1)} %get-tuple-element.66.refs_5_.refs_2_.refs_0_) | copy-start | bytes 1966084
  77.2 17.7 %collective-permute-start.7 = (bf16[256,1280]{1,0:T(8,128)(2,1)S(1)}, bf16[256,1280]{1,0:T(8,128)(2,1)S(1)}, u32[]{:S(2)}, u32[]{:S(2)}) collective-permute-start(bf16[256,1280]{1,0:T(8,128)(2,1)S(1)} %get-tuple-element.66.refs_5_.refs_2_.refs_0_), channel_id=1, source_target_pairs={{0,2},{1,3},{2,0},{3,1},{4,6},{5,7},{6,4},{7,5},{8,10},{9,11},{10,... | collective-permute-start | bytes 1966088 | tf_op jit(solution)/shard_map/ppermute | solution.py:95
  78.1 44.9 %collective-permute-start.12 = (bf16[256,2560]{1,0:T(8,128)(2,1)S(1)}, bf16[256,2560]{1,0:T(8,128)(2,1)S(1)}, u32[]{:S(2)}, u32[]{:S(2)}) collective-permute-start(bf16[256,2560]{1,0:T(8,128)(2,1)S(1)} %get-tuple-element.67.refs_0_.refs_2_), channel_id=1, source_target_pairs={{0,2},{1,3},{2,0},{3,1},{4,6},{5,7},{6,4},{7,5},{8,10},{9,11},{10,... | collective-permute-start | bytes 3932168 | tf_op jit(solution)/shard_map/ppermute | solution.py:95
  80.3 42.7 %copy-start.39 = (bf16[256,1024]{1,0:T(8,128)(2,1)}, bf16[256,1024]{1,0:T(8,128)(2,1)S(1)}, u32[]{:S(2)}) copy-start(bf16[256,1024]{1,0:T(8,128)(2,1)S(1)} %collective-permute-done.6.refs_7_.refs_1_) | copy-start | bytes 1572868
  98.6 21.5 %copy-start.73 = (bf16[4,1280,128]{2,1,0:T(8,128)(2,1)}, bf16[4,1280,128]{2,1,0:T(8,128)(2,1)S(1)}, u32[]{:S(2)}) copy-start(bf16[4,1280,128]{2,1,0:T(8,128)(2,1)S(1)} %get-tuple-element.72.refs_5_.refs_1_) | copy-start | bytes 3932164
  98.6 9.5 %collective-permute-start.9 = (bf16[4,1280,128]{2,1,0:T(8,128)(2,1)S(1)}, bf16[4,1280,128]{2,1,0:T(8,128)(2,1)S(1)}, u32[]{:S(2)}, u32[]{:S(2)}) collective-permute-start(bf16[4,1280,128]{2,1,0:T(8,128)(2,1)S(1)} %get-tuple-element.74), channel_id=1, source_target_pairs={{0,1},{1,0},{2,3},{3,2},{4,5},{5,4},{6,7},{7,6},{8,9},{9,8},{10,11... | collective-permute-start | bytes 3932168 | tf_op jit(solution)/shard_map/ppermute | solution.py:95
  106.4 49.3 %collective-permute-start.8 = (bf16[256,1536]{1,0:T(8,128)(2,1)}, bf16[256,1536]{1,0:T(8,128)(2,1)}, u32[]{:S(2)}, u32[]{:S(2)}) collective-permute-start(bf16[256,1536]{1,0:T(8,128)(2,1)} %get-tuple-element.73.refs_2_.refs_1_), channel_id=1, source_target_pairs={{0,2},{1,3},{2,0},{3,1},{4,6},{5,7},{6,4},{7,5},{8,10},{9,11},{10,... | collective-permute-start | bytes 2359304 | tf_op jit(solution)/shard_map/ppermute | solution.py:95
  108.2 11.9 %collective-permute-start.10 = (bf16[1,1280,128]{2,1,0:T(8,128)(2,1)S(1)}, bf16[1,1280,128]{2,1,0:T(8,128)(2,1)S(1)}, u32[]{:S(2)}, u32[]{:S(2)}) collective-permute-start(bf16[1,1280,128]{2,1,0:T(8,128)(2,1)S(1)} %shard_map.204.refs_5_), channel_id=1, source_target_pairs={{0,4},{4,8},{8,12},{12,0},{1,5},{5,9},{9,13},{13,1},{2,6},{6,10},{... | collective-permute-start | bytes 983048 | tf_op jit(solution)/shard_map/ppermute | solution.py:368
  119.1 24.9 %collective-permute-start.14 = (bf16[256,2048]{1,0:T(8,128)(2,1)}, bf16[256,2048]{1,0:T(8,128)(2,1)}, u32[]{:S(2)}, u32[]{:S(2)}) collective-permute-start(bf16[256,2048]{1,0:T(8,128)(2,1)} %get-tuple-element.77.refs_4_.refs_2_), channel_id=1, source_target_pairs={{0,16},{16,0},{1,17},{17,1},{2,18},{18,2},{3,19},{19,3},{4,20},{20... | collective-permute-start | bytes 3145736 | tf_op jit(solution)/shard_map/ppermute | solution.py:95
  119.6 83.2 %collective-permute-start.21 = (bf16[256,3072]{1,0:T(8,128)(2,1)S(1)}, bf16[256,3072]{1,0:T(8,128)(2,1)S(1)}, u32[]{:S(2)}, u32[]{:S(2)}) collective-permute-start(bf16[256,3072]{1,0:T(8,128)(2,1)S(1)} %get-tuple-element.89.refs_2_), channel_id=1, source_target_pairs={{0,2},{1,3},{2,0},{3,1},{4,6},{5,7},{6,4},{7,5},{8,10},{9,11},{10,... | collective-permute-start | bytes 4718600 | tf_op jit(solution)/shard_map/ppermute | solution.py:95
  120.3 10.6 %collective-permute-start.11 = (bf16[1,1280,128]{2,1,0:T(8,128)(2,1)S(1)}, bf16[1,1280,128]{2,1,0:T(8,128)(2,1)}, u32[]{:S(2)}, u32[]{:S(2)}) collective-permute-start(bf16[1,1280,128]{2,1,0:T(8,128)(2,1)S(1)} %shard_map.206.refs_4_), channel_id=1, source_target_pairs={{0,4},{4,8},{8,12},{12,0},{1,5},{5,9},{9,13},{13,1},{2,6},{6,10},{... | collective-permute-start | bytes 983048 | tf_op jit(solution)/shard_map/ppermute | solution.py:368
  129.9 212.2 %reduce-scatter.5.cloned.1.call-start = ((), (), s32[]{:S(2)}) async-start(), calls=%async_computation.3 | async-start | bytes 7077888 | tf_op jit(solution)/shard_map/reduce_scatter | solution.py:273
  137.3 18.2 %copy-start.18 = (bf16[4,1280,128]{2,1,0:T(8,128)(2,1)S(1)}, bf16[4,1280,128]{2,1,0:T(8,128)(2,1)}, u32[]{:S(2)}) copy-start(bf16[4,1280,128]{2,1,0:T(8,128)(2,1)} %copy-done.16) | copy-start | bytes 3932164
  137.3 18.2 %copy-start.75 = (bf16[4,1280,128]{2,1,0:T(8,128)(2,1)S(1)}, bf16[4,1280,128]{2,1,0:T(8,128)(2,1)}, u32[]{:S(2)}) copy-start(bf16[4,1280,128]{2,1,0:T(8,128)(2,1)} %copy-done.73) | copy-start | bytes 3932164
  137.3 18.2 %collective-permute-start.13 = (bf16[1,1280,128]{2,1,0:T(8,128)(2,1)S(1)}, bf16[1,1280,128]{2,1,0:T(8,128)(2,1)S(1)}, u32[]{:S(2)}, u32[]{:S(2)}) collective-permute-start(bf16[1,1280,128]{2,1,0:T(8,128)(2,1)S(1)} %shard_map.208.refs_6_), channel_id=1, source_target_pairs={{0,4},{4,8},{8,12},{12,0},{1,5},{5,9},{9,13},{13,1},{2,6},{6,10},{... | collective-permute-start | bytes 983048 | tf_op jit(solution)/shard_map/ppermute | solution.py:368
  148.8 71.0 %collective-permute-start.25 = (bf16[256,1024]{1,0:T(8,128)(2,1)}, bf16[256,1024]{1,0:T(8,128)(2,1)}, u32[]{:S(2)}, u32[]{:S(2)}) collective-permute-start(bf16[256,1024]{1,0:T(8,128)(2,1)} %get-tuple-element.91), channel_id=1, source_target_pairs={{0,2},{1,3},{2,0},{3,1},{4,6},{5,7},{6,4},{7,5},{8,10},{9,11},{10,... | collective-permute-start | bytes 1572872 | tf_op jit(solution)/shard_map/ppermute | solution.py:95
  161.1 40.9 %copy-start.78 = (bf16[4,1536,128]{2,1,0:T(8,128)(2,1)}, bf16[4,1536,128]{2,1,0:T(8,128)(2,1)S(1)}, u32[]{:S(2)}) copy-start(bf16[4,1536,128]{2,1,0:T(8,128)(2,1)S(1)} %get-tuple-element.79.refs_12_.refs_1_) | copy-start | bytes 4718596
  161.1 18.8 %collective-permute-start.15 = (bf16[4,1536,128]{2,1,0:T(8,128)(2,1)S(1)}, bf16[4,1536,128]{2,1,0:T(8,128)(2,1)S(1)}, u32[]{:S(2)}, u32[]{:S(2)}) collective-permute-start(bf16[4,1536,128]{2,1,0:T(8,128)(2,1)S(1)} %get-tuple-element.80), channel_id=1, source_target_pairs={{0,1},{1,0},{2,3},{3,2},{4,5},{5,4},{6,7},{7,6},{8,9},{9,8},{10,11... | collective-permute-start | bytes 4718600 | tf_op jit(solution)/shard_map/ppermute | solution.py:95
  177.9 30.9 %copy-start.41 = (bf16[256,1024]{1,0:T(8,128)(2,1)}, bf16[256,1024]{1,0:T(8,128)(2,1)S(1)}, u32[]{:S(2)}) copy-start(bf16[256,1024]{1,0:T(8,128)(2,1)S(1)} %get-tuple-element.83.refs_3_.refs_0_.refs_2_) | copy-start | bytes 1572868
  177.9 30.7 %collective-permute-start.18 = (bf16[256,256]{1,0:T(8,128)(2,1)S(1)}, bf16[256,256]{1,0:T(8,128)(2,1)S(1)}, u32[]{:S(2)}, u32[]{:S(2)}) collective-permute-start(bf16[256,256]{1,0:T(8,128)(2,1)S(1)} %get-tuple-element.86), channel_id=1, source_target_pairs={{0,1},{1,0},{2,3},{3,2},{4,5},{5,4},{6,7},{7,6},{8,9},{9,8},{10,11... | collective-permute-start | bytes 393224 | tf_op jit(solution)/shard_map/ppermute | solution.py:95
  178.3 30.3 %collective-permute-start.19 = (bf16[256,256]{1,0:T(8,128)(2,1)S(1)}, bf16[256,256]{1,0:T(8,128)(2,1)S(1)}, u32[]{:S(2)}, u32[]{:S(2)}) collective-permute-start(bf16[256,256]{1,0:T(8,128)(2,1)S(1)} %get-tuple-element.87), channel_id=1, source_target_pairs={{0,2},{1,3},{2,0},{3,1},{4,6},{5,7},{6,4},{7,5},{8,10},{9,11},{10,... | collective-permute-start | bytes 393224 | tf_op jit(solution)/shard_map/ppermute | solution.py:95
  179.9 22.1 %copy-start.14 = (bf16[4,1536,128]{2,1,0:T(8,128)(2,1)}, bf16[4,1536,128]{2,1,0:T(8,128)(2,1)S(1)}, u32[]{:S(2)}) copy-start(bf16[4,1536,128]{2,1,0:T(8,128)(2,1)S(1)} %collective-permute-done.15.refs_2_) | copy-start | bytes 4718596
  180.0 22.0 %collective-permute-start.22 = (bf16[1,1536,128]{2,1,0:T(8,128)(2,1)S(1)}, bf16[1,1536,128]{2,1,0:T(8,128)(2,1)S(1)}, u32[]{:S(2)}, u32[]{:S(2)}) collective-permute-start(bf16[1,1536,128]{2,1,0:T(8,128)(2,1)S(1)} %shard_map.213.refs_3_), channel_id=1, source_target_pairs={{0,4},{4,8},{8,12},{12,0},{1,5},{5,9},{9,13},{13,1},{2,6},{6,10},{... | collective-permute-start | bytes 1179656 | tf_op jit(solution)/shard_map/ppermute | solution.py:368
  202.0 6.6 %collective-permute-start.20 = (bf16[256,256]{1,0:T(8,128)(2,1)S(1)}, bf16[256,256]{1,0:T(8,128)(2,1)S(1)}, u32[]{:S(2)}, u32[]{:S(2)}) collective-permute-start(bf16[256,256]{1,0:T(8,128)(2,1)S(1)} %get-tuple-element.88), channel_id=1, source_target_pairs={{0,3},{1,2},{2,1},{3,0},{4,7},{5,6},{6,5},{7,4},{8,11},{9,10},{10,... | collective-permute-start | bytes 393224 | tf_op jit(solution)/shard_map/ppermute | solution.py:95
  202.9 13.7 %collective-permute-start.26 = (bf16[1,1536,128]{2,1,0:T(8,128)(2,1)}, bf16[1,1536,128]{2,1,0:T(8,128)(2,1)}, u32[]{:S(2)}, u32[]{:S(2)}) collective-permute-start(bf16[1,1536,128]{2,1,0:T(8,128)(2,1)} %shard_map.215.refs_4_), channel_id=1, source_target_pairs={{0,4},{4,8},{8,12},{12,0},{1,5},{5,9},{9,13},{13,1},{2,6},{6,10},{... | collective-permute-start | bytes 1179656 | tf_op jit(solution)/shard_map/ppermute | solution.py:368
  219.8 25.2 %copy-start.80 = (bf16[4,1536,128]{2,1,0:T(8,128)(2,1)S(1)}, bf16[4,1536,128]{2,1,0:T(8,128)(2,1)}, u32[]{:S(2)}) copy-start(bf16[4,1536,128]{2,1,0:T(8,128)(2,1)} %copy-done.78) | copy-start | bytes 4718596
  222.8 22.3 %copy-start.81 = (bf16[4,1024,128]{2,1,0:T(8,128)(2,1)}, bf16[4,1024,128]{2,1,0:T(8,128)(2,1)S(1)}, u32[]{:S(2)}) copy-start(bf16[4,1024,128]{2,1,0:T(8,128)(2,1)S(1)} %get-tuple-element.92.refs_4_.refs_1_) | copy-start | bytes 3145732
  222.8 22.3 %collective-permute-start.27 = (bf16[4,1024,128]{2,1,0:T(8,128)(2,1)S(1)}, bf16[4,1024,128]{2,1,0:T(8,128)(2,1)S(1)}, u32[]{:S(2)}, u32[]{:S(2)}) collective-permute-start(bf16[4,1024,128]{2,1,0:T(8,128)(2,1)S(1)} %get-tuple-element.93), channel_id=1, source_target_pairs={{0,1},{1,0},{2,3},{3,2},{4,5},{5,4},{6,7},{7,6},{8,9},{9,8},{10,11... | collective-permute-start | bytes 3145736 | tf_op jit(solution)/shard_map/ppermute | solution.py:95
  223.2 21.7 %collective-permute-start.28 = (bf16[1,1536,128]{2,1,0:T(8,128)(2,1)S(1)}, bf16[1,1536,128]{2,1,0:T(8,128)(2,1)S(1)}, u32[]{:S(2)}, u32[]{:S(2)}) collective-permute-start(bf16[1,1536,128]{2,1,0:T(8,128)(2,1)S(1)} %shard_map.219.refs_4_), channel_id=1, source_target_pairs={{0,4},{4,8},{8,12},{12,0},{1,5},{5,9},{9,13},{13,1},{2,6},{6,10},{... | collective-permute-start | bytes 1179656 | tf_op jit(solution)/shard_map/ppermute | solution.py:368
  223.2 22.9 %collective-permute-start.17 = (bf16[256,1024]{1,0:T(8,128)(2,1)S(1)}, bf16[256,1024]{1,0:T(8,128)(2,1)S(1)}, u32[]{:S(2)}, u32[]{:S(2)}) collective-permute-start(bf16[256,1024]{1,0:T(8,128)(2,1)S(1)} %copy-done.38), channel_id=1, source_target_pairs={{0,2},{1,3},{2,0},{3,1},{4,6},{5,7},{6,4},{7,5},{8,10},{9,11},{10,... | collective-permute-start | bytes 1572872 | tf_op jit(solution)/shard_map/ppermute | solution.py:95
  224.8 23.6 %collective-permute-start.24 = (bf16[256,1024]{1,0:T(8,128)(2,1)S(1)}, bf16[256,1024]{1,0:T(8,128)(2,1)S(1)}, u32[]{:S(2)}, u32[]{:S(2)}) collective-permute-start(bf16[256,1024]{1,0:T(8,128)(2,1)S(1)} %copy-done.42), channel_id=1, source_target_pairs={{0,2},{1,3},{2,0},{3,1},{4,6},{5,7},{6,4},{7,5},{8,10},{9,11},{10,... | collective-permute-start | bytes 1572872 | tf_op jit(solution)/shard_map/ppermute | solution.py:95
  246.1 22.5 %copy-start.27 = (bf16[4,1024,128]{2,1,0:T(8,128)(2,1)S(1)}, bf16[4,1024,128]{2,1,0:T(8,128)(2,1)}, u32[]{:S(2)}) copy-start(bf16[4,1024,128]{2,1,0:T(8,128)(2,1)} %copy-done.26) | copy-start | bytes 3145732
  252.1 19.1 %collective-permute-start.29 = (bf16[4,128,1024]{2,1,0:T(8,128)(2,1)}, bf16[4,128,1024]{2,1,0:T(8,128)(2,1)}, u32[]{:S(2)}, u32[]{:S(2)}) collective-permute-start(bf16[4,128,1024]{2,1,0:T(8,128)(2,1)} %bitcast.10), channel_id=1, source_target_pairs={{0,1},{1,0},{2,3},{3,2},{4,5},{5,4},{6,7},{7,6},{8,9},{9,8},{10,11... | collective-permute-start | bytes 3145736 | tf_op jit(solution)/shard_map/ppermute | solution.py:95
  252.1 16.5 %collective-permute-start.30 = (bf16[1,1024,128]{2,1,0:T(8,128)(2,1)S(1)}, bf16[1,1024,128]{2,1,0:T(8,128)(2,1)S(1)}, u32[]{:S(2)}, u32[]{:S(2)}) collective-permute-start(bf16[1,1024,128]{2,1,0:T(8,128)(2,1)S(1)} %shard_map.222.refs_4_), channel_id=1, source_target_pairs={{0,4},{4,8},{8,12},{12,0},{1,5},{5,9},{9,13},{13,1},{2,6},{6,10},{... | collective-permute-start | bytes 786440 | tf_op jit(solution)/shard_map/ppermute | solution.py:368
  252.1 21.5 %collective-permute-start.23 = (bf16[256,256]{1,0:T(8,128)(2,1)S(1)}, bf16[256,256]{1,0:T(8,128)(2,1)S(1)}, u32[]{:S(2)}, u32[]{:S(2)}) collective-permute-start(bf16[256,256]{1,0:T(8,128)(2,1)S(1)} %shard_map.217.refs_1_.refs_5_.refs_2_), channel_id=1, source_target_pairs={{0,2},{1,3},{2,0},{3,1},{4,6},{5,7},{6,4},{7,5},{8,10},{9,11},{10,... | collective-permute-start | bytes 393224 | tf_op jit(solution)/shard_map/ppermute | solution.py:95
  253.7 25.3 %collective-permute-start.32 = (bf16[256,2048]{1,0:T(8,128)(2,1)S(1)}, bf16[256,2048]{1,0:T(8,128)(2,1)S(1)}, u32[]{:S(2)}, u32[]{:S(2)}) collective-permute-start(bf16[256,2048]{1,0:T(8,128)(2,1)S(1)} %shard_map.218.refs_4_.refs_0_), channel_id=1, source_target_pairs={{0,16},{16,0},{1,17},{17,1},{2,18},{18,2},{3,19},{19,3},{4,20},{20... | collective-permute-start | bytes 3145736 | tf_op jit(solution)/shard_map/ppermute | solution.py:95
  282.1 18.6 %copy-start.72 = (bf16[512,256]{1,0:T(8,128)(2,1)S(1)}, bf16[512,256]{1,0:T(8,128)(2,1)}, u32[]{:S(2)}) copy-start(bf16[512,256]{1,0:T(8,128)(2,1)} %copy-done.71) | copy-start | bytes 786436
  285.6 3.8 %collective-permute-start.40 = (f32[2,4,128]{2,1,0:T(4,128)}, f32[2,4,128]{2,1,0:T(4,128)S(1)}, u32[]{:S(2)}, u32[]{:S(2)}) collective-permute-start(f32[2,4,128]{2,1,0:T(4,128)} %bitcast.17), channel_id=1, source_target_pairs={{0,2},{1,3},{2,0},{3,1},{4,6},{5,7},{6,4},{7,5},{8,10},{9,11},{10,... | collective-permute-start | bytes 12296 | tf_op jit(solution)/shard_map/ppermute | solution.py:95
  286.0 3.4 collective-permute-start.39
  286.0 3.4 collective-permute-start.41
  287.7 40.6 %collective-permute-start.16 = (bf16[256,2048]{1,0:T(8,128)(2,1)S(1)}, bf16[256,2048]{1,0:T(8,128)(2,1)S(1)}, u32[]{:S(2)}, u32[]{:S(2)}) collective-permute-start(bf16[256,2048]{1,0:T(8,128)(2,1)S(1)} %copy-done.25), channel_id=1, source_target_pairs={{0,16},{16,0},{1,17},{17,1},{2,18},{18,2},{3,19},{19,3},{4,20},{20... | collective-permute-start | bytes 3145736 | tf_op jit(solution)/shard_map/ppermute | solution.py:95
  290.1 8.5 %collective-permute-start.44 = (f32[2,128]{1,0:T(2,128)S(1)}, f32[2,128]{1,0:T(2,128)S(1)}, u32[]{:S(2)}, u32[]{:S(2)}) collective-permute-start(f32[2,128]{1,0:T(2,128)S(1)} %bitcast.84), channel_id=1, source_target_pairs={{0,12},{4,8},{8,4},{12,0},{1,13},{5,9},{9,5},{13,1},{2,14},{6,10},... | collective-permute-start | bytes 3080 | tf_op jit(solution)/shard_map/ppermute | solution.py:95
  293.7 5.5 %collective-permute-start.42 = (f32[2,128]{1,0:T(2,128)S(1)}, f32[2,128]{1,0:T(2,128)S(1)}, u32[]{:S(2)}, u32[]{:S(2)}) collective-permute-start(f32[2,128]{1,0:T(2,128)S(1)} %bitcast.83), channel_id=1, source_target_pairs={{0,4},{4,0},{8,12},{12,8},{1,5},{5,1},{9,13},{13,9},{2,6},{6,2},{1... | collective-permute-start | bytes 3080 | tf_op jit(solution)/shard_map/ppermute | solution.py:95
  294.5 4.7 %collective-permute-start.43 = (f32[2,128]{1,0:T(2,128)S(1)}, f32[2,128]{1,0:T(2,128)S(1)}, u32[]{:S(2)}, u32[]{:S(2)}) collective-permute-start(f32[2,128]{1,0:T(2,128)S(1)} %bitcast.82), channel_id=1, source_target_pairs={{0,8},{4,12},{8,0},{12,4},{1,9},{5,13},{9,1},{13,5},{2,10},{6,14},... | collective-permute-start | bytes 3080 | tf_op jit(solution)/shard_map/ppermute | solution.py:95
  296.6 10.9 %collective-permute-start.35 = (bf16[1,1024,128]{2,1,0:T(8,128)(2,1)S(1)}, bf16[1,1024,128]{2,1,0:T(8,128)(2,1)S(1)}, u32[]{:S(2)}, u32[]{:S(2)}) collective-permute-start(bf16[1,1024,128]{2,1,0:T(8,128)(2,1)S(1)} %copy-done.48), channel_id=1, source_target_pairs={{0,4},{4,8},{8,12},{12,0},{1,5},{5,9},{9,13},{13,1},{2,6},{6,10},{... | collective-permute-start | bytes 786440 | tf_op jit(solution)/shard_map/ppermute | solution.py:368
  298.6 14.5 %collective-permute-start.34 = (bf16[1,128,1024]{2,1,0:T(8,128)(2,1)S(1)}, bf16[1,128,1024]{2,1,0:T(8,128)(2,1)S(1)}, u32[]{:S(2)}, u32[]{:S(2)}) collective-permute-start(bf16[1,128,1024]{2,1,0:T(8,128)(2,1)S(1)} %copy-done.46), channel_id=1, source_target_pairs={{0,4},{4,8},{8,12},{12,0},{1,5},{5,9},{9,13},{13,1},{2,6},{6,10},{... | collective-permute-start | bytes 786440 | tf_op jit(solution)/shard_map/ppermute | solution.py:368
  299.2 1.5 collective-permute-start.31
  300.8 13.8 %collective-permute-start.33 = (bf16[1,128,256]{2,1,0:T(8,128)(2,1)S(1)}, bf16[1,128,256]{2,1,0:T(8,128)(2,1)S(1)}, u32[]{:S(2)}, u32[]{:S(2)}) collective-permute-start(bf16[1,128,256]{2,1,0:T(8,128)(2,1)S(1)} %shard_map.228.refs_4_), channel_id=1, source_target_pairs={{0,4},{4,8},{8,12},{12,0},{1,5},{5,9},{9,13},{13,1},{2,6},{6,10},{... | collective-permute-start | bytes 196616 | tf_op jit(solution)/shard_map/ppermute | solution.py:368
  307.7 12.5 %collective-permute-start.38 = (bf16[1,1024,128]{2,1,0:T(8,128)(2,1)S(1)}, bf16[1,1024,128]{2,1,0:T(8,128)(2,1)S(1)}, u32[]{:S(2)}, u32[]{:S(2)}) collective-permute-start(bf16[1,1024,128]{2,1,0:T(8,128)(2,1)S(1)} %shard_map.229.refs_4_), channel_id=1, source_target_pairs={{0,4},{4,8},{8,12},{12,0},{1,5},{5,9},{9,13},{13,1},{2,6},{6,10},{... | collective-permute-start | bytes 786440 | tf_op jit(solution)/shard_map/ppermute | solution.py:368
  314.2 11.5 %collective-permute-start.37 = (bf16[1,128,1024]{2,1,0:T(8,128)(2,1)S(1)}, bf16[1,128,1024]{2,1,0:T(8,128)(2,1)S(1)}, u32[]{:S(2)}, u32[]{:S(2)}) collective-permute-start(bf16[1,128,1024]{2,1,0:T(8,128)(2,1)S(1)} %shard_map.230.refs_4_), channel_id=1, source_target_pairs={{0,4},{4,8},{8,12},{12,0},{1,5},{5,9},{9,13},{13,1},{2,6},{6,10},{... | collective-permute-start | bytes 786440 | tf_op jit(solution)/shard_map/ppermute | solution.py:368
  314.6 13.3 %collective-permute-start.36 = (bf16[1,128,256]{2,1,0:T(8,128)(2,1)S(1)}, bf16[1,128,256]{2,1,0:T(8,128)(2,1)S(1)}, u32[]{:S(2)}, u32[]{:S(2)}) collective-permute-start(bf16[1,128,256]{2,1,0:T(8,128)(2,1)S(1)} %shard_map.231.refs_4_), channel_id=1, source_target_pairs={{0,4},{4,8},{8,12},{12,0},{1,5},{5,9},{9,13},{13,1},{2,6},{6,10},{... | collective-permute-start | bytes 196616 | tf_op jit(solution)/shard_map/ppermute | solution.py:368
  327.9 9.4 %collective-permute-start.45 = (bf16[1,128,1024]{2,1,0:T(8,128)(2,1)S(1)}, bf16[1,128,1024]{2,1,0:T(8,128)(2,1)S(1)}, u32[]{:S(2)}, u32[]{:S(2)}) collective-permute-start(bf16[1,128,1024]{2,1,0:T(8,128)(2,1)S(1)} %shard_map.233.refs_4_), channel_id=1, source_target_pairs={{0,4},{4,8},{8,12},{12,0},{1,5},{5,9},{9,13},{13,1},{2,6},{6,10},{... | collective-permute-start | bytes 786440 | tf_op jit(solution)/shard_map/ppermute | solution.py:368
  328.0 12.4 %collective-permute-start.46 = (bf16[1,128,256]{2,1,0:T(8,128)(2,1)S(1)}, bf16[1,128,256]{2,1,0:T(8,128)(2,1)S(1)}, u32[]{:S(2)}, u32[]{:S(2)}) collective-permute-start(bf16[1,128,256]{2,1,0:T(8,128)(2,1)S(1)} %shard_map.234.refs_3_), channel_id=1, source_target_pairs={{0,4},{4,8},{8,12},{12,0},{1,5},{5,9},{9,13},{13,1},{2,6},{6,10},{... | collective-permute-start | bytes 196616 | tf_op jit(solution)/shard_map/ppermute | solution.py:368
  (87 other events, 480.1 us)
Sparse Core Ops, SparseCore 0:
  130.0 75.4 reduce-scatter.2
  215.8 84.9 reduce-scatter.4

commit v3 on v2

--- a/solution.py
+++ b/solution.py
@@ -19,6 +19,14 @@
 BF16 = jnp.bfloat16
 MIB = 1024 * 1024
 WEIGHT = 3.0
+ORDER = (
+    "feed_one", "feed_two", "down_one", "feed_back_one", "D1", "feed_back_two", "D1", "both_one",
+    "D1", "middle", "D1", "down_two", "heads_back", "D2", "both_two", "mixing", "D2", "kv_total",
+    "first_back", "D2", "out_product", "D2", "O", "query_product", "O", "Q", "kv_product", "last",
+    "K", "O", "Q", "K", "O", "Q", "K", "output", "deal", "K", "Q",
+)
+RINGS = ("D1", "D2", "O", "Q", "K")
+HELD = {"h2": ("feed_back_one",), "g2": ("feed_back_one", "feed_back_two")}
 
 
 def dot_nn(a, b):
@@ -57,7 +65,7 @@
         scalars=0,
         after=(),
         carry=(),
-        vmem=40,
+        vmem=32,
         us=1.0,
     ):
         waits = list(carry) + self.last + list(after)
@@ -879,7 +887,6 @@
         us=2.0,
         out_specs=[whole(flat)] * 2 + share_specs,
         scalars=1,
-        after=attn_pieces,
     )
     two_cols = exchange_chips(shares_of(normed_two, two_shares, by_core=True))
 
@@ -888,137 +895,221 @@
     cut = blocks * 5 // 11
     weights = (gate_weight, up_weight)
     feed = partial(feed_part, chain, normed_two, cot, *weights, down_weight)
-    hidden_one, both_one = feed(0, cut, block)
-    hidden_one_pieces, both_one_pieces = gather_chips(hidden_one), gather_chips(both_one)
-    hidden_two, both_two = feed(cut, blocks - cut, block, after=two_cols)
-    down_one = Ring(chain, *column_products(chain, hidden_one_pieces, cot_cols))
-    d_two, hidden_two, both_two = feed_back(
-        chain,
+    v = {"h1": None}
+
+    def held(name, kernel):
+        return [v[name]] if name in v and kernel in HELD[name] else []
+
+    def feed_one():
+        v["h1"], v["g1"] = feed(0, cut, block)
+        v["h1s"], v["g1s"] = gather_chips(v["h1"]), gather_chips(v["g1"])
+
+    def feed_two():
+        v["h2"], v["g2"] = feed(cut, blocks - cut, block, after=two_cols + attn_pieces)
+
+    def feed_back_one():
+        outs = feed_back(
+            chain,
+            v["g1"],
+            *weights,
+            0,
+            block,
+            [],
+            F32,
+            7.0,
+            carry=held("h2", "feed_back_one") + held("g2", "feed_back_one"),
+        )
+        release(outs, "feed_back_one")
+
+    def feed_back_two():
+        outs = feed_back(
+            chain,
+            v["g2"],
+            *weights,
+            cut,
+            block,
+            [v["d_two"]],
+            BF16,
+            8.0,
+            carry=held("h2", "feed_back_two") + held("g2", "feed_back_two"),
+        )
+        release(outs, "feed_back_two")
+        v["d_two_other"] = swap(v["d_two"], "tensor", 1)
+
+    def release(outs, kernel):
+        outs = list(outs) if isinstance(outs, (list, tuple)) else [outs]
+        v["d_two"] = outs.pop(0)
+        for name in ("h2", "g2"):
+            if held(name, kernel):
+                v[name] = outs.pop(0)
+
+    def pieces(name):
+        if name + "s" not in v:
+            v[name + "s"] = gather_chips(v[name])
+        return v[name + "s"]
+
+    def down_one():
+        v["D1"] = Ring(chain, *column_products(chain, pieces("h1"), cot_cols))
+
+    def down_two():
+        v["D2"] = Ring(chain, *column_products(chain, pieces("h2"), cot_cols))
+
+    def both_one():
+        v["both_one"] = row_scatter(chain, two_cols, pieces("g1"))
+
+    def both_two():
+        v["both_two"] = row_scatter(chain, two_cols, pieces("g2"))
+
+    def middle():
+        v["d_resid"], v["d_resid_b"], v["feed_gain_sum"], *resid_shares = chain(
+            second_back_kernel,
+            [shaped(flat, F32), shaped(flat, BF16), shaped(gain, F32)] + shares,
+            here,
+            cot,
+            v["d_two"],
+            v["d_two_other"],
+            resid,
+            feed_gain,
+            in_specs=[whole(flat)] * 4 + [whole(gain)],
+            us=4.0,
+            out_specs=[whole(flat)] * 2 + [whole(gain)] + share_specs,
+            scalars=1,
+        )
+        v["resid_cols"] = exchange_chips(shares_of(v["d_resid_b"], resid_shares))
+
+    def heads_back():
+        v["d_query"], d_kv_parts = attend_back(
+            chain, here, queries, attn_b, lse, v["d_resid_b"], output_matrix, tables, kv_pieces
+        )
+        v["d_kv_pieces"] = exchange_context(d_kv_parts)
+        v["d_querys"] = gather_chips(v["d_query"])
+
+    def kv_total():
+        received = v["d_kv_pieces"]
+        v["d_kv"] = chain(
+            partial(kv_total_kernel, len(received)),
+            shaped((tokens, 2 * kv_width), BF16),
+            *received,
+            *tables,
+            in_specs=[whole((tokens, 2 * kv_width))] * len(received) + [table] * 2,
+            out_specs=whole((tokens, 2 * kv_width)),
+        )
+        v["d_kvs"] = gather_chips(v["d_kv"])
+
+    def first_back():
+        row_block = pick_block(width, 512)
+        v["d_one"] = chain(
+            first_back_kernel,
+            shaped(flat, BF16),
+            v["d_query"],
+            v["d_kv"],
+            query_weight,
+            key_matrix,
+            value_matrix,
+            grid=(width // row_block,),
+            in_specs=[
+                whole((tokens, q_width)),
+                whole((tokens, 2 * kv_width)),
+                pl.BlockSpec((row_block, q_width), lambda j: (j, 0)),
+                pl.BlockSpec((row_block, kv_width), lambda j: (j, 0)),
+                pl.BlockSpec((row_block, kv_width), lambda j: (j, 0)),
+            ],
+            us=2.5,
+            out_specs=pl.BlockSpec((tokens, row_block), lambda j: (0, j)),
+        )
+        v["d_one_other"] = swap(v["d_one"], "tensor", 1)
+
+    def first_columns():
+        if "first_cols" not in v:
+            v["first_cols"] = exchange_chips(first_shares)
+        return v["first_cols"]
+
+    def out_product():
+        v["O"] = Ring(chain, *column_products(chain, attn_pieces, v["resid_cols"]))
+
+    def query_product():
+        v["Q"] = Ring(chain, *row_products(chain, first_columns(), v["d_querys"]))
+
+    def kv_product():
+        v["K"] = Ring(chain, *row_products(chain, first_columns(), v["d_kvs"]))
+
+    def mixing():
+        v["mixed"] = mix(chain, [v["h1"], v["h2"]], down_weight, block)
+        v["mixed_other"] = swap(v["mixed"], "tensor", 1)
+
+    def output():
+        v["layer_output"] = chain(
+            output_kernel,
+            shaped(flat, BF16),
+            resid,
+            v["mixed"],
+            v["mixed_other"],
+            in_specs=[whole(flat)] * 3,
+            us=2.0,
+            out_specs=whole(flat),
+        )
+
+    def last():
+        v["input_grad"], attn_gain_sum = chain(
+            last_kernel,
+            [shaped(flat, BF16), shaped(gain, F32)],
+            v["d_one"],
+            v["d_one_other"],
+            x,
+            attn_gain,
+            v["d_resid"],
+            in_specs=[whole(flat)] * 3 + [whole(gain), whole(flat)],
+            us=3.0,
+            out_specs=[whole(flat), whole(gain)],
+        )
+        gain_sums = jnp.concatenate([attn_gain_sum, v["feed_gain_sum"]], axis=0)
+        v["gains"] = scatter_gains(gain_sums)
+
+    def deal():
+        both = [v["both_one"], v["both_two"]]
+        share = both[0].shape[0]
+        v["gate_share"], v["up_share"] = chain(
+            partial(dealt_kernel, block),
+            [shaped((share, feed_width), F32)] * 2,
+            *both,
+            in_specs=[whole(b.shape) for b in both],
+            out_specs=[whole((share, feed_width))] * 2,
+        )
+
+    tasks = (
+        feed_one,
+        feed_two,
+        feed_back_one,
+        feed_back_two,
+        down_one,
+        down_two,
         both_one,
-        *weights,
-        0,
-        block,
-        [],
-        F32,
-        7.0,
-        carry=[hidden_two, both_two],
-    )
-    hidden_two_pieces = gather_chips(hidden_two)
-    down_one.step()
-    d_two, both_two = feed_back(
-        chain, both_two, *weights, cut, block, [d_two], BF16, 8.0, carry=[both_two]
-    )
-    both_two_pieces = gather_chips(both_two)
-    d_two_other = swap(d_two, "tensor", 1)
-    down_one.step()
-    both_one_share = row_scatter(chain, two_cols, both_one_pieces)
-    down_one.step()
-    d_resid, d_resid_b, feed_gain_sum, *resid_shares = chain(
-        second_back_kernel,
-        [shaped(flat, F32), shaped(flat, BF16), shaped(gain, F32)] + shares,
-        here,
-        cot,
-        d_two,
-        d_two_other,
-        resid,
-        feed_gain,
-        in_specs=[whole(flat)] * 4 + [whole(gain)],
-        us=4.0,
-        out_specs=[whole(flat)] * 2 + [whole(gain)] + share_specs,
-        scalars=1,
-    )
-    down_one.step()
-    down_two = Ring(chain, *column_products(chain, hidden_two_pieces, cot_cols))
-    d_query, d_kv_parts = attend_back(
-        chain, here, queries, attn_b, lse, d_resid_b, output_matrix, tables, kv_pieces
-    )
-    resid_cols = exchange_chips(shares_of(d_resid_b, resid_shares))
-    d_kv_pieces = exchange_context(d_kv_parts)
-    query_pieces = gather_chips(d_query)
-    down_two.step()
-    mixed = mix(chain, [hidden_one, hidden_two], down_weight, block)
-    down_two.step()
-    both_two_share = row_scatter(chain, two_cols, both_two_pieces)
-    d_kv = chain(
-        partial(kv_total_kernel, len(d_kv_pieces)),
-        shaped((tokens, 2 * kv_width), BF16),
-        *d_kv_pieces,
-        *tables,
-        in_specs=[whole((tokens, 2 * kv_width))] * len(d_kv_pieces) + [table] * 2,
-        out_specs=whole((tokens, 2 * kv_width)),
-    )
-    row_block = pick_block(width, 512)
-    d_one = chain(
-        first_back_kernel,
-        shaped(flat, BF16),
-        d_query,
-        d_kv,
-        query_weight,
-        key_matrix,
-        value_matrix,
-        grid=(width // row_block,),
-        in_specs=[
-            whole((tokens, q_width)),
-            whole((tokens, 2 * kv_width)),
-            pl.BlockSpec((row_block, q_width), lambda j: (j, 0)),
-            pl.BlockSpec((row_block, kv_width), lambda j: (j, 0)),
-            pl.BlockSpec((row_block, kv_width), lambda j: (j, 0)),
-        ],
-        us=2.5,
-        out_specs=pl.BlockSpec((tokens, row_block), lambda j: (0, j)),
-    )
-    d_one_other = swap(d_one, "tensor", 1)
-    kv_grad_pieces = gather_chips(d_kv)
-    first_cols = exchange_chips(first_shares)
-    down_two.step()
-    out_ring = Ring(chain, *column_products(chain, attn_pieces, resid_cols))
-    down_two.step()
-    out_ring.step()
-    query_ring = Ring(chain, *row_products(chain, first_cols, query_pieces))
-    out_ring.step()
-    query_ring.step()
-    kv_ring = Ring(chain, *row_products(chain, first_cols, kv_grad_pieces))
-    input_grad, attn_gain_sum = chain(
-        last_kernel,
-        [shaped(flat, BF16), shaped(gain, F32)],
-        d_one,
-        d_one_other,
-        x,
-        attn_gain,
-        d_resid,
-        in_specs=[whole(flat)] * 3 + [whole(gain), whole(flat)],
-        us=3.0,
-        out_specs=[whole(flat), whole(gain)],
-    )
-    mixed_other = swap(mixed, "tensor", 1)
-    gains = scatter_gains(jnp.concatenate([attn_gain_sum, feed_gain_sum], axis=0))
-    kv_ring.step()
-    out_ring.step()
-    query_ring.step()
-    kv_ring.step()
-    out_ring.step()
-    query_ring.step()
-    kv_ring.step()
-    layer_output = chain(
-        output_kernel,
-        shaped(flat, BF16),
-        resid,
-        mixed,
-        mixed_other,
-        in_specs=[whole(flat)] * 3,
-        us=2.0,
-        out_specs=whole(flat),
-    )
-    finish([down_one, down_two, out_ring, query_ring, kv_ring])
-    both = [both_one_share, both_two_share]
-    share = both[0].shape[0]
-    gate_share, up_share = chain(
-        partial(dealt_kernel, block),
-        [shaped((share, feed_width), F32)] * 2,
-        *both,
-        in_specs=[whole(b.shape) for b in both],
-        out_specs=[whole((share, feed_width))] * 2,
-    )
+        both_two,
+        middle,
+        heads_back,
+        kv_total,
+        first_back,
+        out_product,
+        query_product,
+        kv_product,
+        mixing,
+        output,
+        last,
+        deal,
+    )
+    by_name = {task.__name__: task for task in tasks}
+    for name in ORDER:
+        if name in by_name:
+            by_name[name]()
+        elif v[name].open:
+            v[name].step()
+    for name in RINGS:
+        while v[name].open:
+            v[name].step()
+    layer_output, input_grad, gains = v["layer_output"], v["input_grad"], v["gains"]
+    out_ring, query_ring, kv_ring = v["O"], v["Q"], v["K"]
+    gate_share, up_share = v["gate_share"], v["up_share"]
+    down_one, down_two = v["D1"], v["D2"]
 
     return (
         layer_output.reshape(block_shape),

time: 354 us -> 346 us (0.977)
  waiting for transfers between devices: 119 us -> 113 us
  Pallas kernels: 130 us -> 125 us
    unnamed x205 -> x233, local copies, waits for them, and re-layouts: 40.7 us -> 45.9 us
    ppermute x15, waiting for transfers between devices: 77.4 us -> 72.3 us  [step(): self.arrived = lax.ppermute(total, 'dp', ring)]
    pallas_call x45, Pallas kernels: 130 us -> 125 us  [__call__(): pl.pallas_call(stripped, out_shape=out_shape + [shaped(c.shape, c.dtype)...]
  transfers between devices with their start and end apart: 49 -> 49, of which waited for: 22 -> 22; matrix products, arithmetic and copies ran while one was open for 2% -> 1% of each run, Pallas kernels for 31% -> 32%
where the time goes in v3:
time: 346 us; the launch traced here: 344 us
  Pallas kernels  125 us (36%)
  waiting for transfers between devices  113 us (33%)
  local copies, waits for them, and re-layouts  47.1 us (14%)
  starting transfers between devices  41 us (12%)
  between operations  15.3 us (4%)
    pallas_call x45, Pallas kernels, __call__(): pl.pallas_call(stripped, out_shape=out_shape + [shaped(c.shape, c.dtype)...  125 us
    ppermute x15, waiting for transfers between devices, step(): self.arrived = lax.ppermute(total, 'dp', ring)  72.3 us
    unnamed x233, local copies, waits for them, and re-layouts  45.9 us
    ppermute x32, waiting for transfers between devices, swap(): return lax.ppermute(value, axis, [(i, i ^ flip) for i in range(count)])  40.8 us
    ppermute x32, starting transfers between devices, swap(): return lax.ppermute(value, axis, [(i, i ^ flip) for i in range(count)])  29.3 us
    ppermute x15, starting transfers between devices, step(): self.arrived = lax.ppermute(total, 'dp', ring)  11.6 us
  transfers between devices with their start and end apart: 49, of which 22 were waited for; matrix products, arithmetic and copies ran while one was open for 1% of the time, Pallas kernels for 32%

profile of v3, /device:TPU:0, one launch (start us, length us, event | category | flops | bytes accessed | tf_op | source)
XLA Modules:
  0.0 343.9 jit_solution(10238834084526760230)
XLA Ops:
  8.1 1.3 copy-done.17
  13.2 2.5 collective-permute-start.2
  16.4 3.0 shard_map.195.refs_2_.refs_1_
  20.5 2.0 collective-permute-done.1.refs_4_.refs_10_
  22.6 14.7 %shard_map.197 = (bf16[256,1024]{1,0:T(8,128)(2,1)S(1)}, f32[4,4,256]{2,1,0:T(4,128)S(1)}, bf16[256,2048]{1,0:T(8,128)(2,1)S(1)}) custom-call(s32[1]{0:T(128)} %bitcast.refs_0_, bf16[256,1024]{1,0:T(8,128)(2,1)S(1)} %shard_map.195.refs_2_.refs_1_, bf16[256,256]{1,0:T(8,128)(2,1)S(1)} %get-tuple-element.58.refs_2_.refs_8_, ...), custom_call_target="tpu_custom_call" | custom-call | flops 46200000512 | bytes 1000 | tf_op jit(solution)/shard_map/pallas_call | solution.py:81
  38.7 2.3 collective-permute-start.3
  41.0 1.5 collective-permute-start.4
  43.0 13.1 %collective-permute-done.4.refs_4_.refs_1_ = bf16[256,1024]{1,0:T(8,128)(2,1)} collective-permute-done((bf16[256,1024]{1,0:T(8,128)(2,1)}, bf16[256,1024]{1,0:T(8,128)(2,1)}, u32[]{:S(2)}, u32[]{:S(2)}) %collective-permute-start.4) | collective-permute-done | bytes 524320 | tf_op jit(solution)/shard_map/ppermute | solution.py:103
  60.5 3.8 %collective-permute-done.3.refs_3_ = bf16[256,2048]{1,0:T(8,128)(2,1)S(1)} collective-permute-done((bf16[256,2048]{1,0:T(8,128)(2,1)S(1)}, bf16[256,2048]{1,0:T(8,128)(2,1)S(1)}, u32[]{:S(2)}, u32[]{:S(2)}) %collective-permute-start.3) | collective-permute-done | bytes 1048608 | tf_op jit(solution)/shard_map/ppermute | solution.py:103
  64.3 1.4 copy-done.28
  67.0 1.9 collective-permute-start.5
  69.0 8.8 %shard_map.200 = (bf16[256,1280]{1,0:T(8,128)(2,1)S(1)}, bf16[256,2560]{1,0:T(8,128)(2,1)}) custom-call(bf16[256,2048]{1,0:T(8,128)(2,1)S(1)} %get-tuple-element.65.refs_0_, bf16[256,2048]{1,0:T(8,128)(2,1)S(1)} %bitcast.55, bf16[2048,2816]{1,0:T(8,128)(2,1)S(1)} %bitcast.53, bf16[2048,2816]{1,0:T(8,128)(2,1)} %refs_2_.11, bf16[2816,2048]{1,0:T(8,128)(2,1)} %refs_2_.12, ...), custom_call_target="tpu_custom_call" | custom-call | flops 32999999488 | bytes 1000 | tf_op jit(solution)/shard_map/pallas_call | solution.py:81
  79.8 1.7 collective-permute-done.5.refs_7_.refs_1_
  81.5 10.2 %shard_map.201 = (bf16[256,1536]{1,0:T(8,128)(2,1)}, bf16[256,3072]{1,0:T(8,128)(2,1)S(1)}) custom-call(bf16[256,2048]{1,0:T(8,128)(2,1)S(1)} %get-tuple-element.65.refs_0_, bf16[256,2048]{1,0:T(8,128)(2,1)S(1)} %bitcast.56, bf16[2048,2816]{1,0:T(8,128)(2,1)S(1)} %bitcast.53, bf16[2048,2816]{1,0:T(8,128)(2,1)} %refs_2_.11, bf16[2816,2048]{1,0:T(8,128)(2,1)} %refs_2_.12, ...), custom_call_target="tpu_custom_call" | custom-call | flops 32999999488 | bytes 1000 | tf_op jit(solution)/shard_map/pallas_call | solution.py:81
  91.7 3.9 %collective-permute-done.7.refs_3_ = bf16[256,1280]{1,0:T(8,128)(2,1)S(1)} collective-permute-done((bf16[256,1280]{1,0:T(8,128)(2,1)S(1)}, bf16[256,1280]{1,0:T(8,128)(2,1)S(1)}, u32[]{:S(2)}, u32[]{:S(2)}) %collective-permute-start.7) | collective-permute-done | bytes 655392 | tf_op jit(solution)/shard_map/ppermute | solution.py:103
  95.5 3.6 %shard_map.202 = (bf16[4,1280,128]{2,1,0:T(8,128)(2,1)S(1)}, bf16[4,1280,128]{2,1,0:T(8,128)(2,1)S(1)}) custom-call(bf16[256,1024]{1,0:T(8,128)(2,1)S(1)} %copy-done.101, bf16[256,1024]{1,0:T(8,128)(2,1)} %collective-permute-done.4.refs_4_.refs_1_, bf16[256,1280]{1,0:T(8,128)(2,1)S(1)} %get-tuple-element.66.refs_5_.refs_2_.refs_0_, ...), custom_call_target="tpu_custom_call" | custom-call | flops 9900000256 | bytes 1000 | tf_op jit(solution)/shard_map/pallas_call | solution.py:81
  99.2 6.9 %shard_map.203 = (f32[256,2048]{1,0:T(8,128)S(1)}, bf16[256,1536]{1,0:T(8,128)(2,1)}, bf16[256,3072]{1,0:T(8,128)(2,1)S(1)}) custom-call(bf16[256,2560]{1,0:T(8,128)(2,1)} %get-tuple-element.67.refs_0_.refs_2_, bf16[2048,2816]{1,0:T(8,128)(2,1)S(1)} %bitcast.53, bf16[2048,2816]{1,0:T(8,128)(2,1)} %refs_2_.11, ...), custom_call_target="tpu_custom_call", output_to_operand_aliasing={{1}: (3, {}), {2}: (4, {})} | custom-call | flops 23100000256 | bytes 1000 | tf_op jit(solution)/shard_map/pallas_call | solution.py:81
  106.1 2.1 collective-permute-start.10
  108.4 1.6 collective-permute-start.11
  110.0 4.3 %copy-done.9 = bf16[2048,2816]{1,0:T(8,128)(2,1)S(1)} copy-done((bf16[2048,2816]{1,0:T(8,128)(2,1)S(1)}, bf16[2048,2816]{1,0:T(8,128)(2,1)}, u32[]{:S(2)}) %copy-start.9) | copy-done | bytes 11534360
  114.3 8.4 %shard_map.205 = (bf16[256,2048]{1,0:T(8,128)(2,1)}, bf16[256,3072]{1,0:T(8,128)(2,1)S(1)}) custom-call(bf16[256,3072]{1,0:T(8,128)(2,1)S(1)} %get-tuple-element.74.refs_0_, bf16[2048,2816]{1,0:T(8,128)(2,1)S(1)} %copy-done.9, bf16[2048,2816]{1,0:T(8,128)(2,1)} %refs_2_.11, ...), custom_call_target="tpu_custom_call", output_to_operand_aliasing={{1}: (4, {})} | custom-call | flops 26400000000 | bytes 1000 | tf_op jit(solution)/shard_map/pallas_call | solution.py:81
  122.7 1.5 collective-permute-start.15
  124.3 1.6 collective-permute-start.12
  126.0 5.9 %shard_map.207.refs_4_ = bf16[4,2,128,2560]{3,2,1,0:T(8,128)(2,1)S(1)} custom-call(bf16[256,1024]{1,0:T(8,128)(2,1)S(1)} %get-tuple-element.68.refs_6_.refs_0_, bf16[256,1024]{1,0:T(8,128)(2,1)S(1)} %collective-permute-done.5.refs_7_.refs_1_, bf16[256,2560]{1,0:T(8,128)(2,1)} %get-tuple-element.67.refs_0_.refs_2_, ...), custom_call_target="tpu_custom_call" | custom-call | flops 16499999744 | bytes 1000 | tf_op jit(solution)/shard_map/pallas_call | solution.py:81
  131.9 2.4 copy-done.1
  135.1 2.5 copy-done.2
  137.6 1.3 copy-done.81
  140.0 7.7 %collective-permute-done.15.refs_3_ = bf16[256,2048]{1,0:T(8,128)(2,1)} collective-permute-done((bf16[256,2048]{1,0:T(8,128)(2,1)}, bf16[256,2048]{1,0:T(8,128)(2,1)}, u32[]{:S(2)}, u32[]{:S(2)}) %collective-permute-start.15) | collective-permute-done | bytes 1048608 | tf_op jit(solution)/shard_map/ppermute | solution.py:103
  147.7 4.7 %shard_map.209 = (f32[256,2048]{1,0:T(8,128)S(1)}, bf16[256,2048]{1,0:T(8,128)(2,1)S(1)}, f32[1,2048]{1,0:T(1,128)S(1)}, bf16[256,1024]{1,0:T(8,128)(2,1)S(1)}, bf16[256,1024]{1,0:T(8,128)(2,1)}) custom-call(s32[1]{0:T(128)} %bitcast.refs_0_, bf16[256,2048]{1,0:T(8,128)(2,1)S(1)} %bitcast.57, bf16[256,2048]{1,0:T(8,128)(2,1)} %get-tuple-element.78.refs_4_.refs_2_, ...), custom_call_target="tpu_custom_call" | custom-call | flops 13200000000 | bytes 1000 | tf_op jit(solution)/shard_map/pallas_call | solution.py:81
  153.5 2.4 collective-permute-done.14.refs_3_
  157.0 4.6 %shard_map.211 = (bf16[4,1536,128]{2,1,0:T(8,128)(2,1)S(1)}, bf16[4,1536,128]{2,1,0:T(8,128)(2,1)S(1)}) custom-call(bf16[256,1024]{1,0:T(8,128)(2,1)S(1)} %copy-done.102, bf16[256,1024]{1,0:T(8,128)(2,1)} %collective-permute-done.4.refs_4_.refs_1_, bf16[256,1536]{1,0:T(8,128)(2,1)} %get-tuple-element.73.refs_2_.refs_1_, ...), custom_call_target="tpu_custom_call" | custom-call | flops 9900000256 | bytes 1000 | tf_op jit(solution)/shard_map/pallas_call | solution.py:81
  161.8 16.4 %shard_map.212 = (bf16[256,1024]{1,0:T(8,128)(2,1)S(1)}, bf16[256,256]{1,0:T(8,128)(2,1)S(1)}, bf16[256,256]{1,0:T(8,128)(2,1)}, bf16[256,256]{1,0:T(8,128)(2,1)}, bf16[256,256]{1,0:T(8,128)(2,1)S(1)}) custom-call(s32[1]{0:T(128)} %bitcast.refs_0_, bf16[256,1024]{1,0:T(8,128)(2,1)S(1)} %copy-done.104, bf16[256,1024]{1,0:T(8,128)(2,1)S(1)} %copy-done.42, ...), custom_call_target="tpu_custom_call" | custom-call | flops 52800000000 | bytes 1000 | tf_op jit(solution)/shard_map/pallas_call | solution.py:81
  178.7 2.0 collective-permute-start.20
  182.1 6.4 %shard_map.214.refs_3_ = bf16[4,2,128,3072]{3,2,1,0:T(8,128)(2,1)S(1)} custom-call(bf16[256,1024]{1,0:T(8,128)(2,1)S(1)} %copy-done.106, bf16[256,1024]{1,0:T(8,128)(2,1)S(1)} %copy-done.49, bf16[256,3072]{1,0:T(8,128)(2,1)S(1)} %get-tuple-element.77.refs_2_, bf16[256,3072]{1,0:T(8,128)(2,1)} %collective-permute-done.9.refs_3_, ...), custom_call_target="tpu_custom_call" | custom-call | flops 16499999744 | bytes 1000 | tf_op jit(solution)/shard_map/pallas_call | solution.py:81
  188.6 4.3 %copy-done.10 = bf16[2816,2048]{1,0:T(8,128)(2,1)S(1)} copy-done((bf16[2816,2048]{1,0:T(8,128)(2,1)S(1)}, bf16[2816,2048]{1,0:T(8,128)(2,1)}, u32[]{:S(2)}) %copy-start.10) | copy-done | bytes 11534360
  192.9 7.1 %shard_map.215.refs_4_.refs_1_ = bf16[256,2048]{1,0:T(8,128)(2,1)S(1)} custom-call(bf16[256,1280]{1,0:T(8,128)(2,1)S(1)} %copy-done.34, bf16[256,1536]{1,0:T(8,128)(2,1)} %get-tuple-element.73.refs_2_.refs_1_, bf16[2816,2048]{1,0:T(8,128)(2,1)S(1)} %copy-done.10, bf16[4,2,128,3072]{3,2,1,0:T(8,128)(2,1)S(1)} %shard_map.214.refs_3_), custom_call_target="tpu_custom_call" | custom-call | flops 26400000000 | bytes 1000 | tf_op jit(solution)/shard_map/pallas_call | solution.py:81
  200.1 3.9 %collective-permute-done.22.refs_3_ = bf16[1,1536,128]{2,1,0:T(8,128)(2,1)} collective-permute-done((bf16[1,1536,128]{2,1,0:T(8,128)(2,1)}, bf16[1,1536,128]{2,1,0:T(8,128)(2,1)}, u32[]{:S(2)}, u32[]{:S(2)}) %collective-permute-start.22) | collective-permute-done | bytes 393248 | tf_op jit(solution)/shard_map/ppermute | solution.py:376
  203.9 1.4 copy-done.86
  206.7 1.4 shard_map.217.refs_1_.refs_5_.refs_2_
  209.5 2.3 shard_map.218.refs_4_.refs_0_
  211.9 9.1 %collective-permute-done.26.refs_3_ = bf16[1,1536,128]{2,1,0:T(8,128)(2,1)S(1)} collective-permute-done((bf16[1,1536,128]{2,1,0:T(8,128)(2,1)S(1)}, bf16[1,1536,128]{2,1,0:T(8,128)(2,1)S(1)}, u32[]{:S(2)}, u32[]{:S(2)}) %collective-permute-start.26) | collective-permute-done | bytes 393248 | tf_op jit(solution)/shard_map/ppermute | solution.py:376
  221.3 2.8 shard_map.220
  224.2 2.7 collective-permute-start.18
  227.0 19.3 %collective-permute-done.28.refs_3_ = bf16[1,1536,128]{2,1,0:T(8,128)(2,1)S(1)} collective-permute-done((bf16[1,1536,128]{2,1,0:T(8,128)(2,1)S(1)}, bf16[1,1536,128]{2,1,0:T(8,128)(2,1)S(1)}, u32[]{:S(2)}, u32[]{:S(2)}) %collective-permute-start.28) | collective-permute-done | bytes 393248 | tf_op jit(solution)/shard_map/ppermute | solution.py:376
  247.4 3.1 collective-permute-done.24.refs_3_
  250.6 2.7 shard_map.223
  254.3 1.7 collective-permute-start.23
  256.0 14.7 %collective-permute-done.30.refs_3_ = bf16[1,1024,128]{2,1,0:T(8,128)(2,1)S(1)} collective-permute-done((bf16[1,1024,128]{2,1,0:T(8,128)(2,1)S(1)}, bf16[1,1024,128]{2,1,0:T(8,128)(2,1)S(1)}, u32[]{:S(2)}, u32[]{:S(2)}) %collective-permute-start.30) | collective-permute-done | bytes 262176 | tf_op jit(solution)/shard_map/ppermute | solution.py:376
  275.0 1.5 copy-done.71
  278.2 3.3 collective-permute-done.32.refs_1_
  281.5 3.1 shard_map.227
  285.0 1.9 collective-permute-start.41
  288.4 3.6 %collective-permute-start.44 = (f32[2,128]{1,0:T(2,128)S(1)}, f32[2,128]{1,0:T(2,128)S(1)}, u32[]{:S(2)}, u32[]{:S(2)}) collective-permute-start(f32[2,128]{1,0:T(2,128)S(1)} %bitcast.88), channel_id=1, source_target_pairs={{0,12},{4,8},{8,4},{12,0},{1,13},{5,9},{9,5},{13,1},{2,14},{6,10},... | collective-permute-start | bytes 3080 | tf_op jit(solution)/shard_map/ppermute | solution.py:103
  294.1 1.5 collective-permute-start.35
  295.6 1.9 collective-permute-start.34
  300.4 4.7 %collective-permute-done.35.refs_3_ = bf16[1,1024,128]{2,1,0:T(8,128)(2,1)S(1)} collective-permute-done((bf16[1,1024,128]{2,1,0:T(8,128)(2,1)S(1)}, bf16[1,1024,128]{2,1,0:T(8,128)(2,1)S(1)}, u32[]{:S(2)}, u32[]{:S(2)}) %collective-permute-start.35) | collective-permute-done | bytes 262176 | tf_op jit(solution)/shard_map/ppermute | solution.py:376
  305.2 5.4 %collective-permute-done.34.refs_3_ = bf16[1,128,1024]{2,1,0:T(8,128)(2,1)S(1)} collective-permute-done((bf16[1,128,1024]{2,1,0:T(8,128)(2,1)S(1)}, bf16[1,128,1024]{2,1,0:T(8,128)(2,1)S(1)}, u32[]{:S(2)}, u32[]{:S(2)}) %collective-permute-start.34) | collective-permute-done | bytes 262176 | tf_op jit(solution)/shard_map/ppermute | solution.py:376
  312.7 5.0 %collective-permute-done.38.refs_3_ = bf16[1,1024,128]{2,1,0:T(8,128)(2,1)S(1)} collective-permute-done((bf16[1,1024,128]{2,1,0:T(8,128)(2,1)S(1)}, bf16[1,1024,128]{2,1,0:T(8,128)(2,1)S(1)}, u32[]{:S(2)}, u32[]{:S(2)}) %collective-permute-start.38) | collective-permute-done | bytes 262176 | tf_op jit(solution)/shard_map/ppermute | solution.py:376
  318.6 4.2 %collective-permute-done.37.refs_3_ = bf16[1,128,1024]{2,1,0:T(8,128)(2,1)S(1)} collective-permute-done((bf16[1,128,1024]{2,1,0:T(8,128)(2,1)S(1)}, bf16[1,128,1024]{2,1,0:T(8,128)(2,1)S(1)}, u32[]{:S(2)}, u32[]{:S(2)}) %collective-permute-start.37) | collective-permute-done | bytes 262176 | tf_op jit(solution)/shard_map/ppermute | solution.py:376
  324.1 1.3 collective-permute-start.46
  325.5 1.3 shard_map.235.refs_2_
  330.3 1.8 shard_map.236
  332.0 1.6 collective-permute-done.46.refs_3_
  333.6 1.4 copy-done.68
  (328 shorter events, 50.3 us)
Async XLA Ops:
  7.2 319.6 %reduce-scatter.3.cloned.1.call-start = ((), (), s32[]{:S(2)}) async-start(), calls=%async_computation.2 | async-start | bytes 5898240 | tf_op jit(solution)/shard_map/reduce_scatter | solution.py:281
  13.2 7.3 %collective-permute-start.2 = (bf16[256,256]{1,0:T(8,128)(2,1)S(1)}, bf16[256,256]{1,0:T(8,128)(2,1)S(1)}, u32[]{:S(2)}, u32[]{:S(2)}) collective-permute-start(bf16[256,256]{1,0:T(8,128)(2,1)S(1)} %get-tuple-element.58.refs_2_.refs_8_), channel_id=1, source_target_pairs={{0,3},{1,2},{2,1},{3,0},{4,7},{5,6},{6,5},{7,4},{8,11},{9,10},{10,... | collective-permute-start | bytes 393224 | tf_op jit(solution)/shard_map/ppermute | solution.py:103
  15.7 6.9 %collective-permute-start.1 = (bf16[256,256]{1,0:T(8,128)(2,1)S(1)}, bf16[256,256]{1,0:T(8,128)(2,1)S(1)}, u32[]{:S(2)}, u32[]{:S(2)}) collective-permute-start(bf16[256,256]{1,0:T(8,128)(2,1)S(1)} %get-tuple-element.58.refs_2_.refs_8_), channel_id=1, source_target_pairs={{0,2},{1,3},{2,0},{3,1},{4,6},{5,7},{6,4},{7,5},{8,10},{9,11},{10,... | collective-permute-start | bytes 393224 | tf_op jit(solution)/shard_map/ppermute | solution.py:103
  16.3 6.2 %collective-permute-start = (bf16[256,256]{1,0:T(8,128)(2,1)S(1)}, bf16[256,256]{1,0:T(8,128)(2,1)S(1)}, u32[]{:S(2)}, u32[]{:S(2)}) collective-permute-start(bf16[256,256]{1,0:T(8,128)(2,1)S(1)} %get-tuple-element.58.refs_2_.refs_8_), channel_id=1, source_target_pairs={{0,1},{1,0},{2,3},{3,2},{4,5},{5,4},{6,7},{7,6},{8,9},{9,8},{10,11... | collective-permute-start | bytes 393224 | tf_op jit(solution)/shard_map/ppermute | solution.py:103
  20.5 16.8 %copy-start.99 = (bf16[256,1024]{1,0:T(8,128)(2,1)}, bf16[256,1024]{1,0:T(8,128)(2,1)S(1)}, u32[]{:S(2)}) copy-start(bf16[256,1024]{1,0:T(8,128)(2,1)S(1)} %get-tuple-element.59.refs_7_.refs_3_.refs_0_) | copy-start | bytes 1572868
  20.5 16.8 %copy-start.58 = (bf16[256,256]{1,0:T(8,128)(2,1)}, bf16[256,256]{1,0:T(8,128)(2,1)S(1)}, u32[]{:S(2)}) copy-start(bf16[256,256]{1,0:T(8,128)(2,1)S(1)} %collective-permute-done.2.refs_5_.refs_11_) | copy-start | bytes 393220
  22.5 14.7 %copy-start.60 = (bf16[256,256]{1,0:T(8,128)(2,1)}, bf16[256,256]{1,0:T(8,128)(2,1)S(1)}, u32[]{:S(2)}) copy-start(bf16[256,256]{1,0:T(8,128)(2,1)S(1)} %collective-permute-done.1.refs_4_.refs_10_) | copy-start | bytes 393220
  22.5 14.8 %copy-start.62 = (bf16[256,256]{1,0:T(8,128)(2,1)}, bf16[256,256]{1,0:T(8,128)(2,1)S(1)}, u32[]{:S(2)}) copy-start(bf16[256,256]{1,0:T(8,128)(2,1)S(1)} %collective-permute-done.refs_3_.refs_9_) | copy-start | bytes 393220
  38.7 21.0 %copy-start.27 = (bf16[256,2048]{1,0:T(8,128)(2,1)}, bf16[256,2048]{1,0:T(8,128)(2,1)S(1)}, u32[]{:S(2)}) copy-start(bf16[256,2048]{1,0:T(8,128)(2,1)S(1)} %get-tuple-element.60.refs_2_) | copy-start | bytes 3145732
  38.7 25.6 %collective-permute-start.3 = (bf16[256,2048]{1,0:T(8,128)(2,1)S(1)}, bf16[256,2048]{1,0:T(8,128)(2,1)S(1)}, u32[]{:S(2)}, u32[]{:S(2)}) collective-permute-start(bf16[256,2048]{1,0:T(8,128)(2,1)S(1)} %get-tuple-element.60.refs_2_), channel_id=1, source_target_pairs={{0,16},{16,0},{1,17},{17,1},{2,18},{18,2},{3,19},{19,3},{4,20},{20... | collective-permute-start | bytes 3145736 | tf_op jit(solution)/shard_map/ppermute | solution.py:103
  41.0 15.1 %collective-permute-start.4 = (bf16[256,1024]{1,0:T(8,128)(2,1)}, bf16[256,1024]{1,0:T(8,128)(2,1)}, u32[]{:S(2)}, u32[]{:S(2)}) collective-permute-start(bf16[256,1024]{1,0:T(8,128)(2,1)} %get-tuple-element.62), channel_id=1, source_target_pairs={{0,2},{1,3},{2,0},{3,1},{4,6},{5,7},{6,4},{7,5},{8,10},{9,11},{10,... | collective-permute-start | bytes 1572872 | tf_op jit(solution)/shard_map/ppermute | solution.py:103
  42.5 21.8 %copy-start.18 = (bf16[256,1,2048]{2,0,1:T(8,128)(2,1)S(1)}, bf16[256,1,2048]{2,0,1:T(8,128)(2,1)}, u32[]{:S(2)}) copy-start(bf16[256,1,2048]{2,0,1:T(8,128)(2,1)} %param.11) | copy-start | bytes 3145732
  42.5 37.3 %collective-permute-start.6 = (bf16[256,1024]{1,0:T(8,128)(2,1)}, bf16[256,1024]{1,0:T(8,128)(2,1)S(1)}, u32[]{:S(2)}, u32[]{:S(2)}) collective-permute-start(bf16[256,1024]{1,0:T(8,128)(2,1)} %copy-done.39), channel_id=1, source_target_pairs={{0,2},{1,3},{2,0},{3,1},{4,6},{5,7},{6,4},{7,5},{8,10},{9,11},{10,... | collective-permute-start | bytes 1572872 | tf_op jit(solution)/shard_map/ppermute | solution.py:103
  67.0 59.0 %copy-start.105 = (bf16[256,1024]{1,0:T(8,128)(2,1)}, bf16[256,1024]{1,0:T(8,128)(2,1)S(1)}, u32[]{:S(2)}) copy-start(bf16[256,1024]{1,0:T(8,128)(2,1)S(1)} %get-tuple-element.68.refs_6_.refs_0_) | copy-start | bytes 1572868
  67.0 14.5 %collective-permute-start.5 = (bf16[256,1024]{1,0:T(8,128)(2,1)S(1)}, bf16[256,1024]{1,0:T(8,128)(2,1)S(1)}, u32[]{:S(2)}, u32[]{:S(2)}) collective-permute-start(bf16[256,1024]{1,0:T(8,128)(2,1)S(1)} %get-tuple-element.69), channel_id=1, source_target_pairs={{0,2},{1,3},{2,0},{3,1},{4,6},{5,7},{6,4},{7,5},{8,10},{9,11},{10,... | collective-permute-start | bytes 1572872 | tf_op jit(solution)/shard_map/ppermute | solution.py:103
  77.7 17.8 %copy-start.33 = (bf16[256,1280]{1,0:T(8,128)(2,1)}, bf16[256,1280]{1,0:T(8,128)(2,1)S(1)}, u32[]{:S(2)}) copy-start(bf16[256,1280]{1,0:T(8,128)(2,1)S(1)} %get-tuple-element.66.refs_5_.refs_2_.refs_0_) | copy-start | bytes 1966084
  77.7 17.8 %collective-permute-start.7 = (bf16[256,1280]{1,0:T(8,128)(2,1)S(1)}, bf16[256,1280]{1,0:T(8,128)(2,1)S(1)}, u32[]{:S(2)}, u32[]{:S(2)}) collective-permute-start(bf16[256,1280]{1,0:T(8,128)(2,1)S(1)} %get-tuple-element.66.refs_5_.refs_2_.refs_0_), channel_id=1, source_target_pairs={{0,2},{1,3},{2,0},{3,1},{4,6},{5,7},{6,4},{7,5},{8,10},{9,11},{10,... | collective-permute-start | bytes 1966088 | tf_op jit(solution)/shard_map/ppermute | solution.py:103
  78.6 47.4 %collective-permute-start.13 = (bf16[256,2560]{1,0:T(8,128)(2,1)}, bf16[256,2560]{1,0:T(8,128)(2,1)}, u32[]{:S(2)}, u32[]{:S(2)}) collective-permute-start(bf16[256,2560]{1,0:T(8,128)(2,1)} %get-tuple-element.67.refs_0_.refs_2_), channel_id=1, source_target_pairs={{0,2},{1,3},{2,0},{3,1},{4,6},{5,7},{6,4},{7,5},{8,10},{9,11},{10,... | collective-permute-start | bytes 3932168 | tf_op jit(solution)/shard_map/ppermute | solution.py:103
  81.5 44.5 %copy-start.48 = (bf16[256,1024]{1,0:T(8,128)(2,1)}, bf16[256,1024]{1,0:T(8,128)(2,1)S(1)}, u32[]{:S(2)}) copy-start(bf16[256,1024]{1,0:T(8,128)(2,1)S(1)} %collective-permute-done.5.refs_7_.refs_1_) | copy-start | bytes 1572868
  81.5 14.0 %copy-start.101 = (bf16[256,1024]{1,0:T(8,128)(2,1)S(1)}, bf16[256,1024]{1,0:T(8,128)(2,1)}, u32[]{:S(2)}) copy-start(bf16[256,1024]{1,0:T(8,128)(2,1)} %copy-done.99) | copy-start | bytes 1572868
  99.2 25.1 %copy-start.80 = (bf16[4,1280,128]{2,1,0:T(8,128)(2,1)}, bf16[4,1280,128]{2,1,0:T(8,128)(2,1)S(1)}, u32[]{:S(2)}) copy-start(bf16[4,1280,128]{2,1,0:T(8,128)(2,1)S(1)} %get-tuple-element.72.refs_5_.refs_1_) | copy-start | bytes 3932164
  99.2 9.1 %collective-permute-start.8 = (bf16[4,1280,128]{2,1,0:T(8,128)(2,1)S(1)}, bf16[4,1280,128]{2,1,0:T(8,128)(2,1)S(1)}, u32[]{:S(2)}, u32[]{:S(2)}) collective-permute-start(bf16[4,1280,128]{2,1,0:T(8,128)(2,1)S(1)} %get-tuple-element.76), channel_id=1, source_target_pairs={{0,1},{1,0},{2,3},{3,2},{4,5},{5,4},{6,7},{7,6},{8,9},{9,8},{10,11... | collective-permute-start | bytes 3932168 | tf_op jit(solution)/shard_map/ppermute | solution.py:103
  106.1 50.0 %collective-permute-start.10 = (bf16[256,1536]{1,0:T(8,128)(2,1)}, bf16[256,1536]{1,0:T(8,128)(2,1)}, u32[]{:S(2)}, u32[]{:S(2)}) collective-permute-start(bf16[256,1536]{1,0:T(8,128)(2,1)} %get-tuple-element.73.refs_2_.refs_1_), channel_id=1, source_target_pairs={{0,2},{1,3},{2,0},{3,1},{4,6},{5,7},{6,4},{7,5},{8,10},{9,11},{10,... | collective-permute-start | bytes 2359304 | tf_op jit(solution)/shard_map/ppermute | solution.py:103
  108.4 15.8 %collective-permute-start.11 = (bf16[1,1280,128]{2,1,0:T(8,128)(2,1)S(1)}, bf16[1,1280,128]{2,1,0:T(8,128)(2,1)S(1)}, u32[]{:S(2)}, u32[]{:S(2)}) collective-permute-start(bf16[1,1280,128]{2,1,0:T(8,128)(2,1)S(1)} %shard_map.204.refs_5_), channel_id=1, source_target_pairs={{0,4},{4,8},{8,12},{12,0},{1,5},{5,9},{9,13},{13,1},{2,6},{6,10},{... | collective-permute-start | bytes 983048 | tf_op jit(solution)/shard_map/ppermute | solution.py:376
  122.7 24.9 %collective-permute-start.15 = (bf16[256,2048]{1,0:T(8,128)(2,1)}, bf16[256,2048]{1,0:T(8,128)(2,1)}, u32[]{:S(2)}, u32[]{:S(2)}) collective-permute-start(bf16[256,2048]{1,0:T(8,128)(2,1)} %get-tuple-element.78.refs_4_.refs_2_), channel_id=1, source_target_pairs={{0,16},{16,0},{1,17},{17,1},{2,18},{18,2},{3,19},{19,3},{4,20},{20... | collective-permute-start | bytes 3145736 | tf_op jit(solution)/shard_map/ppermute | solution.py:103
  124.2 57.4 %collective-permute-start.9 = (bf16[256,3072]{1,0:T(8,128)(2,1)S(1)}, bf16[256,3072]{1,0:T(8,128)(2,1)}, u32[]{:S(2)}, u32[]{:S(2)}) collective-permute-start(bf16[256,3072]{1,0:T(8,128)(2,1)S(1)} %get-tuple-element.77.refs_2_), channel_id=1, source_target_pairs={{0,2},{1,3},{2,0},{3,1},{4,6},{5,7},{6,4},{7,5},{8,10},{9,11},{10,... | collective-permute-start | bytes 4718600 | tf_op jit(solution)/shard_map/ppermute | solution.py:103
  124.3 10.7 %collective-permute-start.12 = (bf16[1,1280,128]{2,1,0:T(8,128)(2,1)S(1)}, bf16[1,1280,128]{2,1,0:T(8,128)(2,1)S(1)}, u32[]{:S(2)}, u32[]{:S(2)}) collective-permute-start(bf16[1,1280,128]{2,1,0:T(8,128)(2,1)S(1)} %shard_map.206.refs_4_), channel_id=1, source_target_pairs={{0,4},{4,8},{8,12},{12,0},{1,5},{5,9},{9,13},{13,1},{2,6},{6,10},{... | collective-permute-start | bytes 983048 | tf_op jit(solution)/shard_map/ppermute | solution.py:376
  134.4 192.5 %reduce-scatter.5.cloned.1.call-start = ((), (), s32[]{:S(2)}) async-start(), calls=%async_computation.3 | async-start | bytes 7077888 | tf_op jit(solution)/shard_map/reduce_scatter | solution.py:281
  139.0 16.9 %copy-start.82 = (bf16[4,1280,128]{2,1,0:T(8,128)(2,1)S(1)}, bf16[4,1280,128]{2,1,0:T(8,128)(2,1)}, u32[]{:S(2)}) copy-start(bf16[4,1280,128]{2,1,0:T(8,128)(2,1)} %copy-done.80) | copy-start | bytes 3932164
  139.0 16.8 %collective-permute-start.14 = (bf16[1,1280,128]{2,1,0:T(8,128)(2,1)S(1)}, bf16[1,1280,128]{2,1,0:T(8,128)(2,1)S(1)}, u32[]{:S(2)}, u32[]{:S(2)}) collective-permute-start(bf16[1,1280,128]{2,1,0:T(8,128)(2,1)S(1)} %shard_map.208.refs_6_), channel_id=1, source_target_pairs={{0,4},{4,8},{8,12},{12,0},{1,5},{5,9},{9,13},{13,1},{2,6},{6,10},{... | collective-permute-start | bytes 983048 | tf_op jit(solution)/shard_map/ppermute | solution.py:376
  153.2 68.0 %collective-permute-start.25 = (bf16[256,1024]{1,0:T(8,128)(2,1)}, bf16[256,1024]{1,0:T(8,128)(2,1)}, u32[]{:S(2)}, u32[]{:S(2)}) collective-permute-start(bf16[256,1024]{1,0:T(8,128)(2,1)} %get-tuple-element.91), channel_id=1, source_target_pairs={{0,2},{1,3},{2,0},{3,1},{4,6},{5,7},{6,4},{7,5},{8,10},{9,11},{10,... | collective-permute-start | bytes 1572872 | tf_op jit(solution)/shard_map/ppermute | solution.py:103
  161.6 19.1 %copy-start.85 = (bf16[4,1536,128]{2,1,0:T(8,128)(2,1)}, bf16[4,1536,128]{2,1,0:T(8,128)(2,1)S(1)}, u32[]{:S(2)}) copy-start(bf16[4,1536,128]{2,1,0:T(8,128)(2,1)S(1)} %get-tuple-element.80.refs_12_.refs_1_) | copy-start | bytes 4718596
  161.6 19.0 %collective-permute-start.16 = (bf16[4,1536,128]{2,1,0:T(8,128)(2,1)S(1)}, bf16[4,1536,128]{2,1,0:T(8,128)(2,1)S(1)}, u32[]{:S(2)}, u32[]{:S(2)}) collective-permute-start(bf16[4,1536,128]{2,1,0:T(8,128)(2,1)S(1)} %get-tuple-element.81), channel_id=1, source_target_pairs={{0,1},{1,0},{2,3},{3,2},{4,5},{5,4},{6,7},{7,6},{8,9},{9,8},{10,11... | collective-permute-start | bytes 4718600 | tf_op jit(solution)/shard_map/ppermute | solution.py:103
  178.2 28.4 %collective-permute-start.19 = (bf16[256,256]{1,0:T(8,128)(2,1)}, bf16[256,256]{1,0:T(8,128)(2,1)}, u32[]{:S(2)}, u32[]{:S(2)}) collective-permute-start(bf16[256,256]{1,0:T(8,128)(2,1)} %get-tuple-element.87), channel_id=1, source_target_pairs={{0,1},{1,0},{2,3},{3,2},{4,5},{5,4},{6,7},{7,6},{8,9},{9,8},{10,11... | collective-permute-start | bytes 393224 | tf_op jit(solution)/shard_map/ppermute | solution.py:103
  178.7 27.9 %collective-permute-start.20 = (bf16[256,256]{1,0:T(8,128)(2,1)}, bf16[256,256]{1,0:T(8,128)(2,1)}, u32[]{:S(2)}, u32[]{:S(2)}) collective-permute-start(bf16[256,256]{1,0:T(8,128)(2,1)} %get-tuple-element.88), channel_id=1, source_target_pairs={{0,2},{1,3},{2,0},{3,1},{4,6},{5,7},{6,4},{7,5},{8,10},{9,11},{10,... | collective-permute-start | bytes 393224 | tf_op jit(solution)/shard_map/ppermute | solution.py:103
  180.7 26.0 %collective-permute-start.21 = (bf16[256,256]{1,0:T(8,128)(2,1)S(1)}, bf16[256,256]{1,0:T(8,128)(2,1)}, u32[]{:S(2)}, u32[]{:S(2)}) collective-permute-start(bf16[256,256]{1,0:T(8,128)(2,1)S(1)} %get-tuple-element.89), channel_id=1, source_target_pairs={{0,3},{1,2},{2,1},{3,0},{4,7},{5,6},{6,5},{7,4},{8,11},{9,10},{10,... | collective-permute-start | bytes 393224 | tf_op jit(solution)/shard_map/ppermute | solution.py:103
  181.6 22.4 %collective-permute-start.22 = (bf16[1,1536,128]{2,1,0:T(8,128)(2,1)}, bf16[1,1536,128]{2,1,0:T(8,128)(2,1)}, u32[]{:S(2)}, u32[]{:S(2)}) collective-permute-start(bf16[1,1536,128]{2,1,0:T(8,128)(2,1)} %shard_map.213.refs_4_), channel_id=1, source_target_pairs={{0,4},{4,8},{8,12},{12,0},{1,5},{5,9},{9,13},{13,1},{2,6},{6,10},{... | collective-permute-start | bytes 1179656 | tf_op jit(solution)/shard_map/ppermute | solution.py:376
  206.5 14.5 %collective-permute-start.26 = (bf16[1,1536,128]{2,1,0:T(8,128)(2,1)S(1)}, bf16[1,1536,128]{2,1,0:T(8,128)(2,1)S(1)}, u32[]{:S(2)}, u32[]{:S(2)}) collective-permute-start(bf16[1,1536,128]{2,1,0:T(8,128)(2,1)S(1)} %shard_map.216.refs_6_), channel_id=1, source_target_pairs={{0,4},{4,8},{8,12},{12,0},{1,5},{5,9},{9,13},{13,1},{2,6},{6,10},{... | collective-permute-start | bytes 1179656 | tf_op jit(solution)/shard_map/ppermute | solution.py:376
  224.0 22.4 %copy-start.88 = (bf16[4,1024,128]{2,1,0:T(8,128)(2,1)}, bf16[4,1024,128]{2,1,0:T(8,128)(2,1)S(1)}, u32[]{:S(2)}) copy-start(bf16[4,1024,128]{2,1,0:T(8,128)(2,1)S(1)} %get-tuple-element.92.refs_4_.refs_1_) | copy-start | bytes 3145732
  224.0 22.4 %collective-permute-start.27 = (bf16[4,1024,128]{2,1,0:T(8,128)(2,1)S(1)}, bf16[4,1024,128]{2,1,0:T(8,128)(2,1)S(1)}, u32[]{:S(2)}, u32[]{:S(2)}) collective-permute-start(bf16[4,1024,128]{2,1,0:T(8,128)(2,1)S(1)} %get-tuple-element.93), channel_id=1, source_target_pairs={{0,1},{1,0},{2,3},{3,2},{4,5},{5,4},{6,7},{7,6},{8,9},{9,8},{10,11... | collective-permute-start | bytes 3145736 | tf_op jit(solution)/shard_map/ppermute | solution.py:103
  224.1 22.1 %collective-permute-start.28 = (bf16[1,1536,128]{2,1,0:T(8,128)(2,1)S(1)}, bf16[1,1536,128]{2,1,0:T(8,128)(2,1)S(1)}, u32[]{:S(2)}, u32[]{:S(2)}) collective-permute-start(bf16[1,1536,128]{2,1,0:T(8,128)(2,1)S(1)} %shard_map.219.refs_4_), channel_id=1, source_target_pairs={{0,4},{4,8},{8,12},{12,0},{1,5},{5,9},{9,13},{13,1},{2,6},{6,10},{... | collective-permute-start | bytes 1179656 | tf_op jit(solution)/shard_map/ppermute | solution.py:376
  224.2 23.2 %collective-permute-start.18 = (bf16[256,1024]{1,0:T(8,128)(2,1)S(1)}, bf16[256,1024]{1,0:T(8,128)(2,1)S(1)}, u32[]{:S(2)}, u32[]{:S(2)}) collective-permute-start(bf16[256,1024]{1,0:T(8,128)(2,1)S(1)} %copy-done.45), channel_id=1, source_target_pairs={{0,2},{1,3},{2,0},{3,1},{4,6},{5,7},{6,4},{7,5},{8,10},{9,11},{10,... | collective-permute-start | bytes 1572872 | tf_op jit(solution)/shard_map/ppermute | solution.py:103
  226.9 23.7 %collective-permute-start.24 = (bf16[256,1024]{1,0:T(8,128)(2,1)S(1)}, bf16[256,1024]{1,0:T(8,128)(2,1)S(1)}, u32[]{:S(2)}, u32[]{:S(2)}) collective-permute-start(bf16[256,1024]{1,0:T(8,128)(2,1)S(1)} %copy-done.51), channel_id=1, source_target_pairs={{0,2},{1,3},{2,0},{3,1},{4,6},{5,7},{6,4},{7,5},{8,10},{9,11},{10,... | collective-permute-start | bytes 1572872 | tf_op jit(solution)/shard_map/ppermute | solution.py:103
  247.4 24.0 %copy-start.25 = (bf16[4,1024,128]{2,1,0:T(8,128)(2,1)S(1)}, bf16[4,1024,128]{2,1,0:T(8,128)(2,1)}, u32[]{:S(2)}) copy-start(bf16[4,1024,128]{2,1,0:T(8,128)(2,1)} %copy-done.24) | copy-start | bytes 3145732
  254.3 20.7 %collective-permute-start.29 = (bf16[4,128,1024]{2,1,0:T(8,128)(2,1)}, bf16[4,128,1024]{2,1,0:T(8,128)(2,1)S(1)}, u32[]{:S(2)}, u32[]{:S(2)}) collective-permute-start(bf16[4,128,1024]{2,1,0:T(8,128)(2,1)} %bitcast.10), channel_id=1, source_target_pairs={{0,1},{1,0},{2,3},{3,2},{4,5},{5,4},{6,7},{7,6},{8,9},{9,8},{10,11... | collective-permute-start | bytes 3145736 | tf_op jit(solution)/shard_map/ppermute | solution.py:103
  254.3 16.5 %collective-permute-start.30 = (bf16[1,1024,128]{2,1,0:T(8,128)(2,1)S(1)}, bf16[1,1024,128]{2,1,0:T(8,128)(2,1)S(1)}, u32[]{:S(2)}, u32[]{:S(2)}) collective-permute-start(bf16[1,1024,128]{2,1,0:T(8,128)(2,1)S(1)} %shard_map.222.refs_4_), channel_id=1, source_target_pairs={{0,4},{4,8},{8,12},{12,0},{1,5},{5,9},{9,13},{13,1},{2,6},{6,10},{... | collective-permute-start | bytes 786440 | tf_op jit(solution)/shard_map/ppermute | solution.py:376
  254.3 22.4 %collective-permute-start.23 = (bf16[256,256]{1,0:T(8,128)(2,1)S(1)}, bf16[256,256]{1,0:T(8,128)(2,1)S(1)}, u32[]{:S(2)}, u32[]{:S(2)}) collective-permute-start(bf16[256,256]{1,0:T(8,128)(2,1)S(1)} %shard_map.217.refs_1_.refs_5_.refs_2_), channel_id=1, source_target_pairs={{0,2},{1,3},{2,0},{3,1},{4,6},{5,7},{6,4},{7,5},{8,10},{9,11},{10,... | collective-permute-start | bytes 393224 | tf_op jit(solution)/shard_map/ppermute | solution.py:103
  256.0 25.5 %collective-permute-start.32 = (bf16[256,2048]{1,0:T(8,128)(2,1)}, bf16[256,2048]{1,0:T(8,128)(2,1)S(1)}, u32[]{:S(2)}, u32[]{:S(2)}) collective-permute-start(bf16[256,2048]{1,0:T(8,128)(2,1)} %copy-done.29), channel_id=1, source_target_pairs={{0,16},{16,0},{1,17},{17,1},{2,18},{18,2},{3,19},{19,3},{4,20},{20... | collective-permute-start | bytes 3145736 | tf_op jit(solution)/shard_map/ppermute | solution.py:103
  284.7 3.7 %collective-permute-start.40 = (f32[2,4,128]{2,1,0:T(4,128)S(1)}, f32[2,4,128]{2,1,0:T(4,128)S(1)}, u32[]{:S(2)}, u32[]{:S(2)}) collective-permute-start(f32[2,4,128]{2,1,0:T(4,128)S(1)} %bitcast.82), channel_id=1, source_target_pairs={{0,2},{1,3},{2,0},{3,1},{4,6},{5,7},{6,4},{7,5},{8,10},{9,11},{10,... | collective-permute-start | bytes 12296 | tf_op jit(solution)/shard_map/ppermute | solution.py:103
  285.0 3.3 collective-permute-start.39
  285.0 3.3 collective-permute-start.41
  286.9 38.5 %collective-permute-start.17 = (bf16[256,2048]{1,0:T(8,128)(2,1)S(1)}, bf16[256,2048]{1,0:T(8,128)(2,1)S(1)}, u32[]{:S(2)}, u32[]{:S(2)}) collective-permute-start(bf16[256,2048]{1,0:T(8,128)(2,1)S(1)} %copy-done.21), channel_id=1, source_target_pairs={{0,16},{16,0},{1,17},{17,1},{2,18},{18,2},{3,19},{19,3},{4,20},{20... | collective-permute-start | bytes 3145736 | tf_op jit(solution)/shard_map/ppermute | solution.py:103
  288.4 7.2 %collective-permute-start.44 = (f32[2,128]{1,0:T(2,128)S(1)}, f32[2,128]{1,0:T(2,128)S(1)}, u32[]{:S(2)}, u32[]{:S(2)}) collective-permute-start(f32[2,128]{1,0:T(2,128)S(1)} %bitcast.88), channel_id=1, source_target_pairs={{0,12},{4,8},{8,4},{12,0},{1,13},{5,9},{9,5},{13,1},{2,14},{6,10},... | collective-permute-start | bytes 3080 | tf_op jit(solution)/shard_map/ppermute | solution.py:103
  292.0 5.5 %collective-permute-start.42 = (f32[2,128]{1,0:T(2,128)S(1)}, f32[2,128]{1,0:T(2,128)S(1)}, u32[]{:S(2)}, u32[]{:S(2)}) collective-permute-start(f32[2,128]{1,0:T(2,128)S(1)} %bitcast.87), channel_id=1, source_target_pairs={{0,4},{4,0},{8,12},{12,8},{1,5},{5,1},{9,13},{13,9},{2,6},{6,2},{1... | collective-permute-start | bytes 3080 | tf_op jit(solution)/shard_map/ppermute | solution.py:103
  292.9 4.7 %collective-permute-start.43 = (f32[2,128]{1,0:T(2,128)S(1)}, f32[2,128]{1,0:T(2,128)S(1)}, u32[]{:S(2)}, u32[]{:S(2)}) collective-permute-start(f32[2,128]{1,0:T(2,128)S(1)} %bitcast.86), channel_id=1, source_target_pairs={{0,8},{4,12},{8,0},{12,4},{1,9},{5,13},{9,1},{13,5},{2,10},{6,14},... | collective-permute-start | bytes 3080 | tf_op jit(solution)/shard_map/ppermute | solution.py:103
  294.1 11.0 %collective-permute-start.35 = (bf16[1,1024,128]{2,1,0:T(8,128)(2,1)S(1)}, bf16[1,1024,128]{2,1,0:T(8,128)(2,1)S(1)}, u32[]{:S(2)}, u32[]{:S(2)}) collective-permute-start(bf16[1,1024,128]{2,1,0:T(8,128)(2,1)S(1)} %shard_map.224.refs_3_), channel_id=1, source_target_pairs={{0,4},{4,8},{8,12},{12,0},{1,5},{5,9},{9,13},{13,1},{2,6},{6,10},{... | collective-permute-start | bytes 786440 | tf_op jit(solution)/shard_map/ppermute | solution.py:376
  295.6 15.1 %collective-permute-start.34 = (bf16[1,128,1024]{2,1,0:T(8,128)(2,1)S(1)}, bf16[1,128,1024]{2,1,0:T(8,128)(2,1)S(1)}, u32[]{:S(2)}, u32[]{:S(2)}) collective-permute-start(bf16[1,128,1024]{2,1,0:T(8,128)(2,1)S(1)} %shard_map.225.refs_4_), channel_id=1, source_target_pairs={{0,4},{4,8},{8,12},{12,0},{1,5},{5,9},{9,13},{13,1},{2,6},{6,10},{... | collective-permute-start | bytes 786440 | tf_op jit(solution)/shard_map/ppermute | solution.py:376
  297.6 1.5 collective-permute-start.31
  299.2 12.9 %collective-permute-start.33 = (bf16[1,128,256]{2,1,0:T(8,128)(2,1)S(1)}, bf16[1,128,256]{2,1,0:T(8,128)(2,1)S(1)}, u32[]{:S(2)}, u32[]{:S(2)}) collective-permute-start(bf16[1,128,256]{2,1,0:T(8,128)(2,1)S(1)} %shard_map.228.refs_4_), channel_id=1, source_target_pairs={{0,4},{4,8},{8,12},{12,0},{1,5},{5,9},{9,13},{13,1},{2,6},{6,10},{... | collective-permute-start | bytes 196616 | tf_op jit(solution)/shard_map/ppermute | solution.py:376
  305.2 12.5 %collective-permute-start.38 = (bf16[1,1024,128]{2,1,0:T(8,128)(2,1)S(1)}, bf16[1,1024,128]{2,1,0:T(8,128)(2,1)S(1)}, u32[]{:S(2)}, u32[]{:S(2)}) collective-permute-start(bf16[1,1024,128]{2,1,0:T(8,128)(2,1)S(1)} %shard_map.229.refs_4_), channel_id=1, source_target_pairs={{0,4},{4,8},{8,12},{12,0},{1,5},{5,9},{9,13},{13,1},{2,6},{6,10},{... | collective-permute-start | bytes 786440 | tf_op jit(solution)/shard_map/ppermute | solution.py:376
  310.8 12.0 %collective-permute-start.37 = (bf16[1,128,1024]{2,1,0:T(8,128)(2,1)S(1)}, bf16[1,128,1024]{2,1,0:T(8,128)(2,1)S(1)}, u32[]{:S(2)}, u32[]{:S(2)}) collective-permute-start(bf16[1,128,1024]{2,1,0:T(8,128)(2,1)S(1)} %shard_map.230.refs_4_), channel_id=1, source_target_pairs={{0,4},{4,8},{8,12},{12,0},{1,5},{5,9},{9,13},{13,1},{2,6},{6,10},{... | collective-permute-start | bytes 786440 | tf_op jit(solution)/shard_map/ppermute | solution.py:376
  312.1 11.9 %collective-permute-start.36 = (bf16[1,128,256]{2,1,0:T(8,128)(2,1)S(1)}, bf16[1,128,256]{2,1,0:T(8,128)(2,1)S(1)}, u32[]{:S(2)}, u32[]{:S(2)}) collective-permute-start(bf16[1,128,256]{2,1,0:T(8,128)(2,1)S(1)} %shard_map.231.refs_4_), channel_id=1, source_target_pairs={{0,4},{4,8},{8,12},{12,0},{1,5},{5,9},{9,13},{13,1},{2,6},{6,10},{... | collective-permute-start | bytes 196616 | tf_op jit(solution)/shard_map/ppermute | solution.py:376
  323.9 11.7 %collective-permute-start.45 = (bf16[1,128,1024]{2,1,0:T(8,128)(2,1)S(1)}, bf16[1,128,1024]{2,1,0:T(8,128)(2,1)S(1)}, u32[]{:S(2)}, u32[]{:S(2)}) collective-permute-start(bf16[1,128,1024]{2,1,0:T(8,128)(2,1)S(1)} %shard_map.233.refs_4_), channel_id=1, source_target_pairs={{0,4},{4,8},{8,12},{12,0},{1,5},{5,9},{9,13},{13,1},{2,6},{6,10},{... | collective-permute-start | bytes 786440 | tf_op jit(solution)/shard_map/ppermute | solution.py:376
  324.1 9.5 %collective-permute-start.46 = (bf16[1,128,256]{2,1,0:T(8,128)(2,1)S(1)}, bf16[1,128,256]{2,1,0:T(8,128)(2,1)S(1)}, u32[]{:S(2)}, u32[]{:S(2)}) collective-permute-start(bf16[1,128,256]{2,1,0:T(8,128)(2,1)S(1)} %shard_map.234.refs_3_), channel_id=1, source_target_pairs={{0,4},{4,8},{8,12},{12,0},{1,5},{5,9},{9,13},{13,1},{2,6},{6,10},{... | collective-permute-start | bytes 196616 | tf_op jit(solution)/shard_map/ppermute | solution.py:376
  (101 other events, 461.9 us)
Sparse Core Ops, SparseCore 0:
  134.5 73.0 reduce-scatter.2
  209.9 83.2 reduce-scatter.4

commit v4 on v3

--- a/solution.py
+++ b/solution.py
@@ -448,6 +448,37 @@
         bias_ref[k * tokens : (k + 1) * tokens, :] = jnp.where(allowed, 0.0, NEG_FILL)
 
 
+def write_triangle(bias_ref):
+    key = lax.broadcasted_iota(jnp.int32, bias_ref.shape, 0)
+    query = lax.broadcasted_iota(jnp.int32, bias_ref.shape, 1)
+    bias_ref[...] = jnp.where(key <= query, 0.0, NEG_FILL)
+
+
+def widened_keys(here, k, keys):
+    lane = lax.broadcasted_iota(jnp.int32, (keys.shape[0], LANES), 1)
+    fill = jnp.where((here ^ k) > here, NEG_FILL, 0.0)
+    wide = jnp.concatenate([keys.astype(F32), jnp.zeros_like(keys, F32)], axis=1)
+    return jnp.where(lane == HEAD_WIDTH, fill, wide).astype(BF16)
+
+
+def widened_query(q_ref, h):
+    start = h * HEAD_WIDTH // LANES * LANES
+    pair = q_ref[:, start : start + LANES].astype(F32)
+    if h * HEAD_WIDTH != start:
+        pair = pltpu.roll(pair, LANES - HEAD_WIDTH, 1)
+    lane = lax.broadcasted_iota(jnp.int32, pair.shape, 1)
+    return jnp.where(
+        lane < HEAD_WIDTH, pair, jnp.where(lane == HEAD_WIDTH, 1.0, 0.0)
+    ).astype(BF16)
+
+
+def piece_scores(keys, query, bias_ref, count):
+    tokens = bias_ref.shape[0]
+    scores = [dot_nt(keys[k * tokens : (k + 1) * tokens], query) for k in range(count)]
+    scores[0] += bias_ref[...]
+    return scores
+
+
 def attend_kernel(count, kv_heads, group_blocks, here_ref, *refs):
     q_ref, kv_refs, weight_ref = refs[0], refs[1 : 1 + count], refs[1 + count]
     attn_ref, lse_ref, proj_ref, key_ref, turned_ref, bias_ref, total_ref = refs[2 + count :]
@@ -456,13 +487,13 @@
 
     @pl.when(step == 0)
     def _():
-        write_bias(here_ref[0], bias_ref, count)
+        write_triangle(bias_ref)
         for k in range(count):
             rows = slice(k * tokens, (k + 1) * tokens)
             values_t = kv_refs[k][:, kv_heads * HEAD_WIDTH :].T
             for g in range(kv_heads):
                 cut = slice(g * HEAD_WIDTH, (g + 1) * HEAD_WIDTH)
-                key_ref[g, rows, :] = kv_refs[k][:, cut]
+                key_ref[g, rows, :] = widened_keys(here_ref[0], k, kv_refs[k][:, cut])
                 turned_ref[g, :, rows] = values_t[cut, :]
 
     group = step // group_blocks
@@ -470,12 +501,18 @@
     heads = q_ref.shape[1] // HEAD_WIDTH
     outs = []
     for h in range(heads):
-        query = q_ref[:, h * HEAD_WIDTH : (h + 1) * HEAD_WIDTH]
-        scores = dot_nt(keys, query) + bias_ref[...]
-        top = jnp.max(scores, axis=0, keepdims=True)
-        expo = jnp.exp(scores - top)
-        total = jnp.sum(expo, axis=0, keepdims=True)
-        outs.append(dot_nn(values_t, expo.astype(BF16)) / total)
+        query = widened_query(q_ref, h)
+        scores = piece_scores(keys, query, bias_ref, count)
+        top = scores[0]
+        for piece in scores[1:]:
+            top = jnp.maximum(top, piece)
+        top = jnp.max(top, axis=0, keepdims=True)
+        total, out = jnp.zeros((1, tokens), F32), jnp.zeros((HEAD_WIDTH, tokens), F32)
+        for k, piece in enumerate(scores):
+            expo = jnp.exp(piece - top)
+            total += jnp.sum(expo, axis=0, keepdims=True)
+            out += dot_nn(values_t[:, k * tokens : (k + 1) * tokens], expo.astype(BF16))
+        outs.append(out / total)
         lse_ref[0, h : h + 1, :] = top + jnp.log(total)
     attn_ref[...] = jnp.concatenate(outs, axis=0).T.astype(BF16)
     term = dot_nn(attn_ref[...], weight_ref[...])
@@ -519,9 +556,9 @@
             whole((tokens, width)),
         ],
         scratch=[
-            pltpu.VMEM((kv_heads, count * tokens, HEAD_WIDTH), BF16),
+            pltpu.VMEM((kv_heads, count * tokens, LANES), BF16),
             pltpu.VMEM((kv_heads, HEAD_WIDTH, count * tokens), BF16),
-            pltpu.VMEM((count * tokens, tokens), F32),
+            pltpu.VMEM((tokens, tokens), F32),
             pltpu.VMEM((tokens, width), F32),
         ],
         scalars=1,

time: 346 us -> 344 us (level)
  no operation moved by 1% of the time
where the time goes in v4:
time: 344 us; the launch traced here: 342 us
  Pallas kernels  123 us (36%)
  waiting for transfers between devices  115 us (33%)
  local copies, waits for them, and re-layouts  47.1 us (14%)
  starting transfers between devices  40.3 us (12%)
  between operations  15.3 us (4%)
    pallas_call x45, Pallas kernels, __call__(): pl.pallas_call(stripped, out_shape=out_shape + [shaped(c.shape, c.dtype)...  123 us
    ppermute x15, waiting for transfers between devices, step(): self.arrived = lax.ppermute(total, 'dp', ring)  74.5 us
    unnamed x233, local copies, waits for them, and re-layouts  45.9 us
    ppermute x32, waiting for transfers between devices, swap(): return lax.ppermute(value, axis, [(i, i ^ flip) for i in range(count)])  40.2 us
    ppermute x32, starting transfers between devices, swap(): return lax.ppermute(value, axis, [(i, i ^ flip) for i in range(count)])  28.5 us
    ppermute x15, starting transfers between devices, step(): self.arrived = lax.ppermute(total, 'dp', ring)  11.7 us
  transfers between devices with their start and end apart: 49, of which 22 were waited for; matrix products, arithmetic and copies ran while one was open for 1% of the time, Pallas kernels for 32%

profile of v4, /device:TPU:0, one launch (start us, length us, event | category | flops | bytes accessed | tf_op | source)
XLA Modules:
  0.0 342.4 jit_solution(2441476296626756664)
XLA Ops:
  8.1 1.3 copy-done.17
  13.2 2.5 collective-permute-start.2
  16.4 3.0 shard_map.195.refs_2_.refs_1_
  20.5 2.0 collective-permute-done.1.refs_4_.refs_10_
  22.6 12.4 %shard_map.197 = (bf16[256,1024]{1,0:T(8,128)(2,1)S(1)}, f32[4,4,256]{2,1,0:T(4,128)S(1)}, bf16[256,2048]{1,0:T(8,128)(2,1)S(1)}) custom-call(s32[1]{0:T(128)} %bitcast.refs_0_, bf16[256,1024]{1,0:T(8,128)(2,1)S(1)} %shard_map.195.refs_2_.refs_1_, bf16[256,256]{1,0:T(8,128)(2,1)S(1)} %get-tuple-element.58.refs_2_.refs_8_, ...), custom_call_target="tpu_custom_call" | custom-call | flops 46200000512 | bytes 1000 | tf_op jit(solution)/shard_map/pallas_call | solution.py:81
  36.4 2.3 collective-permute-start.3
  38.7 1.5 collective-permute-start.4
  40.7 13.1 %collective-permute-done.4.refs_4_.refs_1_ = bf16[256,1024]{1,0:T(8,128)(2,1)} collective-permute-done((bf16[256,1024]{1,0:T(8,128)(2,1)}, bf16[256,1024]{1,0:T(8,128)(2,1)}, u32[]{:S(2)}, u32[]{:S(2)}) %collective-permute-start.4) | collective-permute-done | bytes 524320 | tf_op jit(solution)/shard_map/ppermute | solution.py:103
  58.3 3.8 %collective-permute-done.3.refs_3_ = bf16[256,2048]{1,0:T(8,128)(2,1)S(1)} collective-permute-done((bf16[256,2048]{1,0:T(8,128)(2,1)S(1)}, bf16[256,2048]{1,0:T(8,128)(2,1)S(1)}, u32[]{:S(2)}, u32[]{:S(2)}) %collective-permute-start.3) | collective-permute-done | bytes 1048608 | tf_op jit(solution)/shard_map/ppermute | solution.py:103
  62.1 1.4 copy-done.28
  64.8 1.9 collective-permute-start.5
  66.7 8.8 %shard_map.200 = (bf16[256,1280]{1,0:T(8,128)(2,1)S(1)}, bf16[256,2560]{1,0:T(8,128)(2,1)}) custom-call(bf16[256,2048]{1,0:T(8,128)(2,1)S(1)} %get-tuple-element.65.refs_0_, bf16[256,2048]{1,0:T(8,128)(2,1)S(1)} %bitcast.55, bf16[2048,2816]{1,0:T(8,128)(2,1)S(1)} %bitcast.53, bf16[2048,2816]{1,0:T(8,128)(2,1)} %refs_2_.11, bf16[2816,2048]{1,0:T(8,128)(2,1)} %refs_2_.12, ...), custom_call_target="tpu_custom_call" | custom-call | flops 32999999488 | bytes 1000 | tf_op jit(solution)/shard_map/pallas_call | solution.py:81
  77.5 1.7 collective-permute-done.5.refs_7_.refs_1_
  79.2 10.2 %shard_map.201 = (bf16[256,1536]{1,0:T(8,128)(2,1)}, bf16[256,3072]{1,0:T(8,128)(2,1)S(1)}) custom-call(bf16[256,2048]{1,0:T(8,128)(2,1)S(1)} %get-tuple-element.65.refs_0_, bf16[256,2048]{1,0:T(8,128)(2,1)S(1)} %bitcast.56, bf16[2048,2816]{1,0:T(8,128)(2,1)S(1)} %bitcast.53, bf16[2048,2816]{1,0:T(8,128)(2,1)} %refs_2_.11, bf16[2816,2048]{1,0:T(8,128)(2,1)} %refs_2_.12, ...), custom_call_target="tpu_custom_call" | custom-call | flops 32999999488 | bytes 1000 | tf_op jit(solution)/shard_map/pallas_call | solution.py:81
  89.4 3.9 %collective-permute-done.7.refs_3_ = bf16[256,1280]{1,0:T(8,128)(2,1)S(1)} collective-permute-done((bf16[256,1280]{1,0:T(8,128)(2,1)S(1)}, bf16[256,1280]{1,0:T(8,128)(2,1)S(1)}, u32[]{:S(2)}, u32[]{:S(2)}) %collective-permute-start.7) | collective-permute-done | bytes 655392 | tf_op jit(solution)/shard_map/ppermute | solution.py:103
  93.3 3.6 %shard_map.202 = (bf16[4,1280,128]{2,1,0:T(8,128)(2,1)S(1)}, bf16[4,1280,128]{2,1,0:T(8,128)(2,1)S(1)}) custom-call(bf16[256,1024]{1,0:T(8,128)(2,1)S(1)} %copy-done.101, bf16[256,1024]{1,0:T(8,128)(2,1)} %collective-permute-done.4.refs_4_.refs_1_, bf16[256,1280]{1,0:T(8,128)(2,1)S(1)} %get-tuple-element.66.refs_5_.refs_2_.refs_0_, ...), custom_call_target="tpu_custom_call" | custom-call | flops 9900000256 | bytes 1000 | tf_op jit(solution)/shard_map/pallas_call | solution.py:81
  97.0 6.9 %shard_map.203 = (f32[256,2048]{1,0:T(8,128)S(1)}, bf16[256,1536]{1,0:T(8,128)(2,1)}, bf16[256,3072]{1,0:T(8,128)(2,1)S(1)}) custom-call(bf16[256,2560]{1,0:T(8,128)(2,1)} %get-tuple-element.67.refs_0_.refs_2_, bf16[2048,2816]{1,0:T(8,128)(2,1)S(1)} %bitcast.53, bf16[2048,2816]{1,0:T(8,128)(2,1)} %refs_2_.11, ...), custom_call_target="tpu_custom_call", output_to_operand_aliasing={{1}: (3, {}), {2}: (4, {})} | custom-call | flops 23100000256 | bytes 1000 | tf_op jit(solution)/shard_map/pallas_call | solution.py:81
  103.9 2.1 collective-permute-start.10
  106.2 1.8 collective-permute-start.11
  108.0 4.3 %copy-done.9 = bf16[2048,2816]{1,0:T(8,128)(2,1)S(1)} copy-done((bf16[2048,2816]{1,0:T(8,128)(2,1)S(1)}, bf16[2048,2816]{1,0:T(8,128)(2,1)}, u32[]{:S(2)}) %copy-start.9) | copy-done | bytes 11534360
  112.2 8.4 %shard_map.205 = (bf16[256,2048]{1,0:T(8,128)(2,1)}, bf16[256,3072]{1,0:T(8,128)(2,1)S(1)}) custom-call(bf16[256,3072]{1,0:T(8,128)(2,1)S(1)} %get-tuple-element.74.refs_0_, bf16[2048,2816]{1,0:T(8,128)(2,1)S(1)} %copy-done.9, bf16[2048,2816]{1,0:T(8,128)(2,1)} %refs_2_.11, ...), custom_call_target="tpu_custom_call", output_to_operand_aliasing={{1}: (4, {})} | custom-call | flops 26400000000 | bytes 1000 | tf_op jit(solution)/shard_map/pallas_call | solution.py:81
  120.6 1.5 collective-permute-start.15
  122.3 1.7 collective-permute-start.12
  123.9 5.8 %shard_map.207.refs_4_ = bf16[4,2,128,2560]{3,2,1,0:T(8,128)(2,1)S(1)} custom-call(bf16[256,1024]{1,0:T(8,128)(2,1)S(1)} %get-tuple-element.68.refs_6_.refs_0_, bf16[256,1024]{1,0:T(8,128)(2,1)S(1)} %collective-permute-done.5.refs_7_.refs_1_, bf16[256,2560]{1,0:T(8,128)(2,1)} %get-tuple-element.67.refs_0_.refs_2_, ...), custom_call_target="tpu_custom_call" | custom-call | flops 16499999744 | bytes 1000 | tf_op jit(solution)/shard_map/pallas_call | solution.py:81
  129.7 2.4 copy-done.1
  133.0 2.5 copy-done.2
  135.5 1.3 copy-done.81
  137.8 7.8 %collective-permute-done.15.refs_3_ = bf16[256,2048]{1,0:T(8,128)(2,1)} collective-permute-done((bf16[256,2048]{1,0:T(8,128)(2,1)}, bf16[256,2048]{1,0:T(8,128)(2,1)}, u32[]{:S(2)}, u32[]{:S(2)}) %collective-permute-start.15) | collective-permute-done | bytes 1048608 | tf_op jit(solution)/shard_map/ppermute | solution.py:103
  145.6 4.7 %shard_map.209 = (f32[256,2048]{1,0:T(8,128)S(1)}, bf16[256,2048]{1,0:T(8,128)(2,1)S(1)}, f32[1,2048]{1,0:T(1,128)S(1)}, bf16[256,1024]{1,0:T(8,128)(2,1)S(1)}, bf16[256,1024]{1,0:T(8,128)(2,1)}) custom-call(s32[1]{0:T(128)} %bitcast.refs_0_, bf16[256,2048]{1,0:T(8,128)(2,1)S(1)} %bitcast.57, bf16[256,2048]{1,0:T(8,128)(2,1)} %get-tuple-element.78.refs_4_.refs_2_, ...), custom_call_target="tpu_custom_call" | custom-call | flops 13200000000 | bytes 1000 | tf_op jit(solution)/shard_map/pallas_call | solution.py:81
  151.4 2.5 collective-permute-done.14.refs_3_
  155.0 4.6 %shard_map.211 = (bf16[4,1536,128]{2,1,0:T(8,128)(2,1)S(1)}, bf16[4,1536,128]{2,1,0:T(8,128)(2,1)S(1)}) custom-call(bf16[256,1024]{1,0:T(8,128)(2,1)S(1)} %copy-done.102, bf16[256,1024]{1,0:T(8,128)(2,1)} %collective-permute-done.4.refs_4_.refs_1_, bf16[256,1536]{1,0:T(8,128)(2,1)} %get-tuple-element.73.refs_2_.refs_1_, ...), custom_call_target="tpu_custom_call" | custom-call | flops 9900000256 | bytes 1000 | tf_op jit(solution)/shard_map/pallas_call | solution.py:81
  159.9 16.4 %shard_map.212 = (bf16[256,1024]{1,0:T(8,128)(2,1)S(1)}, bf16[256,256]{1,0:T(8,128)(2,1)S(1)}, bf16[256,256]{1,0:T(8,128)(2,1)}, bf16[256,256]{1,0:T(8,128)(2,1)}, bf16[256,256]{1,0:T(8,128)(2,1)S(1)}) custom-call(s32[1]{0:T(128)} %bitcast.refs_0_, bf16[256,1024]{1,0:T(8,128)(2,1)S(1)} %copy-done.104, bf16[256,1024]{1,0:T(8,128)(2,1)S(1)} %copy-done.42, ...), custom_call_target="tpu_custom_call" | custom-call | flops 52800000000 | bytes 1000 | tf_op jit(solution)/shard_map/pallas_call | solution.py:81
  176.8 1.8 collective-permute-start.20
  180.1 6.4 %shard_map.214.refs_3_ = bf16[4,2,128,3072]{3,2,1,0:T(8,128)(2,1)S(1)} custom-call(bf16[256,1024]{1,0:T(8,128)(2,1)S(1)} %copy-done.106, bf16[256,1024]{1,0:T(8,128)(2,1)S(1)} %copy-done.49, bf16[256,3072]{1,0:T(8,128)(2,1)S(1)} %get-tuple-element.77.refs_2_, bf16[256,3072]{1,0:T(8,128)(2,1)} %collective-permute-done.9.refs_3_, ...), custom_call_target="tpu_custom_call" | custom-call | flops 16499999744 | bytes 1000 | tf_op jit(solution)/shard_map/pallas_call | solution.py:81
  186.5 4.3 %copy-done.10 = bf16[2816,2048]{1,0:T(8,128)(2,1)S(1)} copy-done((bf16[2816,2048]{1,0:T(8,128)(2,1)S(1)}, bf16[2816,2048]{1,0:T(8,128)(2,1)}, u32[]{:S(2)}) %copy-start.10) | copy-done | bytes 11534360
  190.9 7.2 %shard_map.215.refs_4_.refs_1_ = bf16[256,2048]{1,0:T(8,128)(2,1)S(1)} custom-call(bf16[256,1280]{1,0:T(8,128)(2,1)S(1)} %copy-done.34, bf16[256,1536]{1,0:T(8,128)(2,1)} %get-tuple-element.73.refs_2_.refs_1_, bf16[2816,2048]{1,0:T(8,128)(2,1)S(1)} %copy-done.10, bf16[4,2,128,3072]{3,2,1,0:T(8,128)(2,1)S(1)} %shard_map.214.refs_3_), custom_call_target="tpu_custom_call" | custom-call | flops 26400000000 | bytes 1000 | tf_op jit(solution)/shard_map/pallas_call | solution.py:81
  198.1 4.1 %collective-permute-done.22.refs_3_ = bf16[1,1536,128]{2,1,0:T(8,128)(2,1)} collective-permute-done((bf16[1,1536,128]{2,1,0:T(8,128)(2,1)}, bf16[1,1536,128]{2,1,0:T(8,128)(2,1)}, u32[]{:S(2)}, u32[]{:S(2)}) %collective-permute-start.22) | collective-permute-done | bytes 393248 | tf_op jit(solution)/shard_map/ppermute | solution.py:376
  202.1 1.4 copy-done.86
  204.9 1.4 shard_map.217.refs_1_.refs_5_.refs_2_
  207.7 2.3 shard_map.218.refs_4_.refs_0_
  210.1 10.2 %collective-permute-done.26.refs_3_ = bf16[1,1536,128]{2,1,0:T(8,128)(2,1)S(1)} collective-permute-done((bf16[1,1536,128]{2,1,0:T(8,128)(2,1)S(1)}, bf16[1,1536,128]{2,1,0:T(8,128)(2,1)S(1)}, u32[]{:S(2)}, u32[]{:S(2)}) %collective-permute-start.26) | collective-permute-done | bytes 393248 | tf_op jit(solution)/shard_map/ppermute | solution.py:376
  220.5 2.8 shard_map.220
  223.4 2.0 collective-permute-start.18
  225.5 20.0 %collective-permute-done.28.refs_3_ = bf16[1,1536,128]{2,1,0:T(8,128)(2,1)S(1)} collective-permute-done((bf16[1,1536,128]{2,1,0:T(8,128)(2,1)S(1)}, bf16[1,1536,128]{2,1,0:T(8,128)(2,1)S(1)}, u32[]{:S(2)}, u32[]{:S(2)}) %collective-permute-start.28) | collective-permute-done | bytes 393248 | tf_op jit(solution)/shard_map/ppermute | solution.py:376
  246.6 2.4 collective-permute-done.24.refs_3_
  249.0 2.7 shard_map.223
  252.7 1.7 collective-permute-start.23
  254.5 14.7 %collective-permute-done.30.refs_3_ = bf16[1,1024,128]{2,1,0:T(8,128)(2,1)S(1)} collective-permute-done((bf16[1,1024,128]{2,1,0:T(8,128)(2,1)S(1)}, bf16[1,1024,128]{2,1,0:T(8,128)(2,1)S(1)}, u32[]{:S(2)}, u32[]{:S(2)}) %collective-permute-start.30) | collective-permute-done | bytes 262176 | tf_op jit(solution)/shard_map/ppermute | solution.py:376
  273.5 1.5 copy-done.71
  276.7 3.3 collective-permute-done.32.refs_1_
  280.0 3.1 shard_map.227
  283.5 1.9 collective-permute-start.41
  286.9 3.6 %collective-permute-start.44 = (f32[2,128]{1,0:T(2,128)S(1)}, f32[2,128]{1,0:T(2,128)S(1)}, u32[]{:S(2)}, u32[]{:S(2)}) collective-permute-start(f32[2,128]{1,0:T(2,128)S(1)} %bitcast.88), channel_id=1, source_target_pairs={{0,12},{4,8},{8,4},{12,0},{1,13},{5,9},{9,5},{13,1},{2,14},{6,10},... | collective-permute-start | bytes 3080 | tf_op jit(solution)/shard_map/ppermute | solution.py:103
  292.5 1.5 collective-permute-start.35
  294.1 1.9 collective-permute-start.34
  298.9 4.7 %collective-permute-done.35.refs_3_ = bf16[1,1024,128]{2,1,0:T(8,128)(2,1)S(1)} collective-permute-done((bf16[1,1024,128]{2,1,0:T(8,128)(2,1)S(1)}, bf16[1,1024,128]{2,1,0:T(8,128)(2,1)S(1)}, u32[]{:S(2)}, u32[]{:S(2)}) %collective-permute-start.35) | collective-permute-done | bytes 262176 | tf_op jit(solution)/shard_map/ppermute | solution.py:376
  303.7 5.4 %collective-permute-done.34.refs_3_ = bf16[1,128,1024]{2,1,0:T(8,128)(2,1)S(1)} collective-permute-done((bf16[1,128,1024]{2,1,0:T(8,128)(2,1)S(1)}, bf16[1,128,1024]{2,1,0:T(8,128)(2,1)S(1)}, u32[]{:S(2)}, u32[]{:S(2)}) %collective-permute-start.34) | collective-permute-done | bytes 262176 | tf_op jit(solution)/shard_map/ppermute | solution.py:376
  311.1 5.0 %collective-permute-done.38.refs_3_ = bf16[1,1024,128]{2,1,0:T(8,128)(2,1)S(1)} collective-permute-done((bf16[1,1024,128]{2,1,0:T(8,128)(2,1)S(1)}, bf16[1,1024,128]{2,1,0:T(8,128)(2,1)S(1)}, u32[]{:S(2)}, u32[]{:S(2)}) %collective-permute-start.38) | collective-permute-done | bytes 262176 | tf_op jit(solution)/shard_map/ppermute | solution.py:376
  317.1 4.2 %collective-permute-done.37.refs_3_ = bf16[1,128,1024]{2,1,0:T(8,128)(2,1)S(1)} collective-permute-done((bf16[1,128,1024]{2,1,0:T(8,128)(2,1)S(1)}, bf16[1,128,1024]{2,1,0:T(8,128)(2,1)S(1)}, u32[]{:S(2)}, u32[]{:S(2)}) %collective-permute-start.37) | collective-permute-done | bytes 262176 | tf_op jit(solution)/shard_map/ppermute | solution.py:376
  322.5 1.3 collective-permute-start.46
  324.0 1.3 shard_map.235.refs_2_
  328.8 1.8 shard_map.236
  330.5 1.6 collective-permute-done.46.refs_3_
  332.1 1.4 copy-done.68
  (328 shorter events, 50.4 us)
Async XLA Ops:
  7.2 318.1 %reduce-scatter.3.cloned.1.call-start = ((), (), s32[]{:S(2)}) async-start(), calls=%async_computation.2 | async-start | bytes 5898240 | tf_op jit(solution)/shard_map/reduce_scatter | solution.py:281
  13.2 7.3 %collective-permute-start.2 = (bf16[256,256]{1,0:T(8,128)(2,1)S(1)}, bf16[256,256]{1,0:T(8,128)(2,1)S(1)}, u32[]{:S(2)}, u32[]{:S(2)}) collective-permute-start(bf16[256,256]{1,0:T(8,128)(2,1)S(1)} %get-tuple-element.58.refs_2_.refs_8_), channel_id=1, source_target_pairs={{0,3},{1,2},{2,1},{3,0},{4,7},{5,6},{6,5},{7,4},{8,11},{9,10},{10,... | collective-permute-start | bytes 393224 | tf_op jit(solution)/shard_map/ppermute | solution.py:103
  15.7 6.9 %collective-permute-start.1 = (bf16[256,256]{1,0:T(8,128)(2,1)S(1)}, bf16[256,256]{1,0:T(8,128)(2,1)S(1)}, u32[]{:S(2)}, u32[]{:S(2)}) collective-permute-start(bf16[256,256]{1,0:T(8,128)(2,1)S(1)} %get-tuple-element.58.refs_2_.refs_8_), channel_id=1, source_target_pairs={{0,2},{1,3},{2,0},{3,1},{4,6},{5,7},{6,4},{7,5},{8,10},{9,11},{10,... | collective-permute-start | bytes 393224 | tf_op jit(solution)/shard_map/ppermute | solution.py:103
  16.3 6.2 %collective-permute-start = (bf16[256,256]{1,0:T(8,128)(2,1)S(1)}, bf16[256,256]{1,0:T(8,128)(2,1)S(1)}, u32[]{:S(2)}, u32[]{:S(2)}) collective-permute-start(bf16[256,256]{1,0:T(8,128)(2,1)S(1)} %get-tuple-element.58.refs_2_.refs_8_), channel_id=1, source_target_pairs={{0,1},{1,0},{2,3},{3,2},{4,5},{5,4},{6,7},{7,6},{8,9},{9,8},{10,11... | collective-permute-start | bytes 393224 | tf_op jit(solution)/shard_map/ppermute | solution.py:103
  20.5 14.5 %copy-start.99 = (bf16[256,1024]{1,0:T(8,128)(2,1)}, bf16[256,1024]{1,0:T(8,128)(2,1)S(1)}, u32[]{:S(2)}) copy-start(bf16[256,1024]{1,0:T(8,128)(2,1)S(1)} %get-tuple-element.59.refs_7_.refs_3_.refs_0_) | copy-start | bytes 1572868
  20.5 14.5 %copy-start.58 = (bf16[256,256]{1,0:T(8,128)(2,1)}, bf16[256,256]{1,0:T(8,128)(2,1)S(1)}, u32[]{:S(2)}) copy-start(bf16[256,256]{1,0:T(8,128)(2,1)S(1)} %collective-permute-done.2.refs_5_.refs_11_) | copy-start | bytes 393220
  36.4 21.0 %copy-start.27 = (bf16[256,2048]{1,0:T(8,128)(2,1)}, bf16[256,2048]{1,0:T(8,128)(2,1)S(1)}, u32[]{:S(2)}) copy-start(bf16[256,2048]{1,0:T(8,128)(2,1)S(1)} %get-tuple-element.60.refs_2_) | copy-start | bytes 3145732
  36.4 25.6 %collective-permute-start.3 = (bf16[256,2048]{1,0:T(8,128)(2,1)S(1)}, bf16[256,2048]{1,0:T(8,128)(2,1)S(1)}, u32[]{:S(2)}, u32[]{:S(2)}) collective-permute-start(bf16[256,2048]{1,0:T(8,128)(2,1)S(1)} %get-tuple-element.60.refs_2_), channel_id=1, source_target_pairs={{0,16},{16,0},{1,17},{17,1},{2,18},{18,2},{3,19},{19,3},{4,20},{20... | collective-permute-start | bytes 3145736 | tf_op jit(solution)/shard_map/ppermute | solution.py:103
  38.7 15.1 %collective-permute-start.4 = (bf16[256,1024]{1,0:T(8,128)(2,1)}, bf16[256,1024]{1,0:T(8,128)(2,1)}, u32[]{:S(2)}, u32[]{:S(2)}) collective-permute-start(bf16[256,1024]{1,0:T(8,128)(2,1)} %get-tuple-element.62), channel_id=1, source_target_pairs={{0,2},{1,3},{2,0},{3,1},{4,6},{5,7},{6,4},{7,5},{8,10},{9,11},{10,... | collective-permute-start | bytes 1572872 | tf_op jit(solution)/shard_map/ppermute | solution.py:103
  40.2 21.8 %copy-start.18 = (bf16[256,1,2048]{2,0,1:T(8,128)(2,1)S(1)}, bf16[256,1,2048]{2,0,1:T(8,128)(2,1)}, u32[]{:S(2)}) copy-start(bf16[256,1,2048]{2,0,1:T(8,128)(2,1)} %param.11) | copy-start | bytes 3145732
  40.2 37.3 %collective-permute-start.6 = (bf16[256,1024]{1,0:T(8,128)(2,1)}, bf16[256,1024]{1,0:T(8,128)(2,1)S(1)}, u32[]{:S(2)}, u32[]{:S(2)}) collective-permute-start(bf16[256,1024]{1,0:T(8,128)(2,1)} %copy-done.39), channel_id=1, source_target_pairs={{0,2},{1,3},{2,0},{3,1},{4,6},{5,7},{6,4},{7,5},{8,10},{9,11},{10,... | collective-permute-start | bytes 1572872 | tf_op jit(solution)/shard_map/ppermute | solution.py:103
  64.8 59.2 %copy-start.105 = (bf16[256,1024]{1,0:T(8,128)(2,1)}, bf16[256,1024]{1,0:T(8,128)(2,1)S(1)}, u32[]{:S(2)}) copy-start(bf16[256,1024]{1,0:T(8,128)(2,1)S(1)} %get-tuple-element.68.refs_6_.refs_0_) | copy-start | bytes 1572868
  64.8 14.5 %collective-permute-start.5 = (bf16[256,1024]{1,0:T(8,128)(2,1)S(1)}, bf16[256,1024]{1,0:T(8,128)(2,1)S(1)}, u32[]{:S(2)}, u32[]{:S(2)}) collective-permute-start(bf16[256,1024]{1,0:T(8,128)(2,1)S(1)} %get-tuple-element.69), channel_id=1, source_target_pairs={{0,2},{1,3},{2,0},{3,1},{4,6},{5,7},{6,4},{7,5},{8,10},{9,11},{10,... | collective-permute-start | bytes 1572872 | tf_op jit(solution)/shard_map/ppermute | solution.py:103
  66.7 12.5 %copy-start.41 = (bf16[256,1024]{1,0:T(8,128)(2,1)S(1)}, bf16[256,1024]{1,0:T(8,128)(2,1)}, u32[]{:S(2)}) copy-start(bf16[256,1024]{1,0:T(8,128)(2,1)} %copy-done.39) | copy-start | bytes 1572868
  75.5 17.8 %copy-start.33 = (bf16[256,1280]{1,0:T(8,128)(2,1)}, bf16[256,1280]{1,0:T(8,128)(2,1)S(1)}, u32[]{:S(2)}) copy-start(bf16[256,1280]{1,0:T(8,128)(2,1)S(1)} %get-tuple-element.66.refs_5_.refs_2_.refs_0_) | copy-start | bytes 1966084
  75.5 17.8 %collective-permute-start.7 = (bf16[256,1280]{1,0:T(8,128)(2,1)S(1)}, bf16[256,1280]{1,0:T(8,128)(2,1)S(1)}, u32[]{:S(2)}, u32[]{:S(2)}) collective-permute-start(bf16[256,1280]{1,0:T(8,128)(2,1)S(1)} %get-tuple-element.66.refs_5_.refs_2_.refs_0_), channel_id=1, source_target_pairs={{0,2},{1,3},{2,0},{3,1},{4,6},{5,7},{6,4},{7,5},{8,10},{9,11},{10,... | collective-permute-start | bytes 1966088 | tf_op jit(solution)/shard_map/ppermute | solution.py:103
  76.4 47.5 %collective-permute-start.13 = (bf16[256,2560]{1,0:T(8,128)(2,1)}, bf16[256,2560]{1,0:T(8,128)(2,1)}, u32[]{:S(2)}, u32[]{:S(2)}) collective-permute-start(bf16[256,2560]{1,0:T(8,128)(2,1)} %get-tuple-element.67.refs_0_.refs_2_), channel_id=1, source_target_pairs={{0,2},{1,3},{2,0},{3,1},{4,6},{5,7},{6,4},{7,5},{8,10},{9,11},{10,... | collective-permute-start | bytes 3932168 | tf_op jit(solution)/shard_map/ppermute | solution.py:103
  79.2 44.7 %copy-start.48 = (bf16[256,1024]{1,0:T(8,128)(2,1)}, bf16[256,1024]{1,0:T(8,128)(2,1)S(1)}, u32[]{:S(2)}) copy-start(bf16[256,1024]{1,0:T(8,128)(2,1)S(1)} %collective-permute-done.5.refs_7_.refs_1_) | copy-start | bytes 1572868
  79.2 14.0 %copy-start.101 = (bf16[256,1024]{1,0:T(8,128)(2,1)S(1)}, bf16[256,1024]{1,0:T(8,128)(2,1)}, u32[]{:S(2)}) copy-start(bf16[256,1024]{1,0:T(8,128)(2,1)} %copy-done.99) | copy-start | bytes 1572868
  96.9 25.2 %copy-start.80 = (bf16[4,1280,128]{2,1,0:T(8,128)(2,1)}, bf16[4,1280,128]{2,1,0:T(8,128)(2,1)S(1)}, u32[]{:S(2)}) copy-start(bf16[4,1280,128]{2,1,0:T(8,128)(2,1)S(1)} %get-tuple-element.72.refs_5_.refs_1_) | copy-start | bytes 3932164
  96.9 9.2 %collective-permute-start.8 = (bf16[4,1280,128]{2,1,0:T(8,128)(2,1)S(1)}, bf16[4,1280,128]{2,1,0:T(8,128)(2,1)S(1)}, u32[]{:S(2)}, u32[]{:S(2)}) collective-permute-start(bf16[4,1280,128]{2,1,0:T(8,128)(2,1)S(1)} %get-tuple-element.76), channel_id=1, source_target_pairs={{0,1},{1,0},{2,3},{3,2},{4,5},{5,4},{6,7},{7,6},{8,9},{9,8},{10,11... | collective-permute-start | bytes 3932168 | tf_op jit(solution)/shard_map/ppermute | solution.py:103
  103.9 50.3 %collective-permute-start.10 = (bf16[256,1536]{1,0:T(8,128)(2,1)}, bf16[256,1536]{1,0:T(8,128)(2,1)}, u32[]{:S(2)}, u32[]{:S(2)}) collective-permute-start(bf16[256,1536]{1,0:T(8,128)(2,1)} %get-tuple-element.73.refs_2_.refs_1_), channel_id=1, source_target_pairs={{0,2},{1,3},{2,0},{3,1},{4,6},{5,7},{6,4},{7,5},{8,10},{9,11},{10,... | collective-permute-start | bytes 2359304 | tf_op jit(solution)/shard_map/ppermute | solution.py:103
  106.2 16.0 %collective-permute-start.11 = (bf16[1,1280,128]{2,1,0:T(8,128)(2,1)S(1)}, bf16[1,1280,128]{2,1,0:T(8,128)(2,1)S(1)}, u32[]{:S(2)}, u32[]{:S(2)}) collective-permute-start(bf16[1,1280,128]{2,1,0:T(8,128)(2,1)S(1)} %shard_map.204.refs_5_), channel_id=1, source_target_pairs={{0,4},{4,8},{8,12},{12,0},{1,5},{5,9},{9,13},{13,1},{2,6},{6,10},{... | collective-permute-start | bytes 983048 | tf_op jit(solution)/shard_map/ppermute | solution.py:376
  120.6 24.9 %collective-permute-start.15 = (bf16[256,2048]{1,0:T(8,128)(2,1)}, bf16[256,2048]{1,0:T(8,128)(2,1)}, u32[]{:S(2)}, u32[]{:S(2)}) collective-permute-start(bf16[256,2048]{1,0:T(8,128)(2,1)} %get-tuple-element.78.refs_4_.refs_2_), channel_id=1, source_target_pairs={{0,16},{16,0},{1,17},{17,1},{2,18},{18,2},{3,19},{19,3},{4,20},{20... | collective-permute-start | bytes 3145736 | tf_op jit(solution)/shard_map/ppermute | solution.py:103
  122.1 57.4 %collective-permute-start.9 = (bf16[256,3072]{1,0:T(8,128)(2,1)S(1)}, bf16[256,3072]{1,0:T(8,128)(2,1)}, u32[]{:S(2)}, u32[]{:S(2)}) collective-permute-start(bf16[256,3072]{1,0:T(8,128)(2,1)S(1)} %get-tuple-element.77.refs_2_), channel_id=1, source_target_pairs={{0,2},{1,3},{2,0},{3,1},{4,6},{5,7},{6,4},{7,5},{8,10},{9,11},{10,... | collective-permute-start | bytes 4718600 | tf_op jit(solution)/shard_map/ppermute | solution.py:103
  122.3 10.7 %collective-permute-start.12 = (bf16[1,1280,128]{2,1,0:T(8,128)(2,1)S(1)}, bf16[1,1280,128]{2,1,0:T(8,128)(2,1)S(1)}, u32[]{:S(2)}, u32[]{:S(2)}) collective-permute-start(bf16[1,1280,128]{2,1,0:T(8,128)(2,1)S(1)} %shard_map.206.refs_4_), channel_id=1, source_target_pairs={{0,4},{4,8},{8,12},{12,0},{1,5},{5,9},{9,13},{13,1},{2,6},{6,10},{... | collective-permute-start | bytes 983048 | tf_op jit(solution)/shard_map/ppermute | solution.py:376
  132.1 193.2 %reduce-scatter.5.cloned.1.call-start = ((), (), s32[]{:S(2)}) async-start(), calls=%async_computation.3 | async-start | bytes 7077888 | tf_op jit(solution)/shard_map/reduce_scatter | solution.py:281
  136.9 17.0 %copy-start.82 = (bf16[4,1280,128]{2,1,0:T(8,128)(2,1)S(1)}, bf16[4,1280,128]{2,1,0:T(8,128)(2,1)}, u32[]{:S(2)}) copy-start(bf16[4,1280,128]{2,1,0:T(8,128)(2,1)} %copy-done.80) | copy-start | bytes 3932164
  137.0 17.0 %collective-permute-start.14 = (bf16[1,1280,128]{2,1,0:T(8,128)(2,1)S(1)}, bf16[1,1280,128]{2,1,0:T(8,128)(2,1)S(1)}, u32[]{:S(2)}, u32[]{:S(2)}) collective-permute-start(bf16[1,1280,128]{2,1,0:T(8,128)(2,1)S(1)} %shard_map.208.refs_6_), channel_id=1, source_target_pairs={{0,4},{4,8},{8,12},{12,0},{1,5},{5,9},{9,13},{13,1},{2,6},{6,10},{... | collective-permute-start | bytes 983048 | tf_op jit(solution)/shard_map/ppermute | solution.py:376
  151.1 69.3 %collective-permute-start.25 = (bf16[256,1024]{1,0:T(8,128)(2,1)}, bf16[256,1024]{1,0:T(8,128)(2,1)}, u32[]{:S(2)}, u32[]{:S(2)}) collective-permute-start(bf16[256,1024]{1,0:T(8,128)(2,1)} %get-tuple-element.91), channel_id=1, source_target_pairs={{0,2},{1,3},{2,0},{3,1},{4,6},{5,7},{6,4},{7,5},{8,10},{9,11},{10,... | collective-permute-start | bytes 1572872 | tf_op jit(solution)/shard_map/ppermute | solution.py:103
  159.7 18.9 %copy-start.85 = (bf16[4,1536,128]{2,1,0:T(8,128)(2,1)}, bf16[4,1536,128]{2,1,0:T(8,128)(2,1)S(1)}, u32[]{:S(2)}) copy-start(bf16[4,1536,128]{2,1,0:T(8,128)(2,1)S(1)} %get-tuple-element.80.refs_12_.refs_1_) | copy-start | bytes 4718596
  159.7 18.9 %collective-permute-start.16 = (bf16[4,1536,128]{2,1,0:T(8,128)(2,1)S(1)}, bf16[4,1536,128]{2,1,0:T(8,128)(2,1)S(1)}, u32[]{:S(2)}, u32[]{:S(2)}) collective-permute-start(bf16[4,1536,128]{2,1,0:T(8,128)(2,1)S(1)} %get-tuple-element.81), channel_id=1, source_target_pairs={{0,1},{1,0},{2,3},{3,2},{4,5},{5,4},{6,7},{7,6},{8,9},{9,8},{10,11... | collective-permute-start | bytes 4718600 | tf_op jit(solution)/shard_map/ppermute | solution.py:103
  176.3 28.5 %collective-permute-start.19 = (bf16[256,256]{1,0:T(8,128)(2,1)}, bf16[256,256]{1,0:T(8,128)(2,1)}, u32[]{:S(2)}, u32[]{:S(2)}) collective-permute-start(bf16[256,256]{1,0:T(8,128)(2,1)} %get-tuple-element.87), channel_id=1, source_target_pairs={{0,1},{1,0},{2,3},{3,2},{4,5},{5,4},{6,7},{7,6},{8,9},{9,8},{10,11... | collective-permute-start | bytes 393224 | tf_op jit(solution)/shard_map/ppermute | solution.py:103
  176.8 28.0 %collective-permute-start.20 = (bf16[256,256]{1,0:T(8,128)(2,1)}, bf16[256,256]{1,0:T(8,128)(2,1)}, u32[]{:S(2)}, u32[]{:S(2)}) collective-permute-start(bf16[256,256]{1,0:T(8,128)(2,1)} %get-tuple-element.88), channel_id=1, source_target_pairs={{0,2},{1,3},{2,0},{3,1},{4,6},{5,7},{6,4},{7,5},{8,10},{9,11},{10,... | collective-permute-start | bytes 393224 | tf_op jit(solution)/shard_map/ppermute | solution.py:103
  178.6 26.2 %collective-permute-start.21 = (bf16[256,256]{1,0:T(8,128)(2,1)S(1)}, bf16[256,256]{1,0:T(8,128)(2,1)}, u32[]{:S(2)}, u32[]{:S(2)}) collective-permute-start(bf16[256,256]{1,0:T(8,128)(2,1)S(1)} %get-tuple-element.89), channel_id=1, source_target_pairs={{0,3},{1,2},{2,1},{3,0},{4,7},{5,6},{6,5},{7,4},{8,11},{9,10},{10,... | collective-permute-start | bytes 393224 | tf_op jit(solution)/shard_map/ppermute | solution.py:103
  179.5 22.6 %collective-permute-start.22 = (bf16[1,1536,128]{2,1,0:T(8,128)(2,1)}, bf16[1,1536,128]{2,1,0:T(8,128)(2,1)}, u32[]{:S(2)}, u32[]{:S(2)}) collective-permute-start(bf16[1,1536,128]{2,1,0:T(8,128)(2,1)} %shard_map.213.refs_4_), channel_id=1, source_target_pairs={{0,4},{4,8},{8,12},{12,0},{1,5},{5,9},{9,13},{13,1},{2,6},{6,10},{... | collective-permute-start | bytes 1179656 | tf_op jit(solution)/shard_map/ppermute | solution.py:376
  204.7 15.5 %collective-permute-start.26 = (bf16[1,1536,128]{2,1,0:T(8,128)(2,1)S(1)}, bf16[1,1536,128]{2,1,0:T(8,128)(2,1)S(1)}, u32[]{:S(2)}, u32[]{:S(2)}) collective-permute-start(bf16[1,1536,128]{2,1,0:T(8,128)(2,1)S(1)} %shard_map.216.refs_6_), channel_id=1, source_target_pairs={{0,4},{4,8},{8,12},{12,0},{1,5},{5,9},{9,13},{13,1},{2,6},{6,10},{... | collective-permute-start | bytes 1179656 | tf_op jit(solution)/shard_map/ppermute | solution.py:376
  207.7 12.6 %copy-start.87 = (bf16[4,1536,128]{2,1,0:T(8,128)(2,1)S(1)}, bf16[4,1536,128]{2,1,0:T(8,128)(2,1)}, u32[]{:S(2)}) copy-start(bf16[4,1536,128]{2,1,0:T(8,128)(2,1)} %copy-done.85) | copy-start | bytes 4718596
  223.2 22.4 %copy-start.88 = (bf16[4,1024,128]{2,1,0:T(8,128)(2,1)}, bf16[4,1024,128]{2,1,0:T(8,128)(2,1)S(1)}, u32[]{:S(2)}) copy-start(bf16[4,1024,128]{2,1,0:T(8,128)(2,1)S(1)} %get-tuple-element.92.refs_4_.refs_1_) | copy-start | bytes 3145732
  223.2 22.4 %collective-permute-start.27 = (bf16[4,1024,128]{2,1,0:T(8,128)(2,1)S(1)}, bf16[4,1024,128]{2,1,0:T(8,128)(2,1)S(1)}, u32[]{:S(2)}, u32[]{:S(2)}) collective-permute-start(bf16[4,1024,128]{2,1,0:T(8,128)(2,1)S(1)} %get-tuple-element.93), channel_id=1, source_target_pairs={{0,1},{1,0},{2,3},{3,2},{4,5},{5,4},{6,7},{7,6},{8,9},{9,8},{10,11... | collective-permute-start | bytes 3145736 | tf_op jit(solution)/shard_map/ppermute | solution.py:103
  223.3 22.1 %collective-permute-start.28 = (bf16[1,1536,128]{2,1,0:T(8,128)(2,1)S(1)}, bf16[1,1536,128]{2,1,0:T(8,128)(2,1)S(1)}, u32[]{:S(2)}, u32[]{:S(2)}) collective-permute-start(bf16[1,1536,128]{2,1,0:T(8,128)(2,1)S(1)} %shard_map.219.refs_4_), channel_id=1, source_target_pairs={{0,4},{4,8},{8,12},{12,0},{1,5},{5,9},{9,13},{13,1},{2,6},{6,10},{... | collective-permute-start | bytes 1179656 | tf_op jit(solution)/shard_map/ppermute | solution.py:376
  223.4 23.2 %collective-permute-start.18 = (bf16[256,1024]{1,0:T(8,128)(2,1)S(1)}, bf16[256,1024]{1,0:T(8,128)(2,1)S(1)}, u32[]{:S(2)}, u32[]{:S(2)}) collective-permute-start(bf16[256,1024]{1,0:T(8,128)(2,1)S(1)} %copy-done.45), channel_id=1, source_target_pairs={{0,2},{1,3},{2,0},{3,1},{4,6},{5,7},{6,4},{7,5},{8,10},{9,11},{10,... | collective-permute-start | bytes 1572872 | tf_op jit(solution)/shard_map/ppermute | solution.py:103
  225.4 23.7 %collective-permute-start.24 = (bf16[256,1024]{1,0:T(8,128)(2,1)S(1)}, bf16[256,1024]{1,0:T(8,128)(2,1)S(1)}, u32[]{:S(2)}, u32[]{:S(2)}) collective-permute-start(bf16[256,1024]{1,0:T(8,128)(2,1)S(1)} %copy-done.51), channel_id=1, source_target_pairs={{0,2},{1,3},{2,0},{3,1},{4,6},{5,7},{6,4},{7,5},{8,10},{9,11},{10,... | collective-permute-start | bytes 1572872 | tf_op jit(solution)/shard_map/ppermute | solution.py:103
  246.6 23.3 %copy-start.25 = (bf16[4,1024,128]{2,1,0:T(8,128)(2,1)S(1)}, bf16[4,1024,128]{2,1,0:T(8,128)(2,1)}, u32[]{:S(2)}) copy-start(bf16[4,1024,128]{2,1,0:T(8,128)(2,1)} %copy-done.24) | copy-start | bytes 3145732
  252.7 20.7 %collective-permute-start.29 = (bf16[4,128,1024]{2,1,0:T(8,128)(2,1)}, bf16[4,128,1024]{2,1,0:T(8,128)(2,1)S(1)}, u32[]{:S(2)}, u32[]{:S(2)}) collective-permute-start(bf16[4,128,1024]{2,1,0:T(8,128)(2,1)} %bitcast.10), channel_id=1, source_target_pairs={{0,1},{1,0},{2,3},{3,2},{4,5},{5,4},{6,7},{7,6},{8,9},{9,8},{10,11... | collective-permute-start | bytes 3145736 | tf_op jit(solution)/shard_map/ppermute | solution.py:103
  252.7 16.5 %collective-permute-start.30 = (bf16[1,1024,128]{2,1,0:T(8,128)(2,1)S(1)}, bf16[1,1024,128]{2,1,0:T(8,128)(2,1)S(1)}, u32[]{:S(2)}, u32[]{:S(2)}) collective-permute-start(bf16[1,1024,128]{2,1,0:T(8,128)(2,1)S(1)} %shard_map.222.refs_4_), channel_id=1, source_target_pairs={{0,4},{4,8},{8,12},{12,0},{1,5},{5,9},{9,13},{13,1},{2,6},{6,10},{... | collective-permute-start | bytes 786440 | tf_op jit(solution)/shard_map/ppermute | solution.py:376
  252.7 22.4 %collective-permute-start.23 = (bf16[256,256]{1,0:T(8,128)(2,1)S(1)}, bf16[256,256]{1,0:T(8,128)(2,1)S(1)}, u32[]{:S(2)}, u32[]{:S(2)}) collective-permute-start(bf16[256,256]{1,0:T(8,128)(2,1)S(1)} %shard_map.217.refs_1_.refs_5_.refs_2_), channel_id=1, source_target_pairs={{0,2},{1,3},{2,0},{3,1},{4,6},{5,7},{6,4},{7,5},{8,10},{9,11},{10,... | collective-permute-start | bytes 393224 | tf_op jit(solution)/shard_map/ppermute | solution.py:103
  254.5 25.5 %collective-permute-start.32 = (bf16[256,2048]{1,0:T(8,128)(2,1)}, bf16[256,2048]{1,0:T(8,128)(2,1)S(1)}, u32[]{:S(2)}, u32[]{:S(2)}) collective-permute-start(bf16[256,2048]{1,0:T(8,128)(2,1)} %copy-done.29), channel_id=1, source_target_pairs={{0,16},{16,0},{1,17},{17,1},{2,18},{18,2},{3,19},{19,3},{4,20},{20... | collective-permute-start | bytes 3145736 | tf_op jit(solution)/shard_map/ppermute | solution.py:103
  283.2 3.7 %collective-permute-start.40 = (f32[2,4,128]{2,1,0:T(4,128)S(1)}, f32[2,4,128]{2,1,0:T(4,128)S(1)}, u32[]{:S(2)}, u32[]{:S(2)}) collective-permute-start(f32[2,4,128]{2,1,0:T(4,128)S(1)} %bitcast.82), channel_id=1, source_target_pairs={{0,2},{1,3},{2,0},{3,1},{4,6},{5,7},{6,4},{7,5},{8,10},{9,11},{10,... | collective-permute-start | bytes 12296 | tf_op jit(solution)/shard_map/ppermute | solution.py:103
  283.5 3.3 collective-permute-start.39
  283.5 3.3 collective-permute-start.41
  285.4 38.5 %collective-permute-start.17 = (bf16[256,2048]{1,0:T(8,128)(2,1)S(1)}, bf16[256,2048]{1,0:T(8,128)(2,1)S(1)}, u32[]{:S(2)}, u32[]{:S(2)}) collective-permute-start(bf16[256,2048]{1,0:T(8,128)(2,1)S(1)} %copy-done.21), channel_id=1, source_target_pairs={{0,16},{16,0},{1,17},{17,1},{2,18},{18,2},{3,19},{19,3},{4,20},{20... | collective-permute-start | bytes 3145736 | tf_op jit(solution)/shard_map/ppermute | solution.py:103
  286.9 7.2 %collective-permute-start.44 = (f32[2,128]{1,0:T(2,128)S(1)}, f32[2,128]{1,0:T(2,128)S(1)}, u32[]{:S(2)}, u32[]{:S(2)}) collective-permute-start(f32[2,128]{1,0:T(2,128)S(1)} %bitcast.88), channel_id=1, source_target_pairs={{0,12},{4,8},{8,4},{12,0},{1,13},{5,9},{9,5},{13,1},{2,14},{6,10},... | collective-permute-start | bytes 3080 | tf_op jit(solution)/shard_map/ppermute | solution.py:103
  290.5 5.5 %collective-permute-start.42 = (f32[2,128]{1,0:T(2,128)S(1)}, f32[2,128]{1,0:T(2,128)S(1)}, u32[]{:S(2)}, u32[]{:S(2)}) collective-permute-start(f32[2,128]{1,0:T(2,128)S(1)} %bitcast.87), channel_id=1, source_target_pairs={{0,4},{4,0},{8,12},{12,8},{1,5},{5,1},{9,13},{13,9},{2,6},{6,2},{1... | collective-permute-start | bytes 3080 | tf_op jit(solution)/shard_map/ppermute | solution.py:103
  291.3 4.7 %collective-permute-start.43 = (f32[2,128]{1,0:T(2,128)S(1)}, f32[2,128]{1,0:T(2,128)S(1)}, u32[]{:S(2)}, u32[]{:S(2)}) collective-permute-start(f32[2,128]{1,0:T(2,128)S(1)} %bitcast.86), channel_id=1, source_target_pairs={{0,8},{4,12},{8,0},{12,4},{1,9},{5,13},{9,1},{13,5},{2,10},{6,14},... | collective-permute-start | bytes 3080 | tf_op jit(solution)/shard_map/ppermute | solution.py:103
  292.5 11.0 %collective-permute-start.35 = (bf16[1,1024,128]{2,1,0:T(8,128)(2,1)S(1)}, bf16[1,1024,128]{2,1,0:T(8,128)(2,1)S(1)}, u32[]{:S(2)}, u32[]{:S(2)}) collective-permute-start(bf16[1,1024,128]{2,1,0:T(8,128)(2,1)S(1)} %shard_map.224.refs_3_), channel_id=1, source_target_pairs={{0,4},{4,8},{8,12},{12,0},{1,5},{5,9},{9,13},{13,1},{2,6},{6,10},{... | collective-permute-start | bytes 786440 | tf_op jit(solution)/shard_map/ppermute | solution.py:376
  294.1 15.1 %collective-permute-start.34 = (bf16[1,128,1024]{2,1,0:T(8,128)(2,1)S(1)}, bf16[1,128,1024]{2,1,0:T(8,128)(2,1)S(1)}, u32[]{:S(2)}, u32[]{:S(2)}) collective-permute-start(bf16[1,128,1024]{2,1,0:T(8,128)(2,1)S(1)} %shard_map.225.refs_4_), channel_id=1, source_target_pairs={{0,4},{4,8},{8,12},{12,0},{1,5},{5,9},{9,13},{13,1},{2,6},{6,10},{... | collective-permute-start | bytes 786440 | tf_op jit(solution)/shard_map/ppermute | solution.py:376
  296.0 1.5 collective-permute-start.31
  297.6 12.9 %collective-permute-start.33 = (bf16[1,128,256]{2,1,0:T(8,128)(2,1)S(1)}, bf16[1,128,256]{2,1,0:T(8,128)(2,1)S(1)}, u32[]{:S(2)}, u32[]{:S(2)}) collective-permute-start(bf16[1,128,256]{2,1,0:T(8,128)(2,1)S(1)} %shard_map.228.refs_4_), channel_id=1, source_target_pairs={{0,4},{4,8},{8,12},{12,0},{1,5},{5,9},{9,13},{13,1},{2,6},{6,10},{... | collective-permute-start | bytes 196616 | tf_op jit(solution)/shard_map/ppermute | solution.py:376
  303.6 12.5 %collective-permute-start.38 = (bf16[1,1024,128]{2,1,0:T(8,128)(2,1)S(1)}, bf16[1,1024,128]{2,1,0:T(8,128)(2,1)S(1)}, u32[]{:S(2)}, u32[]{:S(2)}) collective-permute-start(bf16[1,1024,128]{2,1,0:T(8,128)(2,1)S(1)} %shard_map.229.refs_4_), channel_id=1, source_target_pairs={{0,4},{4,8},{8,12},{12,0},{1,5},{5,9},{9,13},{13,1},{2,6},{6,10},{... | collective-permute-start | bytes 786440 | tf_op jit(solution)/shard_map/ppermute | solution.py:376
  309.3 12.0 %collective-permute-start.37 = (bf16[1,128,1024]{2,1,0:T(8,128)(2,1)S(1)}, bf16[1,128,1024]{2,1,0:T(8,128)(2,1)S(1)}, u32[]{:S(2)}, u32[]{:S(2)}) collective-permute-start(bf16[1,128,1024]{2,1,0:T(8,128)(2,1)S(1)} %shard_map.230.refs_4_), channel_id=1, source_target_pairs={{0,4},{4,8},{8,12},{12,0},{1,5},{5,9},{9,13},{13,1},{2,6},{6,10},{... | collective-permute-start | bytes 786440 | tf_op jit(solution)/shard_map/ppermute | solution.py:376
  310.6 11.9 %collective-permute-start.36 = (bf16[1,128,256]{2,1,0:T(8,128)(2,1)S(1)}, bf16[1,128,256]{2,1,0:T(8,128)(2,1)S(1)}, u32[]{:S(2)}, u32[]{:S(2)}) collective-permute-start(bf16[1,128,256]{2,1,0:T(8,128)(2,1)S(1)} %shard_map.231.refs_4_), channel_id=1, source_target_pairs={{0,4},{4,8},{8,12},{12,0},{1,5},{5,9},{9,13},{13,1},{2,6},{6,10},{... | collective-permute-start | bytes 196616 | tf_op jit(solution)/shard_map/ppermute | solution.py:376
  322.4 11.7 %collective-permute-start.45 = (bf16[1,128,1024]{2,1,0:T(8,128)(2,1)S(1)}, bf16[1,128,1024]{2,1,0:T(8,128)(2,1)S(1)}, u32[]{:S(2)}, u32[]{:S(2)}) collective-permute-start(bf16[1,128,1024]{2,1,0:T(8,128)(2,1)S(1)} %shard_map.233.refs_4_), channel_id=1, source_target_pairs={{0,4},{4,8},{8,12},{12,0},{1,5},{5,9},{9,13},{13,1},{2,6},{6,10},{... | collective-permute-start | bytes 786440 | tf_op jit(solution)/shard_map/ppermute | solution.py:376
  322.5 9.5 %collective-permute-start.46 = (bf16[1,128,256]{2,1,0:T(8,128)(2,1)S(1)}, bf16[1,128,256]{2,1,0:T(8,128)(2,1)S(1)}, u32[]{:S(2)}, u32[]{:S(2)}) collective-permute-start(bf16[1,128,256]{2,1,0:T(8,128)(2,1)S(1)} %shard_map.234.refs_3_), channel_id=1, source_target_pairs={{0,4},{4,8},{8,12},{12,0},{1,5},{5,9},{9,13},{13,1},{2,6},{6,10},{... | collective-permute-start | bytes 196616 | tf_op jit(solution)/shard_map/ppermute | solution.py:376
  (101 other events, 465.7 us)
Sparse Core Ops, SparseCore 0:
  132.2 73.2 reduce-scatter.2
  207.8 83.6 reduce-scatter.4

commit v5 on v4

--- a/solution.py
+++ b/solution.py
@@ -562,6 +562,7 @@
             pltpu.VMEM((tokens, width), F32),
         ],
         scalars=1,
+        vmem=24,
     )
 
 

time: 344 us -> 344 us (level)
  no operation moved by 1% of the time
where the time goes in v5:
time: 344 us; the launch traced here: 342 us
  Pallas kernels  123 us (36%)
  waiting for transfers between devices  115 us (33%)
  local copies, waits for them, and re-layouts  47.1 us (14%)
  starting transfers between devices  40.3 us (12%)
  between operations  15.3 us (4%)
    pallas_call x45, Pallas kernels, __call__(): pl.pallas_call(stripped, out_shape=out_shape + [shaped(c.shape, c.dtype)...  123 us
    ppermute x15, waiting for transfers between devices, step(): self.arrived = lax.ppermute(total, 'dp', ring)  74.5 us
    unnamed x233, local copies, waits for them, and re-layouts  45.9 us
    ppermute x32, waiting for transfers between devices, swap(): return lax.ppermute(value, axis, [(i, i ^ flip) for i in range(count)])  40.2 us
    ppermute x32, starting transfers between devices, swap(): return lax.ppermute(value, axis, [(i, i ^ flip) for i in range(count)])  28.5 us
    ppermute x15, starting transfers between devices, step(): self.arrived = lax.ppermute(total, 'dp', ring)  11.7 us
  transfers between devices with their start and end apart: 49, of which 22 were waited for; matrix products, arithmetic and copies ran while one was open for 1% of the time, Pallas kernels for 32%

profile of v5, /device:TPU:0, one launch (start us, length us, event | category | flops | bytes accessed | tf_op | source)
XLA Modules:
  0.0 342.4 jit_solution(14405801305726840667)
XLA Ops:
  8.1 1.3 copy-done.17
  13.2 2.5 collective-permute-start.2
  16.4 3.0 shard_map.195.refs_2_.refs_1_
  20.5 2.0 collective-permute-done.1.refs_4_.refs_10_
  22.6 12.4 %shard_map.197 = (bf16[256,1024]{1,0:T(8,128)(2,1)S(1)}, f32[4,4,256]{2,1,0:T(4,128)S(1)}, bf16[256,2048]{1,0:T(8,128)(2,1)S(1)}) custom-call(s32[1]{0:T(128)} %bitcast.refs_0_, bf16[256,1024]{1,0:T(8,128)(2,1)S(1)} %shard_map.195.refs_2_.refs_1_, bf16[256,256]{1,0:T(8,128)(2,1)S(1)} %get-tuple-element.58.refs_2_.refs_8_, ...), custom_call_target="tpu_custom_call" | custom-call | flops 46200000512 | bytes 1000 | tf_op jit(solution)/shard_map/pallas_call | solution.py:81
  36.4 2.3 collective-permute-start.3
  38.7 1.5 collective-permute-start.4
  40.7 13.1 %collective-permute-done.4.refs_4_.refs_1_ = bf16[256,1024]{1,0:T(8,128)(2,1)} collective-permute-done((bf16[256,1024]{1,0:T(8,128)(2,1)}, bf16[256,1024]{1,0:T(8,128)(2,1)}, u32[]{:S(2)}, u32[]{:S(2)}) %collective-permute-start.4) | collective-permute-done | bytes 524320 | tf_op jit(solution)/shard_map/ppermute | solution.py:103
  58.3 3.8 %collective-permute-done.3.refs_3_ = bf16[256,2048]{1,0:T(8,128)(2,1)S(1)} collective-permute-done((bf16[256,2048]{1,0:T(8,128)(2,1)S(1)}, bf16[256,2048]{1,0:T(8,128)(2,1)S(1)}, u32[]{:S(2)}, u32[]{:S(2)}) %collective-permute-start.3) | collective-permute-done | bytes 1048608 | tf_op jit(solution)/shard_map/ppermute | solution.py:103
  62.1 1.4 copy-done.28
  64.8 1.9 collective-permute-start.5
  66.7 8.8 %shard_map.200 = (bf16[256,1280]{1,0:T(8,128)(2,1)S(1)}, bf16[256,2560]{1,0:T(8,128)(2,1)}) custom-call(bf16[256,2048]{1,0:T(8,128)(2,1)S(1)} %get-tuple-element.65.refs_0_, bf16[256,2048]{1,0:T(8,128)(2,1)S(1)} %bitcast.55, bf16[2048,2816]{1,0:T(8,128)(2,1)S(1)} %bitcast.53, bf16[2048,2816]{1,0:T(8,128)(2,1)} %refs_2_.11, bf16[2816,2048]{1,0:T(8,128)(2,1)} %refs_2_.12, ...), custom_call_target="tpu_custom_call" | custom-call | flops 32999999488 | bytes 1000 | tf_op jit(solution)/shard_map/pallas_call | solution.py:81
  77.5 1.7 collective-permute-done.5.refs_7_.refs_1_
  79.2 10.2 %shard_map.201 = (bf16[256,1536]{1,0:T(8,128)(2,1)}, bf16[256,3072]{1,0:T(8,128)(2,1)S(1)}) custom-call(bf16[256,2048]{1,0:T(8,128)(2,1)S(1)} %get-tuple-element.65.refs_0_, bf16[256,2048]{1,0:T(8,128)(2,1)S(1)} %bitcast.56, bf16[2048,2816]{1,0:T(8,128)(2,1)S(1)} %bitcast.53, bf16[2048,2816]{1,0:T(8,128)(2,1)} %refs_2_.11, bf16[2816,2048]{1,0:T(8,128)(2,1)} %refs_2_.12, ...), custom_call_target="tpu_custom_call" | custom-call | flops 32999999488 | bytes 1000 | tf_op jit(solution)/shard_map/pallas_call | solution.py:81
  89.4 3.9 %collective-permute-done.7.refs_3_ = bf16[256,1280]{1,0:T(8,128)(2,1)S(1)} collective-permute-done((bf16[256,1280]{1,0:T(8,128)(2,1)S(1)}, bf16[256,1280]{1,0:T(8,128)(2,1)S(1)}, u32[]{:S(2)}, u32[]{:S(2)}) %collective-permute-start.7) | collective-permute-done | bytes 655392 | tf_op jit(solution)/shard_map/ppermute | solution.py:103
  93.3 3.6 %shard_map.202 = (bf16[4,1280,128]{2,1,0:T(8,128)(2,1)S(1)}, bf16[4,1280,128]{2,1,0:T(8,128)(2,1)S(1)}) custom-call(bf16[256,1024]{1,0:T(8,128)(2,1)S(1)} %copy-done.101, bf16[256,1024]{1,0:T(8,128)(2,1)} %collective-permute-done.4.refs_4_.refs_1_, bf16[256,1280]{1,0:T(8,128)(2,1)S(1)} %get-tuple-element.66.refs_5_.refs_2_.refs_0_, ...), custom_call_target="tpu_custom_call" | custom-call | flops 9900000256 | bytes 1000 | tf_op jit(solution)/shard_map/pallas_call | solution.py:81
  97.0 6.9 %shard_map.203 = (f32[256,2048]{1,0:T(8,128)S(1)}, bf16[256,1536]{1,0:T(8,128)(2,1)}, bf16[256,3072]{1,0:T(8,128)(2,1)S(1)}) custom-call(bf16[256,2560]{1,0:T(8,128)(2,1)} %get-tuple-element.67.refs_0_.refs_2_, bf16[2048,2816]{1,0:T(8,128)(2,1)S(1)} %bitcast.53, bf16[2048,2816]{1,0:T(8,128)(2,1)} %refs_2_.11, ...), custom_call_target="tpu_custom_call", output_to_operand_aliasing={{1}: (3, {}), {2}: (4, {})} | custom-call | flops 23100000256 | bytes 1000 | tf_op jit(solution)/shard_map/pallas_call | solution.py:81
  103.9 2.1 collective-permute-start.10
  106.2 1.8 collective-permute-start.11
  108.0 4.3 %copy-done.9 = bf16[2048,2816]{1,0:T(8,128)(2,1)S(1)} copy-done((bf16[2048,2816]{1,0:T(8,128)(2,1)S(1)}, bf16[2048,2816]{1,0:T(8,128)(2,1)}, u32[]{:S(2)}) %copy-start.9) | copy-done | bytes 11534360
  112.2 8.4 %shard_map.205 = (bf16[256,2048]{1,0:T(8,128)(2,1)}, bf16[256,3072]{1,0:T(8,128)(2,1)S(1)}) custom-call(bf16[256,3072]{1,0:T(8,128)(2,1)S(1)} %get-tuple-element.74.refs_0_, bf16[2048,2816]{1,0:T(8,128)(2,1)S(1)} %copy-done.9, bf16[2048,2816]{1,0:T(8,128)(2,1)} %refs_2_.11, ...), custom_call_target="tpu_custom_call", output_to_operand_aliasing={{1}: (4, {})} | custom-call | flops 26400000000 | bytes 1000 | tf_op jit(solution)/shard_map/pallas_call | solution.py:81
  120.6 1.5 collective-permute-start.15
  122.3 1.7 collective-permute-start.12
  123.9 5.8 %shard_map.207.refs_4_ = bf16[4,2,128,2560]{3,2,1,0:T(8,128)(2,1)S(1)} custom-call(bf16[256,1024]{1,0:T(8,128)(2,1)S(1)} %get-tuple-element.68.refs_6_.refs_0_, bf16[256,1024]{1,0:T(8,128)(2,1)S(1)} %collective-permute-done.5.refs_7_.refs_1_, bf16[256,2560]{1,0:T(8,128)(2,1)} %get-tuple-element.67.refs_0_.refs_2_, ...), custom_call_target="tpu_custom_call" | custom-call | flops 16499999744 | bytes 1000 | tf_op jit(solution)/shard_map/pallas_call | solution.py:81
  129.7 2.4 copy-done.1
  133.0 2.5 copy-done.2
  135.5 1.3 copy-done.81
  137.8 7.8 %collective-permute-done.15.refs_3_ = bf16[256,2048]{1,0:T(8,128)(2,1)} collective-permute-done((bf16[256,2048]{1,0:T(8,128)(2,1)}, bf16[256,2048]{1,0:T(8,128)(2,1)}, u32[]{:S(2)}, u32[]{:S(2)}) %collective-permute-start.15) | collective-permute-done | bytes 1048608 | tf_op jit(solution)/shard_map/ppermute | solution.py:103
  145.6 4.7 %shard_map.209 = (f32[256,2048]{1,0:T(8,128)S(1)}, bf16[256,2048]{1,0:T(8,128)(2,1)S(1)}, f32[1,2048]{1,0:T(1,128)S(1)}, bf16[256,1024]{1,0:T(8,128)(2,1)S(1)}, bf16[256,1024]{1,0:T(8,128)(2,1)}) custom-call(s32[1]{0:T(128)} %bitcast.refs_0_, bf16[256,2048]{1,0:T(8,128)(2,1)S(1)} %bitcast.57, bf16[256,2048]{1,0:T(8,128)(2,1)} %get-tuple-element.78.refs_4_.refs_2_, ...), custom_call_target="tpu_custom_call" | custom-call | flops 13200000000 | bytes 1000 | tf_op jit(solution)/shard_map/pallas_call | solution.py:81
  151.4 2.5 collective-permute-done.14.refs_3_
  155.0 4.6 %shard_map.211 = (bf16[4,1536,128]{2,1,0:T(8,128)(2,1)S(1)}, bf16[4,1536,128]{2,1,0:T(8,128)(2,1)S(1)}) custom-call(bf16[256,1024]{1,0:T(8,128)(2,1)S(1)} %copy-done.102, bf16[256,1024]{1,0:T(8,128)(2,1)} %collective-permute-done.4.refs_4_.refs_1_, bf16[256,1536]{1,0:T(8,128)(2,1)} %get-tuple-element.73.refs_2_.refs_1_, ...), custom_call_target="tpu_custom_call" | custom-call | flops 9900000256 | bytes 1000 | tf_op jit(solution)/shard_map/pallas_call | solution.py:81
  159.9 16.4 %shard_map.212 = (bf16[256,1024]{1,0:T(8,128)(2,1)S(1)}, bf16[256,256]{1,0:T(8,128)(2,1)S(1)}, bf16[256,256]{1,0:T(8,128)(2,1)}, bf16[256,256]{1,0:T(8,128)(2,1)}, bf16[256,256]{1,0:T(8,128)(2,1)S(1)}) custom-call(s32[1]{0:T(128)} %bitcast.refs_0_, bf16[256,1024]{1,0:T(8,128)(2,1)S(1)} %copy-done.104, bf16[256,1024]{1,0:T(8,128)(2,1)S(1)} %copy-done.42, ...), custom_call_target="tpu_custom_call" | custom-call | flops 52800000000 | bytes 1000 | tf_op jit(solution)/shard_map/pallas_call | solution.py:81
  176.8 1.8 collective-permute-start.20
  180.1 6.4 %shard_map.214.refs_3_ = bf16[4,2,128,3072]{3,2,1,0:T(8,128)(2,1)S(1)} custom-call(bf16[256,1024]{1,0:T(8,128)(2,1)S(1)} %copy-done.106, bf16[256,1024]{1,0:T(8,128)(2,1)S(1)} %copy-done.49, bf16[256,3072]{1,0:T(8,128)(2,1)S(1)} %get-tuple-element.77.refs_2_, bf16[256,3072]{1,0:T(8,128)(2,1)} %collective-permute-done.9.refs_3_, ...), custom_call_target="tpu_custom_call" | custom-call | flops 16499999744 | bytes 1000 | tf_op jit(solution)/shard_map/pallas_call | solution.py:81
  186.5 4.3 %copy-done.10 = bf16[2816,2048]{1,0:T(8,128)(2,1)S(1)} copy-done((bf16[2816,2048]{1,0:T(8,128)(2,1)S(1)}, bf16[2816,2048]{1,0:T(8,128)(2,1)}, u32[]{:S(2)}) %copy-start.10) | copy-done | bytes 11534360
  190.9 7.2 %shard_map.215.refs_4_.refs_1_ = bf16[256,2048]{1,0:T(8,128)(2,1)S(1)} custom-call(bf16[256,1280]{1,0:T(8,128)(2,1)S(1)} %copy-done.34, bf16[256,1536]{1,0:T(8,128)(2,1)} %get-tuple-element.73.refs_2_.refs_1_, bf16[2816,2048]{1,0:T(8,128)(2,1)S(1)} %copy-done.10, bf16[4,2,128,3072]{3,2,1,0:T(8,128)(2,1)S(1)} %shard_map.214.refs_3_), custom_call_target="tpu_custom_call" | custom-call | flops 26400000000 | bytes 1000 | tf_op jit(solution)/shard_map/pallas_call | solution.py:81
  198.1 4.1 %collective-permute-done.22.refs_3_ = bf16[1,1536,128]{2,1,0:T(8,128)(2,1)} collective-permute-done((bf16[1,1536,128]{2,1,0:T(8,128)(2,1)}, bf16[1,1536,128]{2,1,0:T(8,128)(2,1)}, u32[]{:S(2)}, u32[]{:S(2)}) %collective-permute-start.22) | collective-permute-done | bytes 393248 | tf_op jit(solution)/shard_map/ppermute | solution.py:376
  202.1 1.4 copy-done.86
  204.9 1.4 shard_map.217.refs_1_.refs_5_.refs_2_
  207.7 2.3 shard_map.218.refs_4_.refs_0_
  210.1 10.2 %collective-permute-done.26.refs_3_ = bf16[1,1536,128]{2,1,0:T(8,128)(2,1)S(1)} collective-permute-done((bf16[1,1536,128]{2,1,0:T(8,128)(2,1)S(1)}, bf16[1,1536,128]{2,1,0:T(8,128)(2,1)S(1)}, u32[]{:S(2)}, u32[]{:S(2)}) %collective-permute-start.26) | collective-permute-done | bytes 393248 | tf_op jit(solution)/shard_map/ppermute | solution.py:376
  220.5 2.8 shard_map.220
  223.4 2.0 collective-permute-start.18
  225.5 20.0 %collective-permute-done.28.refs_3_ = bf16[1,1536,128]{2,1,0:T(8,128)(2,1)S(1)} collective-permute-done((bf16[1,1536,128]{2,1,0:T(8,128)(2,1)S(1)}, bf16[1,1536,128]{2,1,0:T(8,128)(2,1)S(1)}, u32[]{:S(2)}, u32[]{:S(2)}) %collective-permute-start.28) | collective-permute-done | bytes 393248 | tf_op jit(solution)/shard_map/ppermute | solution.py:376
  246.6 2.4 collective-permute-done.24.refs_3_
  249.0 2.7 shard_map.223
  252.7 1.7 collective-permute-start.23
  254.5 14.7 %collective-permute-done.30.refs_3_ = bf16[1,1024,128]{2,1,0:T(8,128)(2,1)S(1)} collective-permute-done((bf16[1,1024,128]{2,1,0:T(8,128)(2,1)S(1)}, bf16[1,1024,128]{2,1,0:T(8,128)(2,1)S(1)}, u32[]{:S(2)}, u32[]{:S(2)}) %collective-permute-start.30) | collective-permute-done | bytes 262176 | tf_op jit(solution)/shard_map/ppermute | solution.py:376
  273.5 1.5 copy-done.71
  276.7 3.3 collective-permute-done.32.refs_1_
  280.0 3.1 shard_map.227
  283.5 1.9 collective-permute-start.41
  286.9 3.6 %collective-permute-start.44 = (f32[2,128]{1,0:T(2,128)S(1)}, f32[2,128]{1,0:T(2,128)S(1)}, u32[]{:S(2)}, u32[]{:S(2)}) collective-permute-start(f32[2,128]{1,0:T(2,128)S(1)} %bitcast.88), channel_id=1, source_target_pairs={{0,12},{4,8},{8,4},{12,0},{1,13},{5,9},{9,5},{13,1},{2,14},{6,10},... | collective-permute-start | bytes 3080 | tf_op jit(solution)/shard_map/ppermute | solution.py:103
  292.5 1.5 collective-permute-start.35
  294.1 1.9 collective-permute-start.34
  298.9 4.7 %collective-permute-done.35.refs_3_ = bf16[1,1024,128]{2,1,0:T(8,128)(2,1)S(1)} collective-permute-done((bf16[1,1024,128]{2,1,0:T(8,128)(2,1)S(1)}, bf16[1,1024,128]{2,1,0:T(8,128)(2,1)S(1)}, u32[]{:S(2)}, u32[]{:S(2)}) %collective-permute-start.35) | collective-permute-done | bytes 262176 | tf_op jit(solution)/shard_map/ppermute | solution.py:376
  303.7 5.4 %collective-permute-done.34.refs_3_ = bf16[1,128,1024]{2,1,0:T(8,128)(2,1)S(1)} collective-permute-done((bf16[1,128,1024]{2,1,0:T(8,128)(2,1)S(1)}, bf16[1,128,1024]{2,1,0:T(8,128)(2,1)S(1)}, u32[]{:S(2)}, u32[]{:S(2)}) %collective-permute-start.34) | collective-permute-done | bytes 262176 | tf_op jit(solution)/shard_map/ppermute | solution.py:376
  311.1 5.0 %collective-permute-done.38.refs_3_ = bf16[1,1024,128]{2,1,0:T(8,128)(2,1)S(1)} collective-permute-done((bf16[1,1024,128]{2,1,0:T(8,128)(2,1)S(1)}, bf16[1,1024,128]{2,1,0:T(8,128)(2,1)S(1)}, u32[]{:S(2)}, u32[]{:S(2)}) %collective-permute-start.38) | collective-permute-done | bytes 262176 | tf_op jit(solution)/shard_map/ppermute | solution.py:376
  317.1 4.2 %collective-permute-done.37.refs_3_ = bf16[1,128,1024]{2,1,0:T(8,128)(2,1)S(1)} collective-permute-done((bf16[1,128,1024]{2,1,0:T(8,128)(2,1)S(1)}, bf16[1,128,1024]{2,1,0:T(8,128)(2,1)S(1)}, u32[]{:S(2)}, u32[]{:S(2)}) %collective-permute-start.37) | collective-permute-done | bytes 262176 | tf_op jit(solution)/shard_map/ppermute | solution.py:376
  322.5 1.3 collective-permute-start.46
  324.0 1.3 shard_map.235.refs_2_
  328.8 1.8 shard_map.236
  330.5 1.6 collective-permute-done.46.refs_3_
  332.1 1.4 copy-done.68
  (328 shorter events, 50.4 us)
Async XLA Ops:
  7.2 318.1 %reduce-scatter.3.cloned.1.call-start = ((), (), s32[]{:S(2)}) async-start(), calls=%async_computation.2 | async-start | bytes 5898240 | tf_op jit(solution)/shard_map/reduce_scatter | solution.py:281
  13.2 7.3 %collective-permute-start.2 = (bf16[256,256]{1,0:T(8,128)(2,1)S(1)}, bf16[256,256]{1,0:T(8,128)(2,1)S(1)}, u32[]{:S(2)}, u32[]{:S(2)}) collective-permute-start(bf16[256,256]{1,0:T(8,128)(2,1)S(1)} %get-tuple-element.58.refs_2_.refs_8_), channel_id=1, source_target_pairs={{0,3},{1,2},{2,1},{3,0},{4,7},{5,6},{6,5},{7,4},{8,11},{9,10},{10,... | collective-permute-start | bytes 393224 | tf_op jit(solution)/shard_map/ppermute | solution.py:103
  15.7 6.9 %collective-permute-start.1 = (bf16[256,256]{1,0:T(8,128)(2,1)S(1)}, bf16[256,256]{1,0:T(8,128)(2,1)S(1)}, u32[]{:S(2)}, u32[]{:S(2)}) collective-permute-start(bf16[256,256]{1,0:T(8,128)(2,1)S(1)} %get-tuple-element.58.refs_2_.refs_8_), channel_id=1, source_target_pairs={{0,2},{1,3},{2,0},{3,1},{4,6},{5,7},{6,4},{7,5},{8,10},{9,11},{10,... | collective-permute-start | bytes 393224 | tf_op jit(solution)/shard_map/ppermute | solution.py:103
  16.3 6.2 %collective-permute-start = (bf16[256,256]{1,0:T(8,128)(2,1)S(1)}, bf16[256,256]{1,0:T(8,128)(2,1)S(1)}, u32[]{:S(2)}, u32[]{:S(2)}) collective-permute-start(bf16[256,256]{1,0:T(8,128)(2,1)S(1)} %get-tuple-element.58.refs_2_.refs_8_), channel_id=1, source_target_pairs={{0,1},{1,0},{2,3},{3,2},{4,5},{5,4},{6,7},{7,6},{8,9},{9,8},{10,11... | collective-permute-start | bytes 393224 | tf_op jit(solution)/shard_map/ppermute | solution.py:103
  20.5 14.5 %copy-start.99 = (bf16[256,1024]{1,0:T(8,128)(2,1)}, bf16[256,1024]{1,0:T(8,128)(2,1)S(1)}, u32[]{:S(2)}) copy-start(bf16[256,1024]{1,0:T(8,128)(2,1)S(1)} %get-tuple-element.59.refs_7_.refs_3_.refs_0_) | copy-start | bytes 1572868
  20.5 14.5 %copy-start.58 = (bf16[256,256]{1,0:T(8,128)(2,1)}, bf16[256,256]{1,0:T(8,128)(2,1)S(1)}, u32[]{:S(2)}) copy-start(bf16[256,256]{1,0:T(8,128)(2,1)S(1)} %collective-permute-done.2.refs_5_.refs_11_) | copy-start | bytes 393220
  36.4 21.0 %copy-start.27 = (bf16[256,2048]{1,0:T(8,128)(2,1)}, bf16[256,2048]{1,0:T(8,128)(2,1)S(1)}, u32[]{:S(2)}) copy-start(bf16[256,2048]{1,0:T(8,128)(2,1)S(1)} %get-tuple-element.60.refs_2_) | copy-start | bytes 3145732
  36.4 25.6 %collective-permute-start.3 = (bf16[256,2048]{1,0:T(8,128)(2,1)S(1)}, bf16[256,2048]{1,0:T(8,128)(2,1)S(1)}, u32[]{:S(2)}, u32[]{:S(2)}) collective-permute-start(bf16[256,2048]{1,0:T(8,128)(2,1)S(1)} %get-tuple-element.60.refs_2_), channel_id=1, source_target_pairs={{0,16},{16,0},{1,17},{17,1},{2,18},{18,2},{3,19},{19,3},{4,20},{20... | collective-permute-start | bytes 3145736 | tf_op jit(solution)/shard_map/ppermute | solution.py:103
  38.7 15.1 %collective-permute-start.4 = (bf16[256,1024]{1,0:T(8,128)(2,1)}, bf16[256,1024]{1,0:T(8,128)(2,1)}, u32[]{:S(2)}, u32[]{:S(2)}) collective-permute-start(bf16[256,1024]{1,0:T(8,128)(2,1)} %get-tuple-element.62), channel_id=1, source_target_pairs={{0,2},{1,3},{2,0},{3,1},{4,6},{5,7},{6,4},{7,5},{8,10},{9,11},{10,... | collective-permute-start | bytes 1572872 | tf_op jit(solution)/shard_map/ppermute | solution.py:103
  40.2 21.8 %copy-start.18 = (bf16[256,1,2048]{2,0,1:T(8,128)(2,1)S(1)}, bf16[256,1,2048]{2,0,1:T(8,128)(2,1)}, u32[]{:S(2)}) copy-start(bf16[256,1,2048]{2,0,1:T(8,128)(2,1)} %param.11) | copy-start | bytes 3145732
  40.2 37.3 %collective-permute-start.6 = (bf16[256,1024]{1,0:T(8,128)(2,1)}, bf16[256,1024]{1,0:T(8,128)(2,1)S(1)}, u32[]{:S(2)}, u32[]{:S(2)}) collective-permute-start(bf16[256,1024]{1,0:T(8,128)(2,1)} %copy-done.39), channel_id=1, source_target_pairs={{0,2},{1,3},{2,0},{3,1},{4,6},{5,7},{6,4},{7,5},{8,10},{9,11},{10,... | collective-permute-start | bytes 1572872 | tf_op jit(solution)/shard_map/ppermute | solution.py:103
  64.8 59.2 %copy-start.105 = (bf16[256,1024]{1,0:T(8,128)(2,1)}, bf16[256,1024]{1,0:T(8,128)(2,1)S(1)}, u32[]{:S(2)}) copy-start(bf16[256,1024]{1,0:T(8,128)(2,1)S(1)} %get-tuple-element.68.refs_6_.refs_0_) | copy-start | bytes 1572868
  64.8 14.5 %collective-permute-start.5 = (bf16[256,1024]{1,0:T(8,128)(2,1)S(1)}, bf16[256,1024]{1,0:T(8,128)(2,1)S(1)}, u32[]{:S(2)}, u32[]{:S(2)}) collective-permute-start(bf16[256,1024]{1,0:T(8,128)(2,1)S(1)} %get-tuple-element.69), channel_id=1, source_target_pairs={{0,2},{1,3},{2,0},{3,1},{4,6},{5,7},{6,4},{7,5},{8,10},{9,11},{10,... | collective-permute-start | bytes 1572872 | tf_op jit(solution)/shard_map/ppermute | solution.py:103
  66.7 12.5 %copy-start.41 = (bf16[256,1024]{1,0:T(8,128)(2,1)S(1)}, bf16[256,1024]{1,0:T(8,128)(2,1)}, u32[]{:S(2)}) copy-start(bf16[256,1024]{1,0:T(8,128)(2,1)} %copy-done.39) | copy-start | bytes 1572868
  75.5 17.8 %copy-start.33 = (bf16[256,1280]{1,0:T(8,128)(2,1)}, bf16[256,1280]{1,0:T(8,128)(2,1)S(1)}, u32[]{:S(2)}) copy-start(bf16[256,1280]{1,0:T(8,128)(2,1)S(1)} %get-tuple-element.66.refs_5_.refs_2_.refs_0_) | copy-start | bytes 1966084
  75.5 17.8 %collective-permute-start.7 = (bf16[256,1280]{1,0:T(8,128)(2,1)S(1)}, bf16[256,1280]{1,0:T(8,128)(2,1)S(1)}, u32[]{:S(2)}, u32[]{:S(2)}) collective-permute-start(bf16[256,1280]{1,0:T(8,128)(2,1)S(1)} %get-tuple-element.66.refs_5_.refs_2_.refs_0_), channel_id=1, source_target_pairs={{0,2},{1,3},{2,0},{3,1},{4,6},{5,7},{6,4},{7,5},{8,10},{9,11},{10,... | collective-permute-start | bytes 1966088 | tf_op jit(solution)/shard_map/ppermute | solution.py:103
  76.4 47.5 %collective-permute-start.13 = (bf16[256,2560]{1,0:T(8,128)(2,1)}, bf16[256,2560]{1,0:T(8,128)(2,1)}, u32[]{:S(2)}, u32[]{:S(2)}) collective-permute-start(bf16[256,2560]{1,0:T(8,128)(2,1)} %get-tuple-element.67.refs_0_.refs_2_), channel_id=1, source_target_pairs={{0,2},{1,3},{2,0},{3,1},{4,6},{5,7},{6,4},{7,5},{8,10},{9,11},{10,... | collective-permute-start | bytes 3932168 | tf_op jit(solution)/shard_map/ppermute | solution.py:103
  79.2 44.7 %copy-start.48 = (bf16[256,1024]{1,0:T(8,128)(2,1)}, bf16[256,1024]{1,0:T(8,128)(2,1)S(1)}, u32[]{:S(2)}) copy-start(bf16[256,1024]{1,0:T(8,128)(2,1)S(1)} %collective-permute-done.5.refs_7_.refs_1_) | copy-start | bytes 1572868
  79.2 14.0 %copy-start.101 = (bf16[256,1024]{1,0:T(8,128)(2,1)S(1)}, bf16[256,1024]{1,0:T(8,128)(2,1)}, u32[]{:S(2)}) copy-start(bf16[256,1024]{1,0:T(8,128)(2,1)} %copy-done.99) | copy-start | bytes 1572868
  96.9 25.2 %copy-start.80 = (bf16[4,1280,128]{2,1,0:T(8,128)(2,1)}, bf16[4,1280,128]{2,1,0:T(8,128)(2,1)S(1)}, u32[]{:S(2)}) copy-start(bf16[4,1280,128]{2,1,0:T(8,128)(2,1)S(1)} %get-tuple-element.72.refs_5_.refs_1_) | copy-start | bytes 3932164
  96.9 9.2 %collective-permute-start.8 = (bf16[4,1280,128]{2,1,0:T(8,128)(2,1)S(1)}, bf16[4,1280,128]{2,1,0:T(8,128)(2,1)S(1)}, u32[]{:S(2)}, u32[]{:S(2)}) collective-permute-start(bf16[4,1280,128]{2,1,0:T(8,128)(2,1)S(1)} %get-tuple-element.76), channel_id=1, source_target_pairs={{0,1},{1,0},{2,3},{3,2},{4,5},{5,4},{6,7},{7,6},{8,9},{9,8},{10,11... | collective-permute-start | bytes 3932168 | tf_op jit(solution)/shard_map/ppermute | solution.py:103
  103.9 50.3 %collective-permute-start.10 = (bf16[256,1536]{1,0:T(8,128)(2,1)}, bf16[256,1536]{1,0:T(8,128)(2,1)}, u32[]{:S(2)}, u32[]{:S(2)}) collective-permute-start(bf16[256,1536]{1,0:T(8,128)(2,1)} %get-tuple-element.73.refs_2_.refs_1_), channel_id=1, source_target_pairs={{0,2},{1,3},{2,0},{3,1},{4,6},{5,7},{6,4},{7,5},{8,10},{9,11},{10,... | collective-permute-start | bytes 2359304 | tf_op jit(solution)/shard_map/ppermute | solution.py:103
  106.2 16.0 %collective-permute-start.11 = (bf16[1,1280,128]{2,1,0:T(8,128)(2,1)S(1)}, bf16[1,1280,128]{2,1,0:T(8,128)(2,1)S(1)}, u32[]{:S(2)}, u32[]{:S(2)}) collective-permute-start(bf16[1,1280,128]{2,1,0:T(8,128)(2,1)S(1)} %shard_map.204.refs_5_), channel_id=1, source_target_pairs={{0,4},{4,8},{8,12},{12,0},{1,5},{5,9},{9,13},{13,1},{2,6},{6,10},{... | collective-permute-start | bytes 983048 | tf_op jit(solution)/shard_map/ppermute | solution.py:376
  120.6 24.9 %collective-permute-start.15 = (bf16[256,2048]{1,0:T(8,128)(2,1)}, bf16[256,2048]{1,0:T(8,128)(2,1)}, u32[]{:S(2)}, u32[]{:S(2)}) collective-permute-start(bf16[256,2048]{1,0:T(8,128)(2,1)} %get-tuple-element.78.refs_4_.refs_2_), channel_id=1, source_target_pairs={{0,16},{16,0},{1,17},{17,1},{2,18},{18,2},{3,19},{19,3},{4,20},{20... | collective-permute-start | bytes 3145736 | tf_op jit(solution)/shard_map/ppermute | solution.py:103
  122.1 57.4 %collective-permute-start.9 = (bf16[256,3072]{1,0:T(8,128)(2,1)S(1)}, bf16[256,3072]{1,0:T(8,128)(2,1)}, u32[]{:S(2)}, u32[]{:S(2)}) collective-permute-start(bf16[256,3072]{1,0:T(8,128)(2,1)S(1)} %get-tuple-element.77.refs_2_), channel_id=1, source_target_pairs={{0,2},{1,3},{2,0},{3,1},{4,6},{5,7},{6,4},{7,5},{8,10},{9,11},{10,... | collective-permute-start | bytes 4718600 | tf_op jit(solution)/shard_map/ppermute | solution.py:103
  122.3 10.7 %collective-permute-start.12 = (bf16[1,1280,128]{2,1,0:T(8,128)(2,1)S(1)}, bf16[1,1280,128]{2,1,0:T(8,128)(2,1)S(1)}, u32[]{:S(2)}, u32[]{:S(2)}) collective-permute-start(bf16[1,1280,128]{2,1,0:T(8,128)(2,1)S(1)} %shard_map.206.refs_4_), channel_id=1, source_target_pairs={{0,4},{4,8},{8,12},{12,0},{1,5},{5,9},{9,13},{13,1},{2,6},{6,10},{... | collective-permute-start | bytes 983048 | tf_op jit(solution)/shard_map/ppermute | solution.py:376
  132.1 193.2 %reduce-scatter.5.cloned.1.call-start = ((), (), s32[]{:S(2)}) async-start(), calls=%async_computation.3 | async-start | bytes 7077888 | tf_op jit(solution)/shard_map/reduce_scatter | solution.py:281
  136.9 17.0 %copy-start.82 = (bf16[4,1280,128]{2,1,0:T(8,128)(2,1)S(1)}, bf16[4,1280,128]{2,1,0:T(8,128)(2,1)}, u32[]{:S(2)}) copy-start(bf16[4,1280,128]{2,1,0:T(8,128)(2,1)} %copy-done.80) | copy-start | bytes 3932164
  137.0 17.0 %collective-permute-start.14 = (bf16[1,1280,128]{2,1,0:T(8,128)(2,1)S(1)}, bf16[1,1280,128]{2,1,0:T(8,128)(2,1)S(1)}, u32[]{:S(2)}, u32[]{:S(2)}) collective-permute-start(bf16[1,1280,128]{2,1,0:T(8,128)(2,1)S(1)} %shard_map.208.refs_6_), channel_id=1, source_target_pairs={{0,4},{4,8},{8,12},{12,0},{1,5},{5,9},{9,13},{13,1},{2,6},{6,10},{... | collective-permute-start | bytes 983048 | tf_op jit(solution)/shard_map/ppermute | solution.py:376
  151.1 69.3 %collective-permute-start.25 = (bf16[256,1024]{1,0:T(8,128)(2,1)}, bf16[256,1024]{1,0:T(8,128)(2,1)}, u32[]{:S(2)}, u32[]{:S(2)}) collective-permute-start(bf16[256,1024]{1,0:T(8,128)(2,1)} %get-tuple-element.91), channel_id=1, source_target_pairs={{0,2},{1,3},{2,0},{3,1},{4,6},{5,7},{6,4},{7,5},{8,10},{9,11},{10,... | collective-permute-start | bytes 1572872 | tf_op jit(solution)/shard_map/ppermute | solution.py:103
  159.7 18.9 %copy-start.85 = (bf16[4,1536,128]{2,1,0:T(8,128)(2,1)}, bf16[4,1536,128]{2,1,0:T(8,128)(2,1)S(1)}, u32[]{:S(2)}) copy-start(bf16[4,1536,128]{2,1,0:T(8,128)(2,1)S(1)} %get-tuple-element.80.refs_12_.refs_1_) | copy-start | bytes 4718596
  159.7 18.9 %collective-permute-start.16 = (bf16[4,1536,128]{2,1,0:T(8,128)(2,1)S(1)}, bf16[4,1536,128]{2,1,0:T(8,128)(2,1)S(1)}, u32[]{:S(2)}, u32[]{:S(2)}) collective-permute-start(bf16[4,1536,128]{2,1,0:T(8,128)(2,1)S(1)} %get-tuple-element.81), channel_id=1, source_target_pairs={{0,1},{1,0},{2,3},{3,2},{4,5},{5,4},{6,7},{7,6},{8,9},{9,8},{10,11... | collective-permute-start | bytes 4718600 | tf_op jit(solution)/shard_map/ppermute | solution.py:103
  176.3 28.5 %collective-permute-start.19 = (bf16[256,256]{1,0:T(8,128)(2,1)}, bf16[256,256]{1,0:T(8,128)(2,1)}, u32[]{:S(2)}, u32[]{:S(2)}) collective-permute-start(bf16[256,256]{1,0:T(8,128)(2,1)} %get-tuple-element.87), channel_id=1, source_target_pairs={{0,1},{1,0},{2,3},{3,2},{4,5},{5,4},{6,7},{7,6},{8,9},{9,8},{10,11... | collective-permute-start | bytes 393224 | tf_op jit(solution)/shard_map/ppermute | solution.py:103
  176.8 28.0 %collective-permute-start.20 = (bf16[256,256]{1,0:T(8,128)(2,1)}, bf16[256,256]{1,0:T(8,128)(2,1)}, u32[]{:S(2)}, u32[]{:S(2)}) collective-permute-start(bf16[256,256]{1,0:T(8,128)(2,1)} %get-tuple-element.88), channel_id=1, source_target_pairs={{0,2},{1,3},{2,0},{3,1},{4,6},{5,7},{6,4},{7,5},{8,10},{9,11},{10,... | collective-permute-start | bytes 393224 | tf_op jit(solution)/shard_map/ppermute | solution.py:103
  178.6 26.2 %collective-permute-start.21 = (bf16[256,256]{1,0:T(8,128)(2,1)S(1)}, bf16[256,256]{1,0:T(8,128)(2,1)}, u32[]{:S(2)}, u32[]{:S(2)}) collective-permute-start(bf16[256,256]{1,0:T(8,128)(2,1)S(1)} %get-tuple-element.89), channel_id=1, source_target_pairs={{0,3},{1,2},{2,1},{3,0},{4,7},{5,6},{6,5},{7,4},{8,11},{9,10},{10,... | collective-permute-start | bytes 393224 | tf_op jit(solution)/shard_map/ppermute | solution.py:103
  179.5 22.6 %collective-permute-start.22 = (bf16[1,1536,128]{2,1,0:T(8,128)(2,1)}, bf16[1,1536,128]{2,1,0:T(8,128)(2,1)}, u32[]{:S(2)}, u32[]{:S(2)}) collective-permute-start(bf16[1,1536,128]{2,1,0:T(8,128)(2,1)} %shard_map.213.refs_4_), channel_id=1, source_target_pairs={{0,4},{4,8},{8,12},{12,0},{1,5},{5,9},{9,13},{13,1},{2,6},{6,10},{... | collective-permute-start | bytes 1179656 | tf_op jit(solution)/shard_map/ppermute | solution.py:376
  204.7 15.5 %collective-permute-start.26 = (bf16[1,1536,128]{2,1,0:T(8,128)(2,1)S(1)}, bf16[1,1536,128]{2,1,0:T(8,128)(2,1)S(1)}, u32[]{:S(2)}, u32[]{:S(2)}) collective-permute-start(bf16[1,1536,128]{2,1,0:T(8,128)(2,1)S(1)} %shard_map.216.refs_6_), channel_id=1, source_target_pairs={{0,4},{4,8},{8,12},{12,0},{1,5},{5,9},{9,13},{13,1},{2,6},{6,10},{... | collective-permute-start | bytes 1179656 | tf_op jit(solution)/shard_map/ppermute | solution.py:376
  207.7 12.6 %copy-start.87 = (bf16[4,1536,128]{2,1,0:T(8,128)(2,1)S(1)}, bf16[4,1536,128]{2,1,0:T(8,128)(2,1)}, u32[]{:S(2)}) copy-start(bf16[4,1536,128]{2,1,0:T(8,128)(2,1)} %copy-done.85) | copy-start | bytes 4718596
  223.2 22.4 %copy-start.88 = (bf16[4,1024,128]{2,1,0:T(8,128)(2,1)}, bf16[4,1024,128]{2,1,0:T(8,128)(2,1)S(1)}, u32[]{:S(2)}) copy-start(bf16[4,1024,128]{2,1,0:T(8,128)(2,1)S(1)} %get-tuple-element.92.refs_4_.refs_1_) | copy-start | bytes 3145732
  223.2 22.4 %collective-permute-start.27 = (bf16[4,1024,128]{2,1,0:T(8,128)(2,1)S(1)}, bf16[4,1024,128]{2,1,0:T(8,128)(2,1)S(1)}, u32[]{:S(2)}, u32[]{:S(2)}) collective-permute-start(bf16[4,1024,128]{2,1,0:T(8,128)(2,1)S(1)} %get-tuple-element.93), channel_id=1, source_target_pairs={{0,1},{1,0},{2,3},{3,2},{4,5},{5,4},{6,7},{7,6},{8,9},{9,8},{10,11... | collective-permute-start | bytes 3145736 | tf_op jit(solution)/shard_map/ppermute | solution.py:103
  223.3 22.1 %collective-permute-start.28 = (bf16[1,1536,128]{2,1,0:T(8,128)(2,1)S(1)}, bf16[1,1536,128]{2,1,0:T(8,128)(2,1)S(1)}, u32[]{:S(2)}, u32[]{:S(2)}) collective-permute-start(bf16[1,1536,128]{2,1,0:T(8,128)(2,1)S(1)} %shard_map.219.refs_4_), channel_id=1, source_target_pairs={{0,4},{4,8},{8,12},{12,0},{1,5},{5,9},{9,13},{13,1},{2,6},{6,10},{... | collective-permute-start | bytes 1179656 | tf_op jit(solution)/shard_map/ppermute | solution.py:376
  223.4 23.2 %collective-permute-start.18 = (bf16[256,1024]{1,0:T(8,128)(2,1)S(1)}, bf16[256,1024]{1,0:T(8,128)(2,1)S(1)}, u32[]{:S(2)}, u32[]{:S(2)}) collective-permute-start(bf16[256,1024]{1,0:T(8,128)(2,1)S(1)} %copy-done.45), channel_id=1, source_target_pairs={{0,2},{1,3},{2,0},{3,1},{4,6},{5,7},{6,4},{7,5},{8,10},{9,11},{10,... | collective-permute-start | bytes 1572872 | tf_op jit(solution)/shard_map/ppermute | solution.py:103
  225.4 23.7 %collective-permute-start.24 = (bf16[256,1024]{1,0:T(8,128)(2,1)S(1)}, bf16[256,1024]{1,0:T(8,128)(2,1)S(1)}, u32[]{:S(2)}, u32[]{:S(2)}) collective-permute-start(bf16[256,1024]{1,0:T(8,128)(2,1)S(1)} %copy-done.51), channel_id=1, source_target_pairs={{0,2},{1,3},{2,0},{3,1},{4,6},{5,7},{6,4},{7,5},{8,10},{9,11},{10,... | collective-permute-start | bytes 1572872 | tf_op jit(solution)/shard_map/ppermute | solution.py:103
  246.6 23.3 %copy-start.25 = (bf16[4,1024,128]{2,1,0:T(8,128)(2,1)S(1)}, bf16[4,1024,128]{2,1,0:T(8,128)(2,1)}, u32[]{:S(2)}) copy-start(bf16[4,1024,128]{2,1,0:T(8,128)(2,1)} %copy-done.24) | copy-start | bytes 3145732
  252.7 20.7 %collective-permute-start.29 = (bf16[4,128,1024]{2,1,0:T(8,128)(2,1)}, bf16[4,128,1024]{2,1,0:T(8,128)(2,1)S(1)}, u32[]{:S(2)}, u32[]{:S(2)}) collective-permute-start(bf16[4,128,1024]{2,1,0:T(8,128)(2,1)} %bitcast.10), channel_id=1, source_target_pairs={{0,1},{1,0},{2,3},{3,2},{4,5},{5,4},{6,7},{7,6},{8,9},{9,8},{10,11... | collective-permute-start | bytes 3145736 | tf_op jit(solution)/shard_map/ppermute | solution.py:103
  252.7 16.5 %collective-permute-start.30 = (bf16[1,1024,128]{2,1,0:T(8,128)(2,1)S(1)}, bf16[1,1024,128]{2,1,0:T(8,128)(2,1)S(1)}, u32[]{:S(2)}, u32[]{:S(2)}) collective-permute-start(bf16[1,1024,128]{2,1,0:T(8,128)(2,1)S(1)} %shard_map.222.refs_4_), channel_id=1, source_target_pairs={{0,4},{4,8},{8,12},{12,0},{1,5},{5,9},{9,13},{13,1},{2,6},{6,10},{... | collective-permute-start | bytes 786440 | tf_op jit(solution)/shard_map/ppermute | solution.py:376
  252.7 22.4 %collective-permute-start.23 = (bf16[256,256]{1,0:T(8,128)(2,1)S(1)}, bf16[256,256]{1,0:T(8,128)(2,1)S(1)}, u32[]{:S(2)}, u32[]{:S(2)}) collective-permute-start(bf16[256,256]{1,0:T(8,128)(2,1)S(1)} %shard_map.217.refs_1_.refs_5_.refs_2_), channel_id=1, source_target_pairs={{0,2},{1,3},{2,0},{3,1},{4,6},{5,7},{6,4},{7,5},{8,10},{9,11},{10,... | collective-permute-start | bytes 393224 | tf_op jit(solution)/shard_map/ppermute | solution.py:103
  254.5 25.5 %collective-permute-start.32 = (bf16[256,2048]{1,0:T(8,128)(2,1)}, bf16[256,2048]{1,0:T(8,128)(2,1)S(1)}, u32[]{:S(2)}, u32[]{:S(2)}) collective-permute-start(bf16[256,2048]{1,0:T(8,128)(2,1)} %copy-done.29), channel_id=1, source_target_pairs={{0,16},{16,0},{1,17},{17,1},{2,18},{18,2},{3,19},{19,3},{4,20},{20... | collective-permute-start | bytes 3145736 | tf_op jit(solution)/shard_map/ppermute | solution.py:103
  283.2 3.7 %collective-permute-start.40 = (f32[2,4,128]{2,1,0:T(4,128)S(1)}, f32[2,4,128]{2,1,0:T(4,128)S(1)}, u32[]{:S(2)}, u32[]{:S(2)}) collective-permute-start(f32[2,4,128]{2,1,0:T(4,128)S(1)} %bitcast.82), channel_id=1, source_target_pairs={{0,2},{1,3},{2,0},{3,1},{4,6},{5,7},{6,4},{7,5},{8,10},{9,11},{10,... | collective-permute-start | bytes 12296 | tf_op jit(solution)/shard_map/ppermute | solution.py:103
  283.5 3.3 collective-permute-start.39
  283.5 3.3 collective-permute-start.41
  285.4 38.5 %collective-permute-start.17 = (bf16[256,2048]{1,0:T(8,128)(2,1)S(1)}, bf16[256,2048]{1,0:T(8,128)(2,1)S(1)}, u32[]{:S(2)}, u32[]{:S(2)}) collective-permute-start(bf16[256,2048]{1,0:T(8,128)(2,1)S(1)} %copy-done.21), channel_id=1, source_target_pairs={{0,16},{16,0},{1,17},{17,1},{2,18},{18,2},{3,19},{19,3},{4,20},{20... | collective-permute-start | bytes 3145736 | tf_op jit(solution)/shard_map/ppermute | solution.py:103
  286.9 7.2 %collective-permute-start.44 = (f32[2,128]{1,0:T(2,128)S(1)}, f32[2,128]{1,0:T(2,128)S(1)}, u32[]{:S(2)}, u32[]{:S(2)}) collective-permute-start(f32[2,128]{1,0:T(2,128)S(1)} %bitcast.88), channel_id=1, source_target_pairs={{0,12},{4,8},{8,4},{12,0},{1,13},{5,9},{9,5},{13,1},{2,14},{6,10},... | collective-permute-start | bytes 3080 | tf_op jit(solution)/shard_map/ppermute | solution.py:103
  290.5 5.5 %collective-permute-start.42 = (f32[2,128]{1,0:T(2,128)S(1)}, f32[2,128]{1,0:T(2,128)S(1)}, u32[]{:S(2)}, u32[]{:S(2)}) collective-permute-start(f32[2,128]{1,0:T(2,128)S(1)} %bitcast.87), channel_id=1, source_target_pairs={{0,4},{4,0},{8,12},{12,8},{1,5},{5,1},{9,13},{13,9},{2,6},{6,2},{1... | collective-permute-start | bytes 3080 | tf_op jit(solution)/shard_map/ppermute | solution.py:103
  291.3 4.7 %collective-permute-start.43 = (f32[2,128]{1,0:T(2,128)S(1)}, f32[2,128]{1,0:T(2,128)S(1)}, u32[]{:S(2)}, u32[]{:S(2)}) collective-permute-start(f32[2,128]{1,0:T(2,128)S(1)} %bitcast.86), channel_id=1, source_target_pairs={{0,8},{4,12},{8,0},{12,4},{1,9},{5,13},{9,1},{13,5},{2,10},{6,14},... | collective-permute-start | bytes 3080 | tf_op jit(solution)/shard_map/ppermute | solution.py:103
  292.5 11.0 %collective-permute-start.35 = (bf16[1,1024,128]{2,1,0:T(8,128)(2,1)S(1)}, bf16[1,1024,128]{2,1,0:T(8,128)(2,1)S(1)}, u32[]{:S(2)}, u32[]{:S(2)}) collective-permute-start(bf16[1,1024,128]{2,1,0:T(8,128)(2,1)S(1)} %shard_map.224.refs_3_), channel_id=1, source_target_pairs={{0,4},{4,8},{8,12},{12,0},{1,5},{5,9},{9,13},{13,1},{2,6},{6,10},{... | collective-permute-start | bytes 786440 | tf_op jit(solution)/shard_map/ppermute | solution.py:376
  294.1 15.1 %collective-permute-start.34 = (bf16[1,128,1024]{2,1,0:T(8,128)(2,1)S(1)}, bf16[1,128,1024]{2,1,0:T(8,128)(2,1)S(1)}, u32[]{:S(2)}, u32[]{:S(2)}) collective-permute-start(bf16[1,128,1024]{2,1,0:T(8,128)(2,1)S(1)} %shard_map.225.refs_4_), channel_id=1, source_target_pairs={{0,4},{4,8},{8,12},{12,0},{1,5},{5,9},{9,13},{13,1},{2,6},{6,10},{... | collective-permute-start | bytes 786440 | tf_op jit(solution)/shard_map/ppermute | solution.py:376
  296.0 1.5 collective-permute-start.31
  297.6 12.9 %collective-permute-start.33 = (bf16[1,128,256]{2,1,0:T(8,128)(2,1)S(1)}, bf16[1,128,256]{2,1,0:T(8,128)(2,1)S(1)}, u32[]{:S(2)}, u32[]{:S(2)}) collective-permute-start(bf16[1,128,256]{2,1,0:T(8,128)(2,1)S(1)} %shard_map.228.refs_4_), channel_id=1, source_target_pairs={{0,4},{4,8},{8,12},{12,0},{1,5},{5,9},{9,13},{13,1},{2,6},{6,10},{... | collective-permute-start | bytes 196616 | tf_op jit(solution)/shard_map/ppermute | solution.py:376
  303.6 12.5 %collective-permute-start.38 = (bf16[1,1024,128]{2,1,0:T(8,128)(2,1)S(1)}, bf16[1,1024,128]{2,1,0:T(8,128)(2,1)S(1)}, u32[]{:S(2)}, u32[]{:S(2)}) collective-permute-start(bf16[1,1024,128]{2,1,0:T(8,128)(2,1)S(1)} %shard_map.229.refs_4_), channel_id=1, source_target_pairs={{0,4},{4,8},{8,12},{12,0},{1,5},{5,9},{9,13},{13,1},{2,6},{6,10},{... | collective-permute-start | bytes 786440 | tf_op jit(solution)/shard_map/ppermute | solution.py:376
  309.3 12.0 %collective-permute-start.37 = (bf16[1,128,1024]{2,1,0:T(8,128)(2,1)S(1)}, bf16[1,128,1024]{2,1,0:T(8,128)(2,1)S(1)}, u32[]{:S(2)}, u32[]{:S(2)}) collective-permute-start(bf16[1,128,1024]{2,1,0:T(8,128)(2,1)S(1)} %shard_map.230.refs_4_), channel_id=1, source_target_pairs={{0,4},{4,8},{8,12},{12,0},{1,5},{5,9},{9,13},{13,1},{2,6},{6,10},{... | collective-permute-start | bytes 786440 | tf_op jit(solution)/shard_map/ppermute | solution.py:376
  310.6 11.9 %collective-permute-start.36 = (bf16[1,128,256]{2,1,0:T(8,128)(2,1)S(1)}, bf16[1,128,256]{2,1,0:T(8,128)(2,1)S(1)}, u32[]{:S(2)}, u32[]{:S(2)}) collective-permute-start(bf16[1,128,256]{2,1,0:T(8,128)(2,1)S(1)} %shard_map.231.refs_4_), channel_id=1, source_target_pairs={{0,4},{4,8},{8,12},{12,0},{1,5},{5,9},{9,13},{13,1},{2,6},{6,10},{... | collective-permute-start | bytes 196616 | tf_op jit(solution)/shard_map/ppermute | solution.py:376
  322.4 11.7 %collective-permute-start.45 = (bf16[1,128,1024]{2,1,0:T(8,128)(2,1)S(1)}, bf16[1,128,1024]{2,1,0:T(8,128)(2,1)S(1)}, u32[]{:S(2)}, u32[]{:S(2)}) collective-permute-start(bf16[1,128,1024]{2,1,0:T(8,128)(2,1)S(1)} %shard_map.233.refs_4_), channel_id=1, source_target_pairs={{0,4},{4,8},{8,12},{12,0},{1,5},{5,9},{9,13},{13,1},{2,6},{6,10},{... | collective-permute-start | bytes 786440 | tf_op jit(solution)/shard_map/ppermute | solution.py:376
  322.5 9.5 %collective-permute-start.46 = (bf16[1,128,256]{2,1,0:T(8,128)(2,1)S(1)}, bf16[1,128,256]{2,1,0:T(8,128)(2,1)S(1)}, u32[]{:S(2)}, u32[]{:S(2)}) collective-permute-start(bf16[1,128,256]{2,1,0:T(8,128)(2,1)S(1)} %shard_map.234.refs_3_), channel_id=1, source_target_pairs={{0,4},{4,8},{8,12},{12,0},{1,5},{5,9},{9,13},{13,1},{2,6},{6,10},{... | collective-permute-start | bytes 196616 | tf_op jit(solution)/shard_map/ppermute | solution.py:376
  (101 other events, 465.7 us)
Sparse Core Ops, SparseCore 0:
  132.2 73.2 reduce-scatter.2
  207.8 83.6 reduce-scatter.4
